TPU v7x, 32 devices: a whole 2x2x4 slice. The times are simulated.
32 devices in a mesh: groups: 2 (over y), fsdp: 4 (over z), tp: 2 (over x), sub: 2 (over core).
Axes of the slice: x: 2, y: 2, z: 4, core: 2. Of those that a mesh axis runs over, the one named last changes fastest.
Arguments:
- activations: bfloat16 [8192, 8192], P(('groups', 'fsdp', 'sub'), 'tp'), parts along dimension 0, may hold values from -6 to 6
- output_gradient: bfloat16 [8192, 2048], P(('groups', 'fsdp', 'sub'), 'tp'), parts along dimension 0, may hold values from -4 to 4
- base_weight: bfloat16 [8192, 2048], P('tp', 'fsdp'), may hold values from -0.0625 to 0.0625
- factor_down: bfloat16 [128, 16, 8192], P(('groups', 'fsdp', 'sub'), None, 'tp'), parts along dimension 0, may hold values from -0.0625 to 0.0625
- factor_up: bfloat16 [128, 16, 2048], P(('groups', 'fsdp', 'sub'), None, 'tp'), parts along dimension 0, may hold values from -1.5 to 1.5
- counts: int32 [16, 64], P(('groups', 'fsdp', 'sub')), parts along dimension 0, may hold values from 1 to 64, 512 in all within a row
- owners: int32 [128], P('groups'), parts along dimension 0, may hold values from 0 to 63, each once
Outputs:
- input_gradient: bfloat16 [8192, 8192], P(('groups', 'fsdp', 'sub'), 'tp'), parts along dimension 0
- grad_down: float32 [128, 16, 8192], P(('groups', 'fsdp', 'sub'), None, 'tp'), parts along dimension 0
- up_factor_gradient: float32 [128, 16, 2048], P(('groups', 'fsdp', 'sub'), None, 'tp'), parts along dimension 0
There are 2 independent parts, one for each index of `groups`. A program takes and returns all parts, laid end to end along the dimension named above; an argument that names none is the same for every part. Nothing has to cross between parts.
Inputs may be any that keep to these rules, and one draw needn't show every extreme that they name: `counts`: each row sums to 512; every adapter has tokens in every block, and some adapter has exactly 64 in a block. `owners`: a permutation of the slots.
All inputs are finite; a program needn't handle non-finite values.
Results may differ from a plain program's by a relative error of at most 0.013.
Values may be sent and summed in bfloat16 or wider, within the bound.
No kernel may reach another device: no remote copies, remote signals or barrier semaphores. Data moves between devices by JAX's collectives and lax.ppermute only.
A program may use at most 256 MiB of HBM per device.

v0:
```python
import jax
import jax.numpy as jnp
from jax import lax
from jax.sharding import PartitionSpec as P

adapter_scale_factor = 0.25


def local(activations, output_gradient, base_weight, factor_down, factor_up, counts, owners):
    tok_rows = activations.shape[0]
    adapter_count = owners.shape[0]
    seg_ends = jnp.cumsum(counts[0])
    seg_starts = seg_ends - counts[0]
    position = lax.broadcasted_iota(jnp.int32, (tok_rows, adapter_count), 0)
    adapter_hot = ((position >= seg_starts[None, :]) & (position < seg_ends[None, :])).astype(
        jnp.float32
    )
    slot_grid = lax.broadcasted_iota(jnp.int32, (adapter_count, adapter_count), 1)
    owner_hot = (owners[:, None] == slot_grid).astype(jnp.float32)
    slot_onehot_matrix = jnp.dot(adapter_hot, owner_hot, precision=lax.Precision.HIGHEST)
    down_projected_every, up_all = (
        lax.all_gather(factor_down, ("fsdp", "sub"), axis=0, tiled=True),
        lax.all_gather(factor_up, ("fsdp", "sub"), axis=0, tiled=True),
    )
    grad_full = lax.all_gather(output_gradient, "tp", axis=1, tiled=True)
    low_part = jnp.einsum(
        "td,grd->tgr", activations, down_projected_every, preferred_element_type=jnp.float32
    )
    back_part = jnp.einsum(
        "tc,grc->tgr", output_gradient, up_all, preferred_element_type=jnp.float32
    )
    low_sel = jnp.sum(low_part * slot_onehot_matrix[:, :, None], axis=1)
    back_sel = jnp.sum(back_part * slot_onehot_matrix[:, :, None], axis=1)
    low_in, backward_total = (
        lax.psum(low_sel.astype(jnp.bfloat16), "tp").astype(jnp.float32),
        lax.psum(back_sel.astype(jnp.bfloat16), "tp").astype(jnp.float32),
    )
    narrow_backward = adapter_scale_factor * backward_total
    broad_backward = (slot_onehot_matrix[:, :, None] * narrow_backward[:, None, :]).astype(
        jnp.bfloat16
    )
    broad_input = (slot_onehot_matrix[:, :, None] * low_in[:, None, :]).astype(jnp.bfloat16)
    adapter_contribution = jnp.einsum(
        "psl,sln->pn", broad_backward, down_projected_every, preferred_element_type=jnp.float32
    )
    reduced_total = adapter_contribution + lax.dot_general(
        grad_full,
        lax.all_gather(base_weight, "fsdp", axis=1, tiled=True),
        (((1,), (1,)), ((), ())),
        preferred_element_type=jnp.float32,
    )
    input_gradient = reduced_total.astype(jnp.bfloat16)
    down_partial = jnp.einsum(
        "tgr,td->grd", broad_backward, activations, preferred_element_type=jnp.float32
    )
    up_factor_pieces = adapter_scale_factor * jnp.einsum(
        "tgr,tc->grc", broad_input, output_gradient, preferred_element_type=jnp.float32
    )
    got_down, got_up = (
        lax.all_to_all(
            down_partial[None].astype(jnp.bfloat16),
            ("fsdp", "sub"),
            split_axis=1,
            concat_axis=0,
            tiled=True,
        ).astype(jnp.float32),
        lax.all_to_all(
            up_factor_pieces[None].astype(jnp.bfloat16),
            ("fsdp", "sub"),
            split_axis=1,
            concat_axis=0,
            tiled=True,
        ).astype(jnp.float32),
    )
    grad_down = jnp.sum(got_down, axis=0)
    up_factor_gradient = jnp.sum(got_up, axis=0)
    return (input_gradient, grad_down, up_factor_gradient)


def solution(mesh):
    placed = (
        P(("groups", "fsdp", "sub"), "tp"),
        P(("groups", "fsdp", "sub"), "tp"),
        P("tp", "fsdp"),
        P(("groups", "fsdp", "sub"), None, "tp"),
        P(("groups", "fsdp", "sub"), None, "tp"),
        P(("groups", "fsdp", "sub"), None),
        P("groups"),
    )
    return jax.shard_map(
        local,
        mesh=mesh,
        in_specs=placed,
        out_specs=(
            P(("groups", "fsdp", "sub"), "tp"),
            P(("groups", "fsdp", "sub"), None, "tp"),
            P(("groups", "fsdp", "sub"), None, "tp"),
        ),
        check_vma=False,
    )
```

profile of v0, /device:TPU:0, one launch (start us, length us, event | category | flops | bytes accessed | tf_op | source)
XLA Modules:
  0.0 679.3 jit_solution(5720070315417383554)
XLA Ops:
  7.2 1.8 copy.21
  9.1 2.9 copy.22
  12.1 0.7 all-gather.9.cloned.1.call-update
  12.8 0.5 all-gather.11.cloned.1.call-update
  13.3 0.1 copy.20
  13.4 0.1 reduce-window.4
  13.5 0.1 reduce
  13.7 0.3 fusion.12
  13.9 28.1 %all-gather.5.cloned.1.call-done = bf16[64,16,1024]{2,0,1:T(8,128)(2,1)} async-done(((bf16[8,16,1024]{2,0,1:T(8,128)(2,1)}), bf16[64,16,1024]{2,0,1:T(8,128)(2,1)}) %all-gather.5.cloned.1.call-update) | async-done | bytes 2097168 | tf_op jit(solution)/shard_map/all_gather | solution.py:23
  42.0 2.9 multiply_reduce_fusion.1
  44.9 80.9 %all-gather.7.cloned.1.call-done = bf16[64,16,4096]{2,0,1:T(8,128)(2,1)} async-done(((bf16[8,16,4096]{2,0,1:T(8,128)(2,1)}), bf16[64,16,4096]{2,0,1:T(8,128)(2,1)}) %all-gather.7.cloned.1.call-update) | async-done | bytes 8388624 | tf_op jit(solution)/shard_map/all_gather | solution.py:22
  125.8 9.2 %multiply_reduce_fusion = bf16[512,16]{0,1:T(8,128)(2,1)S(1)} fusion(bf16[64,16,4096]{2,0,1:T(8,128)(2,1)} %all-gather.7.cloned.1.call-done, bf16[512,4096]{1,0:T(8,128)(2,1)} %param.7, f32[512,64]{0,1:T(8,128)S(1)} %fusion.12), kind=kOutput, calls=%fused_computation.10 | convolution fusion | flops 4296007680 | bytes 12730368 | tf_op jit(solution)/shard_map/td,grd->tgr/dot_general | solution.py:26
  135.0 9.0 %all-reduce = (bf16[512,16]{0,1:T(8,128)(2,1)S(1)}, bf16[512,16]{0,1:T(8,128)(2,1)S(1)}) all-reduce(bf16[512,16]{0,1:T(8,128)(2,1)S(1)} %multiply_reduce_fusion.1, bf16[512,16]{0,1:T(8,128)(2,1)S(1)} %multiply_reduce_fusion), channel_id=1, replica_groups=mesh['groups'=2,'fsdp'=4,'tp'=2,'sub'=2] {'tp'}, use_global_device_ids=true, to_apply=%region_2.3 | all-reduce | flops 16384 | bytes 65536 | tf_op jit(solution)/shard_map/psum | solution.py:36
  144.0 1.6 multiply_convert_fusion.1
  145.5 2.7 fusion.4
  148.3 3.7 all-to-all-start.1
  152.0 9.6 %convert_bitcast_fusion = bf16[1,64,16,4096]{3,2,0,1:T(8,128)(2,1)} fusion(bf16[512,4096]{1,0:T(8,128)(2,1)} %param.7, bf16[512,64,16]{0,1,2:T(8,128)(2,1)S(1)} %copy-done.1), kind=kOutput, calls=%fused_computation.3 | convolution fusion | flops 4299161600 | bytes 13631488 | tf_op jit(solution)/shard_map/tgr,td->grd/dot_general | solution.py:53
  161.6 72.9 %all-to-all-done.1 = bf16[1,64,16,1024]{3,2,0,1:T(8,128)(2,1)S(1)} async-done(((bf16[1,64,16,1024]{3,2,0,1:T(8,128)(2,1)}), bf16[1,64,16,1024]{3,2,0,1:T(8,128)(2,1)S(1)}, u32[]{:S(2)}, u32[]{:S(2)}) %all-to-all-start.1) | async-done | bytes 2097184 | tf_op jit(solution)/shard_map/all_to_all | solution.py:67
  234.6 17.1 %all-to-all-start = ((bf16[1,64,16,4096]{3,2,0,1:T(8,128)(2,1)}), bf16[1,64,16,4096]{3,2,0,1:T(8,128)(2,1)}, u32[]{:S(2)}, u32[]{:S(2)}) async-start(bf16[1,64,16,4096]{3,2,0,1:T(8,128)(2,1)} %convert_bitcast_fusion), calls=%async_computation | async-start | bytes 16777216 | tf_op jit(solution)/shard_map/all_to_all | solution.py:60
  251.7 10.1 %fusion.16 = f32[512,4096,1]{1,0,2:T(8,128)} fusion(bf16[64,16,4096]{2,0,1:T(8,128)(2,1)} %all-gather.7.cloned.1.call-done, f32[512,16]{0,1:T(8,128)S(1)} %convert_multiply_fusion, f32[512,64]{0,1:T(8,128)S(1)} %fusion.12), kind=kOutput, calls=%fused_computation.24 | convolution fusion | flops 4296015872 | bytes 16941056 | tf_op jit(solution)/shard_map/psl,sln->pn/dot_general | solution.py:43
  261.9 1.1 convert_reduce_fusion.1
  263.0 387.9 %all-gather.11.cloned.1.call-done = bf16[4096,2048]{1,0:T(8,128)(2,1)} async-done(((bf16[4096,512]{1,0:T(8,128)(2,1)}), bf16[4096,2048]{1,0:T(8,128)(2,1)}) %all-gather.11.cloned.1.call-update) | async-done | bytes 16777232 | tf_op jit(solution)/shard_map/all_gather | solution.py:48
  650.9 15.6 %fusion = bf16[512,4096]{1,0:T(8,128)(2,1)} fusion(f32[512,4096,1]{1,0,2:T(8,128)} %fusion.16, bf16[512,2048]{1,0:T(8,128)(2,1)} %all-gather.9.cloned.1.call-done, bf16[4096,2048]{1,0:T(8,128)(2,1)} %all-gather.11.cloned.1.call-done), kind=kOutput, calls=%fused_computation.2 | convolution fusion | flops 8594128896 | bytes 31457280 | tf_op jit(solution)/shard_map/dot_general | solution.py:46
  666.4 6.3 convert_reduce_fusion
  (19 shorter events, 0.2 us)
Async XLA Ops:
  7.2 34.8 %all-gather.5.cloned.1.call-start = ((), (), s32[]{:S(2)}) async-start(), calls=%async_computation.2 | async-start | bytes 2359296 | tf_op jit(solution)/shard_map/all_gather | solution.py:23
  9.0 4.3 copy-start.2
  9.0 4.6 copy-start.3
  9.1 33.0 %copy-start = (bf16[512,1024]{1,0:T(8,128)(2,1)S(1)}, bf16[512,1024]{1,0:T(8,128)(2,1)}, u32[]{:S(2)}) copy-start(bf16[512,1024]{1,0:T(8,128)(2,1)} %param.8) | copy-start | bytes 3145732
  9.1 116.7 %all-gather.7.cloned.1.call-start = ((), (), s32[]{:S(2)}) async-start(), calls=%async_computation.3 | async-start | bytes 9437184 | tf_op jit(solution)/shard_map/all_gather | solution.py:22
  12.0 251.0 %all-gather.9.cloned.1.call-start = ((), (), s32[]{:S(2)}) async-start(), calls=%async_computation.4 | async-start | bytes 3145728 | tf_op jit(solution)/shard_map/all_gather | solution.py:25
  12.7 638.1 %all-gather.11.cloned.1.call-start = ((), (), s32[]{:S(2)}) async-start(), calls=%async_computation.5 | async-start | bytes 20971520 | tf_op jit(solution)/shard_map/all_gather | solution.py:48
  148.3 3.7 copy-start.1
  148.3 86.3 %all-to-all-start.1 = ((bf16[1,64,16,1024]{3,2,0,1:T(8,128)(2,1)}), bf16[1,64,16,1024]{3,2,0,1:T(8,128)(2,1)S(1)}, u32[]{:S(2)}, u32[]{:S(2)}) async-start(bf16[1,64,16,1024]{3,2,0,1:T(8,128)(2,1)} %fusion.4), calls=%async_computation.1 | async-start | bytes 4194304 | tf_op jit(solution)/shard_map/all_to_all | solution.py:67
  234.6 431.9 %all-to-all-start = ((bf16[1,64,16,4096]{3,2,0,1:T(8,128)(2,1)}), bf16[1,64,16,4096]{3,2,0,1:T(8,128)(2,1)}, u32[]{:S(2)}, u32[]{:S(2)}) async-start(bf16[1,64,16,4096]{3,2,0,1:T(8,128)(2,1)} %convert_bitcast_fusion), calls=%async_computation | async-start | bytes 16777216 | tf_op jit(solution)/shard_map/all_to_all | solution.py:60
Sparse Core Ops, SparseCore 0:
  10.2 31.7 all-gather.4
  44.2 81.5 all-gather.6
  127.3 32.3 all-gather.8
  161.1 489.6 all-gather.10
where the time goes:
time: 680 us; the launch traced here: 679 us
  waiting for transfers between devices  571 us (84%)
  matrix products  50.4 us (7%)
  starting transfers between devices  21 us (3%)
  between operations  13.9 us (2%)
  other arithmetic  9.24 us (1%)
  blocking collectives  8.97 us (1%)
    all_gather x1, waiting for transfers between devices, local(): lax.all_gather(base_weight, 'fsdp', axis=1, tiled=True)  388 us
    all_gather x1, waiting for transfers between devices, local(): lax.all_gather(factor_down, ('fsdp', 'sub'), axis=0, tiled=True)  80.9 us
    all_to_all x1, waiting for transfers between devices, local(): lax.all_to_all(up_factor_pieces[None].astype(jnp.bfloat16), ('fsdp', 'sub...  72.9 us
    all_gather x1, waiting for transfers between devices, local(): lax.all_gather(factor_up, ('fsdp', 'sub'), axis=0, tiled=True)  28.1 us
    all_to_all x1, starting transfers between devices, local(): lax.all_to_all(down_partial[None].astype(jnp.bfloat16), ('fsdp', 'sub'),...  17.1 us
    dot_general x1, matrix products, local(): lax.dot_general(grad_full, lax.all_gather(base_weight, 'fsdp', axis=1, ti...  15.6 us
  transfers between devices with their start and end apart: 6, of which 4 were waited for; matrix products, arithmetic and copies ran while one was open for 8% of the time, Pallas kernels for 0%

commit v1 on v0

--- a/solution.py
+++ b/solution.py
@@ -43,10 +43,18 @@
     adapter_contribution = jnp.einsum(
         "psl,sln->pn", broad_backward, down_projected_every, preferred_element_type=jnp.float32
     )
-    reduced_total = adapter_contribution + lax.dot_general(
-        grad_full,
-        lax.all_gather(base_weight, "fsdp", axis=1, tiled=True),
-        (((1,), (1,)), ((), ())),
+    copies = lax.axis_size("groups") * lax.axis_size("sub")
+    part = lax.axis_index("groups") * lax.axis_size("sub") + lax.axis_index("sub")
+    rows = base_weight.shape[0] // copies
+    own_rows = lax.dynamic_slice_in_dim(base_weight, part * rows, rows, axis=0)
+    weight = lax.all_gather(own_rows, ("fsdp", "groups", "sub"), axis=0, tiled=True)
+    shards = lax.axis_size("fsdp")
+    width = base_weight.shape[1]
+    weight = weight.reshape(shards, copies * rows, width)
+    reduced_total = adapter_contribution + jnp.einsum(
+        "tfc,fdc->td",
+        grad_full.reshape(tok_rows, shards, width),
+        weight,
         preferred_element_type=jnp.float32,
     )
     input_gradient = reduced_total.astype(jnp.bfloat16)
@@ -56,24 +64,12 @@
     up_factor_pieces = adapter_scale_factor * jnp.einsum(
         "tgr,tc->grc", broad_input, output_gradient, preferred_element_type=jnp.float32
     )
-    got_down, got_up = (
-        lax.all_to_all(
-            down_partial[None].astype(jnp.bfloat16),
-            ("fsdp", "sub"),
-            split_axis=1,
-            concat_axis=0,
-            tiled=True,
-        ).astype(jnp.float32),
-        lax.all_to_all(
-            up_factor_pieces[None].astype(jnp.bfloat16),
-            ("fsdp", "sub"),
-            split_axis=1,
-            concat_axis=0,
-            tiled=True,
-        ).astype(jnp.float32),
+    grad_down, up_factor_gradient = (
+        lax.psum_scatter(
+            piece.astype(jnp.bfloat16), ("fsdp", "sub"), scatter_dimension=0, tiled=True
+        ).astype(jnp.float32)
+        for piece in (down_partial, up_factor_pieces)
     )
-    grad_down = jnp.sum(got_down, axis=0)
-    up_factor_gradient = jnp.sum(got_up, axis=0)
     return (input_gradient, grad_down, up_factor_gradient)
 
 

time: 680 us -> 400 us (0.59)
  waiting for transfers between devices: 571 us -> 309 us
  starting transfers between devices: 21 us -> 0.43 us
    all_gather x1, waiting for transfers between devices: 388 us -> 191 us  [local(): lax.all_gather(own_rows, ('fsdp', 'groups', 'sub'), axis=0, tiled=True)]
    all_to_all x2 -> x0, waiting for transfers between devices: 72.9 us -> none  [the longest x1 72.9 us: local(): lax.all_to_all(up_factor_pieces[None].astype(jnp.bfloat16), ('fsdp', 'sub...]
    all_to_all x2 -> x0, starting transfers between devices: 20.9 us -> none  [the longest x1 17.1 us: local(): lax.all_to_all(down_partial[None].astype(jnp.bfloat16), ('fsdp', 'sub'),...]
    reduce_scatter x0 -> x2, waiting for transfers between devices: none -> 9.55 us  [local(): lax.psum_scatter(piece.astype(jnp.bfloat16), ('fsdp', 'sub'), scatter_dim...]
    reduce_sum x2 -> x0, other arithmetic: 7.46 us -> none  [the longest x1 6.32 us: local(): grad_down = jnp.sum(got_down, axis=0)]
  transfers between devices with their start and end apart: 6 -> 6, of which waited for: 4 -> 4; matrix products, arithmetic and copies ran while one was open for 8% -> 12% of each run, Pallas kernels for 0% -> 0%
where the time goes in v1:
time: 400 us; the launch traced here: 399 us
  waiting for transfers between devices  309 us (77%)
  matrix products  51.4 us (13%)
  between operations  15.3 us (4%)
  local copies, waits for them, and re-layouts  8.99 us (2%)
  blocking collectives  8.33 us (2%)
  other arithmetic  5.94 us (1%)
    all_gather x1, waiting for transfers between devices, local(): lax.all_gather(own_rows, ('fsdp', 'groups', 'sub'), axis=0, tiled=True)  191 us
    all_gather x1, waiting for transfers between devices, local(): lax.all_gather(factor_down, ('fsdp', 'sub'), axis=0, tiled=True)  80.9 us
    all_gather x1, waiting for transfers between devices, local(): lax.all_gather(factor_up, ('fsdp', 'sub'), axis=0, tiled=True)  27.4 us
    dot_general x1, matrix products, local(): jnp.einsum('tfc,fdc->td', grad_full.reshape(tok_rows, shards, width), wei...  15.6 us
    dot_general x1, matrix products, local(): jnp.einsum('psl,sln->pn', broad_backward, down_projected_every, preferred...  10.2 us
    dot_general x1, matrix products, local(): jnp.einsum('tgr,td->grd', broad_backward, activations, preferred_element_...  9.84 us
    reduce_scatter x2, waiting for transfers between devices, local(): lax.psum_scatter(piece.astype(jnp.bfloat16), ('fsdp', 'sub'), scatter_dim...  9.55 us
    dot_general x1, matrix products, local(): jnp.einsum('td,grd->tgr', activations, down_projected_every, preferred_el...  9.19 us
  transfers between devices with their start and end apart: 6, of which 4 were waited for; matrix products, arithmetic and copies ran while one was open for 12% of the time, Pallas kernels for 0%

profile of v1, /device:TPU:0, one launch (start us, length us, event | category | flops | bytes accessed | tf_op | source)
XLA Modules:
  0.0 399.1 jit_solution(3734296010365525471)
XLA Ops:
  8.1 1.9 copy.17
  10.0 2.8 copy.18
  12.9 0.7 copy.16
  13.6 0.1 reduce-window.4
  13.7 0.1 reduce
  13.8 0.7 fusion.17
  14.5 0.9 fusion.11
  15.4 27.4 %all-gather.5.cloned.1.call-done = bf16[64,16,1024]{2,0,1:T(8,128)(2,1)} async-done(((bf16[8,16,1024]{2,0,1:T(8,128)(2,1)}), bf16[64,16,1024]{2,0,1:T(8,128)(2,1)}) %all-gather.5.cloned.1.call-update) | async-done | bytes 2097168 | tf_op jit(solution)/shard_map/all_gather | solution.py:23
  42.9 2.9 multiply_reduce_fusion.1
  45.8 80.9 %all-gather.7.cloned.1.call-done = bf16[64,16,4096]{2,0,1:T(8,128)(2,1)} async-done(((bf16[8,16,4096]{2,0,1:T(8,128)(2,1)}), bf16[64,16,4096]{2,0,1:T(8,128)(2,1)}) %all-gather.7.cloned.1.call-update) | async-done | bytes 8388624 | tf_op jit(solution)/shard_map/all_gather | solution.py:22
  126.6 9.2 %multiply_reduce_fusion = bf16[512,16]{0,1:T(8,128)(2,1)S(1)} fusion(bf16[64,16,4096]{2,0,1:T(8,128)(2,1)} %all-gather.7.cloned.1.call-done, bf16[512,4096]{1,0:T(8,128)(2,1)} %param.7, f32[512,64]{0,1:T(8,128)S(1)} %fusion.11), kind=kOutput, calls=%fused_computation.8 | convolution fusion | flops 4296007680 | bytes 12730368 | tf_op jit(solution)/shard_map/td,grd->tgr/dot_general | solution.py:26
  135.8 8.3 %all-reduce = (bf16[512,16]{0,1:T(8,128)(2,1)S(1)}, bf16[512,16]{0,1:T(8,128)(2,1)S(1)}) all-reduce(bf16[512,16]{0,1:T(8,128)(2,1)S(1)} %multiply_reduce_fusion.1, bf16[512,16]{0,1:T(8,128)(2,1)S(1)} %multiply_reduce_fusion), channel_id=1, replica_groups=mesh['groups'=2,'fsdp'=4,'tp'=2,'sub'=2] {'tp'}, use_global_device_ids=true, to_apply=%region_2.3 | all-reduce | flops 16384 | bytes 65536 | tf_op jit(solution)/shard_map/psum | solution.py:36
  144.2 0.5 multiply_convert_fusion.1
  144.7 2.8 multiply_convert_fusion
  147.5 1.3 copy.19
  148.9 2.3 constant_dynamic-slice_fusion
  151.2 0.2 reduce-scatter.3.cloned.1.call-start
  151.4 9.8 %convolution_convert_fusion = bf16[64,16,4096]{2,1,0:T(8,128)(2,1)} fusion(bf16[512,4096]{1,0:T(8,128)(2,1)} %param.7, bf16[512,64,16]{0,1,2:T(8,128)(2,1)S(1)} %get-tuple-element.6), kind=kOutput, calls=%fused_computation.2 | convolution fusion | flops 4299161600 | bytes 13631488 | tf_op jit(solution)/shard_map/tgr,td->grd/dot_general | solution.py:61
  161.3 10.2 %fusion.15 = f32[512,4096,1]{1,0,2:T(8,128)} fusion(bf16[64,16,4096]{2,0,1:T(8,128)(2,1)} %all-gather.7.cloned.1.call-done, f32[512,16]{0,1:T(8,128)S(1)} %convert_multiply_fusion, f32[512,64]{0,1:T(8,128)S(1)} %fusion.11), kind=kOutput, calls=%fused_computation.21 | convolution fusion | flops 4296015872 | bytes 16941056 | tf_op jit(solution)/shard_map/psl,sln->pn/dot_general | solution.py:43
  171.5 9.6 %reduce-scatter.5.cloned.1.call-done = bf16[8,16,1024]{2,1,0:T(8,128)(2,1)} async-done(((bf16[64,16,1024]{2,1,0:T(8,128)(2,1)}), bf16[8,16,1024]{2,1,0:T(8,128)(2,1)}) %reduce-scatter.5.cloned.1.call-update) | async-done | bytes 262160 | tf_op jit(solution)/shard_map/reduce_scatter | solution.py:68
  181.0 1.8 convert_element_type.45
  182.8 190.8 %all-gather.9.cloned.1.call-done = bf16[16384,512]{1,0:T(8,128)(2,1)} async-done(((bf16[1024,512]{1,0:T(8,128)(2,1)}), bf16[16384,512]{1,0:T(8,128)(2,1)}) %all-gather.9.cloned.1.call-update) | async-done | bytes 16777232 | tf_op jit(solution)/shard_map/all_gather | solution.py:50
  373.6 15.6 %fusion = bf16[512,4096]{1,0:T(8,128)(2,1)} fusion(f32[512,4096,1]{1,0,2:T(8,128)} %fusion.15, bf16[4,4096,512]{2,1,0:T(8,128)(2,1)} %bitcast.35, bf16[512,4,512]{0,2,1:T(8,128)(2,1)} %bitcast.36), kind=kOutput, calls=%fused_computation.1 | convolution fusion | flops 8594128896 | bytes 31457280 | tf_op jit(solution)/shard_map/tfc,fdc->td/dot_general | solution.py:54
  389.3 2.8 convert_element_type.40
  (17 shorter events, 0.3 us)
Async XLA Ops:
  8.0 34.9 %copy-start = (bf16[512,1024]{1,0:T(8,128)(2,1)S(1)}, bf16[512,1024]{1,0:T(8,128)(2,1)}, u32[]{:S(2)}) copy-start(bf16[512,1024]{1,0:T(8,128)(2,1)} %param.8) | copy-start | bytes 3145732
  8.0 34.8 %all-gather.5.cloned.1.call-start = ((), (), s32[]{:S(2)}) async-start(), calls=%async_computation.2 | async-start | bytes 2359296 | tf_op jit(solution)/shard_map/all_gather | solution.py:23
  10.0 116.7 %all-gather.7.cloned.1.call-start = ((), (), s32[]{:S(2)}) async-start(), calls=%async_computation.3 | async-start | bytes 9437184 | tf_op jit(solution)/shard_map/all_gather | solution.py:22
  12.8 168.2 %reduce-scatter.5.cloned.1.call-start = ((), (), s32[]{:S(2)}) async-start(), calls=%async_computation.7 | async-start | bytes 2359296 | tf_op jit(solution)/shard_map/reduce_scatter | solution.py:68
  147.5 35.3 %all-gather.11.cloned.1.call-start = ((), (), s32[]{:S(2)}) async-start(), calls=%async_computation.5 | async-start | bytes 3145728 | tf_op jit(solution)/shard_map/all_gather | solution.py:25
  148.9 224.7 %all-gather.9.cloned.1.call-start = ((), (), s32[]{:S(2)}) async-start(), calls=%async_computation.4 | async-start | bytes 17825792 | tf_op jit(solution)/shard_map/all_gather | solution.py:50
  151.2 238.0 %reduce-scatter.3.cloned.1.call-start = ((), (), s32[]{:S(2)}) async-start(), calls=%async_computation.6 | async-start | bytes 9437184 | tf_op jit(solution)/shard_map/reduce_scatter | solution.py:68
Sparse Core Ops, SparseCore 0:
  11.0 31.7 all-gather.4
  45.0 81.5 all-gather.6
  147.6 33.3 reduce-scatter.4
  183.2 167.4 reduce-scatter.2
Sparse Core Ops, SparseCore 1:
  149.5 30.6 all-gather.10
  182.8 190.8 all-gather.8

commit v2 on v1

v2 whole, which is shorter than its diff:
```python
import functools

import jax
import jax.numpy as jnp
from jax import lax
from jax.experimental import pallas as pl
from jax.experimental.pallas import tpu as pltpu
from jax.sharding import PartitionSpec as P

adapter_scale_factor = 0.25
F32 = jnp.float32
BF16 = jnp.bfloat16
SLOT_AXES = ("fsdp", "sub")


def around(axis):
    count = lax.axis_size(axis)
    return [(i, (i + 1) % count) for i in range(count)]


def line_gather(own):
    count = lax.axis_size("fsdp")
    up, down = [own], [own]
    for step in range(1, count):
        up.append(lax.ppermute(up[-1], "fsdp", [(i, i + 1) for i in range(step - 1, count - 1)]))
        down.append(lax.ppermute(down[-1], "fsdp", [(i, i - 1) for i in range(1, count - step + 1)]))
    return up, down


def in_arrival_order(up, down):
    count, at = lax.axis_size("fsdp"), lax.axis_index("fsdp")
    arrived, whose = [], []
    for step in range(1, count):
        pick, owner = None, 0
        for z in range(count):
            if 2 * z >= count:
                from_up, far = (True, step) if step <= z else (False, step - z)
            else:
                room = count - 1 - z
                from_up, far = (False, step) if step <= room else (True, step - room)
            one = up[far] if from_up else down[far]
            pick = one if pick is None else jnp.where(at == z, one, pick)
            owner = jnp.where(at == z, z - far if from_up else z + far, owner)
        arrived.append(pick)
        whose.append(owner)
    return arrived, whose


def line_scatter_sum(blocks):
    count = lax.axis_size("fsdp")
    from_above = from_below = None
    for step in range(1, count):
        lower = blocks[count - step] if from_above is None else blocks[count - step] + from_above
        upper = blocks[step] if from_below is None else blocks[step] + from_below
        from_above = lax.ppermute(
            lower.astype(BF16), "fsdp", [(i, i - 1) for i in range(count - step, count)]
        ).astype(F32)
        from_below = lax.ppermute(
            upper.astype(BF16), "fsdp", [(i, i + 1) for i in range(step)]
        ).astype(F32)
    total = blocks[0]
    if from_above is not None:
        total = total + from_above + from_below
    return total


def sum_over_tp(part):
    if lax.axis_size("tp") == 2:
        return part + lax.ppermute(part.astype(BF16), "tp", around("tp")).astype(F32)
    return lax.psum(part.astype(BF16), "tp").astype(F32)


def input_gradient_kernel(shards, *refs):
    _, refs = refs[0], refs[1:]
    grads, weights = refs[:shards], refs[shards : 2 * shards]
    wide, factors, out = refs[2 * shards], refs[2 * shards + 1], refs[-1]
    total = jnp.dot(wide[...], factors[...], preferred_element_type=F32)
    for grad, weight in zip(grads, weights, strict=True):
        total += lax.dot_general(
            grad[...], weight[...], (((1,), (1,)), ((), ())), preferred_element_type=F32
        )
    out[...] = total.astype(out.dtype)


def input_gradient_part(scalars, grad_full, weights, wide, factors, so_far):
    tokens, features = wide.shape[0], factors.shape[1]
    shards = len(weights)
    rows, width = weights[0].shape
    block = min(rows, 512)
    steps = rows // block
    grad_spec = [
        pl.BlockSpec((tokens, width), functools.partial(lambda k, j, s: (0, s[k]), k))
        for k in range(shards)
    ]
    weight_spec = [pl.BlockSpec((block, width), lambda j, s: (j, 0)) for _ in range(shards)]
    at = lambda j, s: (0, s[shards] * steps + j)
    in_specs = (
        grad_spec
        + weight_spec
        + [
            pl.BlockSpec(wide.shape, lambda j, s: (0, 0)),
            pl.BlockSpec((factors.shape[0], block), at),
        ]
    )
    operands = [scalars] + [grad_full] * shards + list(weights) + [wide, factors]
    aliases = {}
    if so_far is not None:
        in_specs = in_specs + [pl.BlockSpec(memory_space=pl.ANY)]
        operands.append(so_far)
        aliases = {len(operands) - 1: 0}
    return pl.pallas_call(
        functools.partial(input_gradient_kernel, shards),
        grid_spec=pltpu.PrefetchScalarGridSpec(
            num_scalar_prefetch=1,
            grid=(steps,),
            in_specs=in_specs,
            out_specs=pl.BlockSpec((tokens, block), at),
        ),
        out_shape=jax.ShapeDtypeStruct((tokens, features), BF16),
        input_output_aliases=aliases,
        compiler_params=pltpu.CompilerParams(vmem_limit_bytes=32 * 2**20),
        cost_estimate=pl.CostEstimate(
            flops=2 * tokens * rows * (shards * width + wide.shape[1]),
            bytes_accessed=8 * 2**20,
            transcendentals=0,
        ),
    )(*operands)


def local(activations, output_gradient, base_weight, factor_down, factor_up, counts, owners):
    tokens, features = activations.shape
    columns = output_gradient.shape[1]
    own_slots, rank = factor_down.shape[:2]
    slots = owners.shape[0]
    n, subs = lax.axis_size("fsdp"), lax.axis_size("sub")
    groups = lax.axis_size("groups")
    z, sub, y = lax.axis_index("fsdp"), lax.axis_index("sub"), lax.axis_index("groups")

    up_all = lax.all_gather(factor_up, SLOT_AXES, axis=0, tiled=True)
    down_all = lax.all_gather(factor_down, SLOT_AXES, axis=0, tiled=True)

    copies = groups * subs
    rows, width = base_weight.shape[0] // copies, base_weight.shape[1]
    by_part = base_weight.reshape(copies, rows, width)
    own_rows = lax.dynamic_index_in_dim(by_part, y * subs + sub, 0, keepdims=False)
    arrived, whose = in_arrival_order(*line_gather(own_rows))
    weight_parts = [[] for _ in range(copies)]
    parts = [((y - a) % groups) * subs + (sub - b) % subs for b in range(subs) for a in range(groups)]
    for part, held in zip(parts, weight_parts, strict=True):
        held.append(lax.dynamic_index_in_dim(by_part, part, 0, keepdims=False))
    for mine in arrived:
        over_groups = [mine]
        for _ in range(1, groups):
            over_groups.append(lax.ppermute(over_groups[-1], "groups", around("groups")))
        both = over_groups
        for b in range(subs):
            if b:
                both = [lax.ppermute(one, "sub", around("sub")) for one in both]
            for a in range(groups):
                weight_parts[b * groups + a].append(both[a])
    shard_ids = [z] + whose

    if lax.axis_size("tp") == 2:
        other = lax.ppermute(output_gradient, "tp", around("tp"))
        first = lax.axis_index("tp") == 0
        grad_full = jnp.concatenate(
            [jnp.where(first, output_gradient, other), jnp.where(first, other, output_gradient)], axis=1
        )
    else:
        grad_full = lax.all_gather(output_gradient, "tp", axis=1, tiled=True)

    seg_ends = jnp.cumsum(counts[0])
    seg_starts = seg_ends - counts[0]
    hot = owners[:, None] == lax.broadcasted_iota(jnp.int32, (slots, slots), 1)
    starts = jnp.sum(jnp.where(hot, seg_starts[:, None], 0), axis=0)
    ends = jnp.sum(jnp.where(hot, seg_ends[:, None], 0), axis=0)
    position = lax.broadcasted_iota(jnp.int32, (tokens, slots), 0)
    mask = (position >= starts[None, :]) & (position < ends[None, :])
    by_owner_start = starts.reshape(n, subs, own_slots)
    by_owner_end = ends.reshape(n, subs, own_slots)
    line = [(z - j) % n for j in range(n)]

    def ranged(b):
        s = jnp.concatenate([by_owner_start[at, (sub + b) % subs] for at in line])
        e = jnp.concatenate([by_owner_end[at, (sub + b) % subs] for at in line])
        pos = lax.broadcasted_iota(jnp.int32, (tokens, n * own_slots), 0)
        return (pos >= s[None, :]) & (pos < e[None, :])

    back_part = jnp.einsum("tc,grc->tgr", output_gradient, up_all, preferred_element_type=F32)
    back_sel = jnp.sum(jnp.where(mask[:, :, None], back_part, 0.0), axis=1)
    low_back = adapter_scale_factor * sum_over_tp(back_sel)

    def spread(low, where):
        return jnp.where(where[:, :, None], low[:, None, :], 0.0).astype(BF16)

    pieces = None
    for b in range(subs - 1, -1, -1):
        piece = jnp.einsum(
            "tgr,td->grd", spread(low_back, ranged(b)), activations, preferred_element_type=F32
        )
        if b:
            got = lax.ppermute(piece.astype(BF16), "sub", [(i, (i + b) % subs) for i in range(subs)])
            pieces = got.astype(F32) if pieces is None else pieces + got.astype(F32)
        else:
            pieces = piece if pieces is None else piece + pieces
    grad_down = line_scatter_sum(list(pieces.reshape(n, own_slots, rank, features)))

    low_part = jnp.einsum("td,grd->tgr", activations, down_all, preferred_element_type=F32)
    low_sel = jnp.sum(jnp.where(mask[:, :, None], low_part, 0.0), axis=1)
    low_in = sum_over_tp(low_sel)
    up_pieces = adapter_scale_factor * jnp.einsum(
        "tgr,tc->grc", spread(low_in, mask), output_gradient, preferred_element_type=F32
    )
    up_factor_gradient = jnp.sum(
        lax.all_to_all(
            up_pieces[None].astype(BF16), SLOT_AXES, split_axis=1, concat_axis=0, tiled=True
        ).astype(F32),
        axis=0,
    )

    wide = spread(low_back, mask).reshape(tokens, slots * rank)
    factors = down_all.reshape(slots * rank, features)
    input_gradient = None
    for part, weights in zip(parts, weight_parts, strict=True):
        scalars = jnp.stack(shard_ids + [part]).astype(jnp.int32)
        input_gradient = input_gradient_part(
            scalars, grad_full, weights, wide, factors, input_gradient
        )
    return (input_gradient, grad_down, up_factor_gradient)


def solution(mesh):
    placed = (
        P(("groups", "fsdp", "sub"), "tp"),
        P(("groups", "fsdp", "sub"), "tp"),
        P("tp", "fsdp"),
        P(("groups", "fsdp", "sub"), None, "tp"),
        P(("groups", "fsdp", "sub"), None, "tp"),
        P(("groups", "fsdp", "sub"), None),
        P("groups"),
    )
    return jax.shard_map(
        local,
        mesh=mesh,
        in_specs=placed,
        out_specs=(
            P(("groups", "fsdp", "sub"), "tp"),
            P(("groups", "fsdp", "sub"), None, "tp"),
            P(("groups", "fsdp", "sub"), None, "tp"),
        ),
        check_vma=False,
    )
```

time: 400 us -> 365 us (0.912)
  the two profiles are of different devices: /device:TPU:0 before, /device:TPU:9 now
where the time goes in v2:
time: 365 us; the launch traced here: 364 us
  waiting for transfers between devices  188 us (52%)
  starting transfers between devices  55.6 us (15%)
  local copies, waits for them, and re-layouts  33.3 us (9%)
  Pallas kernels  25.8 us (7%)
  matrix products  24 us (7%)
  other arithmetic  22.6 us (6%)
  between operations  14.6 us (4%)
    ppermute x3, waiting for transfers between devices, line_gather(): lax.ppermute(down[-1], 'fsdp', [(i, i - 1) for i in range(1, count - step...  91.1 us
    ppermute x3, waiting for transfers between devices, line_scatter_sum(): lax.ppermute(lower.astype(BF16), 'fsdp', [(i, i - 1) for i in range(count...  54.2 us
    all_gather x1, waiting for transfers between devices, local(): up_all = lax.all_gather(factor_up, SLOT_AXES, axis=0, tiled=True)  27.3 us
    pallas_call x4, Pallas kernels, input_gradient_part(): pl.pallas_call(functools.partial(input_gradient_kernel, shards), grid_spe...  25.8 us
    all_to_all x1, starting transfers between devices, local(): lax.all_to_all(up_pieces[None].astype(BF16), SLOT_AXES, split_axis=1, con...  12.5 us
    ppermute x3, waiting for transfers between devices, local(): lax.ppermute(over_groups[-1], 'groups', around('groups'))  12.1 us
    unnamed x34, local copies, waits for them, and re-layouts  11.5 us
    all_gather x1, local copies, waits for them, and re-layouts, local(): down_all = lax.all_gather(factor_down, SLOT_AXES, axis=0, tiled=True)  11.3 us
  transfers between devices with their start and end apart: 28, of which 8 were waited for; matrix products, arithmetic and copies ran while one was open for 19% of the time, Pallas kernels for 7%

profile of v2, /device:TPU:9, one launch (start us, length us, event | category | flops | bytes accessed | tf_op | source)
XLA Modules:
  0.0 364.3 jit_solution(14387759905069834834)
XLA Ops:
  13.6 27.3 %all-gather.3.cloned.1.call-done = bf16[64,16,1024]{2,0,1:T(8,128)(2,1)} async-done(((bf16[8,16,1024]{2,0,1:T(8,128)(2,1)}), bf16[64,16,1024]{2,0,1:T(8,128)(2,1)}) %all-gather.3.cloned.1.call-update) | async-done | bytes 2097168 | tf_op jit(solution)/shard_map/all_gather | solution.py:139
  46.6 4.4 %convolution_convert_fusion = bf16[32,16,4096]{2,1,0:T(8,128)(2,1)} fusion(bf16[512,4096]{1,0:T(8,128)(2,1)S(1)} %copy-done.9, bf16[512,16]{0,1:T(8,128)(2,1)S(1)} %add_multiply_fusion, pred[512,32]{0,1:T(8,128)(4,1)S(1)} %fusion.22), kind=kOutput, calls=%fused_computation.1 | convolution fusion | flops 2149842944 | bytes 8421376 | tf_op jit(solution)/shard_map/tgr,td->grd/dot_general | solution.py:198
  52.6 4.8 %dynamic-slice_bitcast_fusion = (bf16[1024,512]{1,0:T(8,128)(2,1)}, bf16[1024,512]{1,0:T(8,128)(2,1)}, bf16[1024,512]{1,0:T(8,128)(2,1)}, bf16[1024,512]{1,0:T(8,128)(2,1)S(1)}, bf16[1024,512]{1,0:T(8,128)(2,1)}) fusion(bf16[4,1024,512]{2,1,0:T(8,128)(2,1)} %bitcast.84, s32[]{:T(128)S(6)} %select_n.294, s32[]{:T(128)S(6)} %select_n.293, s32[]{:T(128)S(6)} %select_n.291, ...), kind=kLoop, calls=%fused_computation.30 | loop fusion | bytes 10485780 | tf_op jit(solution)/shard_map/jit(dynamic_index_in_dim)/squeeze | solution.py:150
  59.5 3.1 collective-permute-start.1
  62.8 4.6 %convert_add_fusion = f32[32,16,4096]{2,1,0:T(8,128)S(1)} fusion(bf16[32,16,4096]{2,1,0:T(8,128)(2,1)} %collective-permute-done.17, bf16[512,4096]{1,0:T(8,128)(2,1)S(1)} %copy-done.10, bf16[512,16]{0,1:T(8,128)(2,1)S(1)} %add_multiply_fusion, pred[512,32]{0,1:T(8,128)(4,1)S(1)} %fusion.21), kind=kOutput, calls=%fused_computation | convolution fusion | flops 2151940096 | bytes 16809984 | tf_op jit(solution)/shard_map/tgr,td->grd/dot_general | solution.py:198
  69.6 62.9 %collective-permute-done.2 = bf16[1024,512]{1,0:T(8,128)(2,1)} collective-permute-done((bf16[1024,512]{1,0:T(8,128)(2,1)S(1)}, bf16[1024,512]{1,0:T(8,128)(2,1)}, u32[]{:S(2)}, u32[]{:S(2)}) %collective-permute-start.2) | collective-permute-done | bytes 1048608 | tf_op jit(solution)/shard_map/ppermute | solution.py:26
  132.4 4.2 %collective-permute-start.6 = (bf16[1024,512]{1,0:T(8,128)(2,1)}, bf16[1024,512]{1,0:T(8,128)(2,1)S(1)}, u32[]{:S(2)}, u32[]{:S(2)}) collective-permute-start(bf16[1024,512]{1,0:T(8,128)(2,1)} %collective-permute-done.2), channel_id=1, source_target_pairs={{4,0},{8,4},{5,1},{9,5},{6,2},{10,6},{7,3},{11,7},{20,16},{24,20},... | collective-permute-start | bytes 3145736 | tf_op jit(solution)/shard_map/ppermute | solution.py:26
  144.0 28.2 %collective-permute-done.6 = bf16[1024,512]{1,0:T(8,128)(2,1)S(1)} collective-permute-done((bf16[1024,512]{1,0:T(8,128)(2,1)}, bf16[1024,512]{1,0:T(8,128)(2,1)S(1)}, u32[]{:S(2)}, u32[]{:S(2)}) %collective-permute-start.6) | collective-permute-done | bytes 1048608 | tf_op jit(solution)/shard_map/ppermute | solution.py:26
  179.5 15.2 %collective-permute-done.19 = bf16[8,16,4096]{2,1,0:T(8,128)(2,1)} collective-permute-done((bf16[8,16,4096]{2,1,0:T(8,128)(2,1)}, bf16[8,16,4096]{2,1,0:T(8,128)(2,1)}, u32[]{:S(2)}, u32[]{:S(2)}) %collective-permute-start.19) | collective-permute-done | bytes 1048608 | tf_op jit(solution)/shard_map/ppermute | solution.py:55
  196.4 4.7 %add_convert_fusion.2 = (bf16[8,16,4096]{2,1,0:T(8,128)(2,1)}, bf16[8,16,4096]{2,1,0:T(8,128)(2,1)}) fusion(bf16[8,16,4096]{2,1,0:T(8,128)(2,1)} %collective-permute-done.19, f32[32,16,4096]{2,1,0:T(8,128)} %copy-done.8, bf16[8,16,4096]{2,1,0:T(8,128)(2,1)} %collective-permute-done.21), kind=kLoop, calls=%fused_computation.16 | loop fusion | flops 3145728 | bytes 8388608 | tf_op jit(solution)/shard_map/convert_element_type | solution.py:56
  201.1 9.2 %select_reduce_fusion = f32[512,16]{0,1:T(8,128)S(1)} fusion(bf16[64,16,4096]{2,0,1:T(8,128)(2,1)} %all-gather.5.cloned.1.call-done, bf16[512,4096]{1,0:T(8,128)(2,1)} %param.7, pred[512,64]{0,1:T(8,128)(4,1)S(1)} %fusion.20), kind=kOutput, calls=%fused_computation.13 | convolution fusion | flops 4296007680 | bytes 12648448 | tf_op jit(solution)/shard_map/td,grd->tgr/dot_general | solution.py:208
  221.7 12.5 %all-to-all-start = ((bf16[1,64,16,1024]{3,2,0,1:T(8,128)(2,1)}), bf16[1,64,16,1024]{3,2,0,1:T(8,128)(2,1)}, u32[]{:S(2)}, u32[]{:S(2)}) async-start(bf16[1,64,16,1024]{3,2,0,1:T(8,128)(2,1)} %fusion.8), calls=%async_computation | async-start | bytes 4194304 | tf_op jit(solution)/shard_map/all_to_all | solution.py:215
  237.7 3.1 add_convert_fusion
  242.7 3.6 collective-permute-start.23
  247.1 3.6 collective-permute-start.14
  250.7 12.1 %collective-permute-done.3.refs_6_ = bf16[1024,512]{1,0:T(8,128)(2,1)} collective-permute-done((bf16[1024,512]{1,0:T(8,128)(2,1)}, bf16[1024,512]{1,0:T(8,128)(2,1)}, u32[]{:S(2)}, u32[]{:S(2)}) %collective-permute-start.3) | collective-permute-done | bytes 1048608 | tf_op jit(solution)/shard_map/ppermute | solution.py:154
  264.9 39.0 %collective-permute-done.20 = bf16[8,16,4096]{2,1,0:T(8,128)(2,1)} collective-permute-done((bf16[8,16,4096]{2,1,0:T(8,128)(2,1)}, bf16[8,16,4096]{2,1,0:T(8,128)(2,1)}, u32[]{:S(2)}, u32[]{:S(2)}) %collective-permute-start.20) | collective-permute-done | bytes 1048608 | tf_op jit(solution)/shard_map/ppermute | solution.py:55
  304.8 3.8 %fusion.7 = f32[8,16,4096]{2,1,0:T(8,128)} fusion(f32[32,16,4096]{2,1,0:T(8,128)} %copy-done.8, bf16[8,16,4096]{2,1,0:T(8,128)(2,1)} %collective-permute-done.23, bf16[8,16,4096]{2,1,0:T(8,128)(2,1)} %collective-permute-done.20), kind=kLoop, calls=%fused_computation.10 | loop fusion | flops 2097152 | bytes 6291456 | tf_op jit(solution)/shard_map/add | solution.py:63
  308.6 11.3 %copy.44 = bf16[64,16,4096]{2,1,0:T(8,128)(2,1)} copy(bf16[64,16,4096]{2,0,1:T(8,128)(2,1)} %all-gather.5.cloned.1.call-done) | data formatting | bytes 16777216 | tf_op jit(solution)/shard_map/all_gather | solution.py:140
  323.0 3.4 copy-done
  328.8 6.5 %shard_map.94.refs_11_ = bf16[512,4096]{1,0:T(8,128)(2,1)} custom-call(s32[5]{0:T(128)S(1)} %stack.59.refs_0_, bf16[512,2048]{1,0:T(8,128)(2,1)S(1)} %pad_maximum_fusion.refs_1_.refs_2_.refs_3_.refs_4_, bf16[512,2048]{1,0:T(8,128)(2,1)S(1)} %pad_maximum_fusion.refs_1_.refs_2_.refs_3_.refs_4_, ...), custom_call_target="tpu_custom_call" | custom-call | flops 3221225472 | bytes 8388608 | tf_op jit(solution)/shard_map/pallas_call | solution.py:111
  335.3 6.4 %shard_map.95.refs_11_ = bf16[512,4096]{1,0:T(8,128)(2,1)} custom-call(s32[5]{0:T(128)S(1)} %stack.57.refs_0_, bf16[512,2048]{1,0:T(8,128)(2,1)S(1)} %pad_maximum_fusion.refs_1_.refs_2_.refs_3_.refs_4_, bf16[512,2048]{1,0:T(8,128)(2,1)S(1)} %pad_maximum_fusion.refs_1_.refs_2_.refs_3_.refs_4_, ...), custom_call_target="tpu_custom_call", output_to_operand_aliasing={{}: (11, {})} | custom-call | flops 3221225472 | bytes 8388608 | tf_op jit(solution)/shard_map/pallas_call | solution.py:111
  341.8 6.4 %shard_map.96.refs_11_ = bf16[512,4096]{1,0:T(8,128)(2,1)} custom-call(s32[5]{0:T(128)S(1)} %stack.55.refs_0_, bf16[512,2048]{1,0:T(8,128)(2,1)S(1)} %pad_maximum_fusion.refs_1_.refs_2_.refs_3_.refs_4_, bf16[512,2048]{1,0:T(8,128)(2,1)S(1)} %pad_maximum_fusion.refs_1_.refs_2_.refs_3_.refs_4_, ...), custom_call_target="tpu_custom_call", output_to_operand_aliasing={{}: (11, {})} | custom-call | flops 3221225472 | bytes 8388608 | tf_op jit(solution)/shard_map/pallas_call | solution.py:111
  348.2 6.4 %shard_map.97 = bf16[512,4096]{1,0:T(8,128)(2,1)} custom-call(s32[5]{0:T(128)S(1)} %stack.53.refs_0_, bf16[512,2048]{1,0:T(8,128)(2,1)S(1)} %pad_maximum_fusion.refs_1_.refs_2_.refs_3_.refs_4_, bf16[512,2048]{1,0:T(8,128)(2,1)S(1)} %pad_maximum_fusion.refs_1_.refs_2_.refs_3_.refs_4_, ...), custom_call_target="tpu_custom_call", output_to_operand_aliasing={{}: (11, {})} | custom-call | flops 3221225472 | bytes 8388608 | tf_op jit(solution)/shard_map/pallas_call | solution.py:111
  (114 shorter events, 63.1 us)
Async XLA Ops:
  7.2 33.7 %all-gather.3.cloned.1.call-start = ((), (), s32[]{:S(2)}) async-start(), calls=%async_computation.1 | async-start | bytes 2359296 | tf_op jit(solution)/shard_map/all_gather | solution.py:139
  9.2 191.9 %all-gather.5.cloned.1.call-start = ((), (), s32[]{:S(2)}) async-start(), calls=%async_computation.2 | async-start | bytes 9437184 | tf_op jit(solution)/shard_map/all_gather | solution.py:140
  57.3 75.1 %collective-permute-start.2 = (bf16[1024,512]{1,0:T(8,128)(2,1)S(1)}, bf16[1024,512]{1,0:T(8,128)(2,1)}, u32[]{:S(2)}, u32[]{:S(2)}) collective-permute-start(bf16[1024,512]{1,0:T(8,128)(2,1)S(1)} %get-tuple-element.12), channel_id=1, source_target_pairs={{4,0},{8,4},{12,8},{5,1},{9,5},{13,9},{6,2},{10,6},{14,10},{7,3},{... | collective-permute-start | bytes 3145736 | tf_op jit(solution)/shard_map/ppermute | solution.py:26
  59.5 77.1 %collective-permute-start.1 = (bf16[1024,512]{1,0:T(8,128)(2,1)S(1)}, bf16[1024,512]{1,0:T(8,128)(2,1)}, u32[]{:S(2)}, u32[]{:S(2)}) collective-permute-start(bf16[1024,512]{1,0:T(8,128)(2,1)S(1)} %get-tuple-element.12), channel_id=1, source_target_pairs={{0,4},{4,8},{8,12},{1,5},{5,9},{9,13},{2,6},{6,10},{10,14},{3,7},{... | collective-permute-start | bytes 3145736 | tf_op jit(solution)/shard_map/ppermute | solution.py:25
  68.8 71.4 %collective-permute-start.18 = (bf16[8,16,4096]{2,1,0:T(8,128)(2,1)S(1)}, bf16[8,16,4096]{2,1,0:T(8,128)(2,1)S(1)}, u32[]{:S(2)}, u32[]{:S(2)}) collective-permute-start(bf16[8,16,4096]{2,1,0:T(8,128)(2,1)S(1)} %get-tuple-element.7), channel_id=1, source_target_pairs={{12,8},{13,9},{14,10},{15,11},{28,24},{29,25},{30,26},{31,27}} | collective-permute-start | bytes 3145736 | tf_op jit(solution)/shard_map/ppermute | solution.py:55
  132.4 39.7 %collective-permute-start.6 = (bf16[1024,512]{1,0:T(8,128)(2,1)}, bf16[1024,512]{1,0:T(8,128)(2,1)S(1)}, u32[]{:S(2)}, u32[]{:S(2)}) collective-permute-start(bf16[1024,512]{1,0:T(8,128)(2,1)} %collective-permute-done.2), channel_id=1, source_target_pairs={{4,0},{8,4},{5,1},{9,5},{6,2},{10,6},{7,3},{11,7},{20,16},{24,20},... | collective-permute-start | bytes 3145736 | tf_op jit(solution)/shard_map/ppermute | solution.py:26
  136.6 36.5 %collective-permute-start.5 = (bf16[1024,512]{1,0:T(8,128)(2,1)}, bf16[1024,512]{1,0:T(8,128)(2,1)}, u32[]{:S(2)}, u32[]{:S(2)}) collective-permute-start(bf16[1024,512]{1,0:T(8,128)(2,1)} %collective-permute-done.1), channel_id=1, source_target_pairs={{4,8},{8,12},{5,9},{9,13},{6,10},{10,14},{7,11},{11,15},{20,24},{2... | collective-permute-start | bytes 3145736 | tf_op jit(solution)/shard_map/ppermute | solution.py:25
  138.9 38.4 %collective-permute-start.21 = (bf16[8,16,4096]{2,1,0:T(8,128)(2,1)}, bf16[8,16,4096]{2,1,0:T(8,128)(2,1)}, u32[]{:S(2)}, u32[]{:S(2)}) collective-permute-start(bf16[8,16,4096]{2,1,0:T(8,128)(2,1)} %get-tuple-element.8), channel_id=1, source_target_pairs={{0,4},{1,5},{2,6},{3,7},{16,20},{17,21},{18,22},{19,23}} | collective-permute-start | bytes 3145736 | tf_op jit(solution)/shard_map/ppermute | solution.py:58
  141.4 53.3 %collective-permute-start.19 = (bf16[8,16,4096]{2,1,0:T(8,128)(2,1)}, bf16[8,16,4096]{2,1,0:T(8,128)(2,1)}, u32[]{:S(2)}, u32[]{:S(2)}) collective-permute-start(bf16[8,16,4096]{2,1,0:T(8,128)(2,1)} %add_convert_fusion.3), channel_id=1, source_target_pairs={{8,4},{12,8},{9,5},{13,9},{10,6},{14,10},{11,7},{15,11},{24,20},{2... | collective-permute-start | bytes 3145736 | tf_op jit(solution)/shard_map/ppermute | solution.py:55
  142.7 98.1 %collective-permute-start = (bf16[512,1024]{1,0:T(8,128)(2,1)S(1)}, bf16[512,1024]{1,0:T(8,128)(2,1)S(1)}, u32[]{:S(2)}, u32[]{:S(2)}) collective-permute-start(bf16[512,1024]{1,0:T(8,128)(2,1)S(1)} %copy-done.12), channel_id=1, source_target_pairs={{0,2},{2,0},{1,3},{3,1},{4,6},{6,4},{5,7},{7,5},{8,10},{10,8},{9,1... | collective-permute-start | bytes 3145736 | tf_op jit(solution)/shard_map/ppermute | solution.py:164
  174.8 67.9 %collective-permute-start.7 = (bf16[1024,512]{1,0:T(8,128)(2,1)S(1)}, bf16[1024,512]{1,0:T(8,128)(2,1)}, u32[]{:S(2)}, u32[]{:S(2)}) collective-permute-start(bf16[1024,512]{1,0:T(8,128)(2,1)S(1)} %select_select_fusion.refs_7_), channel_id=1, source_target_pairs={{0,16},{16,0},{1,17},{17,1},{2,18},{18,2},{3,19},{19,3},{4,20},{20... | collective-permute-start | bytes 3145736 | tf_op jit(solution)/shard_map/ppermute | solution.py:154
  176.1 71.0 %collective-permute-start.15 = (bf16[1024,512]{1,0:T(8,128)(2,1)S(1)}, bf16[1024,512]{1,0:T(8,128)(2,1)}, u32[]{:S(2)}, u32[]{:S(2)}) collective-permute-start(bf16[1024,512]{1,0:T(8,128)(2,1)S(1)} %select_select_fusion.refs_7_), channel_id=1, source_target_pairs={{0,1},{1,0},{2,3},{3,2},{4,5},{5,4},{6,7},{7,6},{8,9},{9,8},{10,11... | collective-permute-start | bytes 3145736 | tf_op jit(solution)/shard_map/ppermute | solution.py:158
  177.3 33.0 %collective-permute-start.10 = (bf16[1024,512]{1,0:T(8,128)(2,1)}, bf16[1024,512]{1,0:T(8,128)(2,1)}, u32[]{:S(2)}, u32[]{:S(2)}) collective-permute-start(bf16[1024,512]{1,0:T(8,128)(2,1)} %copy-done.13), channel_id=1, source_target_pairs={{4,0},{5,1},{6,2},{7,3},{20,16},{21,17},{22,18},{23,19}} | collective-permute-start | bytes 3145736 | tf_op jit(solution)/shard_map/ppermute | solution.py:26
  210.3 26.2 %collective-permute-start.22 = (bf16[8,16,4096]{2,1,0:T(8,128)(2,1)}, bf16[8,16,4096]{2,1,0:T(8,128)(2,1)}, u32[]{:S(2)}, u32[]{:S(2)}) collective-permute-start(bf16[8,16,4096]{2,1,0:T(8,128)(2,1)} %get-tuple-element.6), channel_id=1, source_target_pairs={{0,4},{4,8},{1,5},{5,9},{2,6},{6,10},{3,7},{7,11},{16,20},{20,24},... | collective-permute-start | bytes 3145736 | tf_op jit(solution)/shard_map/ppermute | solution.py:58
  216.5 34.1 %collective-permute-start.11 = (bf16[1024,512]{1,0:T(8,128)(2,1)}, bf16[1024,512]{1,0:T(8,128)(2,1)}, u32[]{:S(2)}, u32[]{:S(2)}) collective-permute-start(bf16[1024,512]{1,0:T(8,128)(2,1)} %get-tuple-element.14.refs_8_), channel_id=1, source_target_pairs={{0,16},{16,0},{1,17},{17,1},{2,18},{18,2},{3,19},{19,3},{4,20},{20... | collective-permute-start | bytes 3145736 | tf_op jit(solution)/shard_map/ppermute | solution.py:154
  221.7 132.9 %all-to-all-start = ((bf16[1,64,16,1024]{3,2,0,1:T(8,128)(2,1)}), bf16[1,64,16,1024]{3,2,0,1:T(8,128)(2,1)}, u32[]{:S(2)}, u32[]{:S(2)}) async-start(bf16[1,64,16,1024]{3,2,0,1:T(8,128)(2,1)} %fusion.8), calls=%async_computation | async-start | bytes 4194304 | tf_op jit(solution)/shard_map/all_to_all | solution.py:215
  236.5 26.4 %collective-permute-start.3 = (bf16[1024,512]{1,0:T(8,128)(2,1)}, bf16[1024,512]{1,0:T(8,128)(2,1)}, u32[]{:S(2)}, u32[]{:S(2)}) collective-permute-start(bf16[1024,512]{1,0:T(8,128)(2,1)} %get-tuple-element.15.refs_6_), channel_id=1, source_target_pairs={{0,16},{16,0},{1,17},{17,1},{2,18},{18,2},{3,19},{19,3},{4,20},{20... | collective-permute-start | bytes 3145736 | tf_op jit(solution)/shard_map/ppermute | solution.py:154
  240.8 63.1 %collective-permute-start.20 = (bf16[8,16,4096]{2,1,0:T(8,128)(2,1)}, bf16[8,16,4096]{2,1,0:T(8,128)(2,1)}, u32[]{:S(2)}, u32[]{:S(2)}) collective-permute-start(bf16[8,16,4096]{2,1,0:T(8,128)(2,1)} %get-tuple-element.5), channel_id=1, source_target_pairs={{4,0},{8,4},{12,8},{5,1},{9,5},{13,9},{6,2},{10,6},{14,10},{7,3},{... | collective-permute-start | bytes 3145736 | tf_op jit(solution)/shard_map/ppermute | solution.py:55
  242.7 62.0 %collective-permute-start.23 = (bf16[8,16,4096]{2,1,0:T(8,128)(2,1)}, bf16[8,16,4096]{2,1,0:T(8,128)(2,1)}, u32[]{:S(2)}, u32[]{:S(2)}) collective-permute-start(bf16[8,16,4096]{2,1,0:T(8,128)(2,1)} %add_convert_fusion), channel_id=1, source_target_pairs={{0,4},{4,8},{8,12},{1,5},{5,9},{9,13},{2,6},{6,10},{10,14},{3,7},{... | collective-permute-start | bytes 3145736 | tf_op jit(solution)/shard_map/ppermute | solution.py:58
  247.1 94.7 %collective-permute-start.14 = (bf16[1024,512]{1,0:T(8,128)(2,1)}, bf16[1024,512]{1,0:T(8,128)(2,1)}, u32[]{:S(2)}, u32[]{:S(2)}) collective-permute-start(bf16[1024,512]{1,0:T(8,128)(2,1)} %get-tuple-element.15.refs_6_), channel_id=1, source_target_pairs={{0,1},{1,0},{2,3},{3,2},{4,5},{5,4},{6,7},{7,6},{8,9},{9,8},{10,11... | collective-permute-start | bytes 3145736 | tf_op jit(solution)/shard_map/ppermute | solution.py:158
  250.7 91.1 %collective-permute-start.16 = (bf16[1024,512]{1,0:T(8,128)(2,1)}, bf16[1024,512]{1,0:T(8,128)(2,1)}, u32[]{:S(2)}, u32[]{:S(2)}) collective-permute-start(bf16[1024,512]{1,0:T(8,128)(2,1)} %get-tuple-element.14.refs_8_), channel_id=1, source_target_pairs={{0,1},{1,0},{2,3},{3,2},{4,5},{5,4},{6,7},{7,6},{8,9},{9,8},{10,11... | collective-permute-start | bytes 3145736 | tf_op jit(solution)/shard_map/ppermute | solution.py:158
  262.9 85.3 %collective-permute-start.8 = (bf16[1024,512]{1,0:T(8,128)(2,1)}, bf16[1024,512]{1,0:T(8,128)(2,1)}, u32[]{:S(2)}, u32[]{:S(2)}) collective-permute-start(bf16[1024,512]{1,0:T(8,128)(2,1)} %collective-permute-done.7.refs_7_), channel_id=1, source_target_pairs={{0,1},{1,0},{2,3},{3,2},{4,5},{5,4},{6,7},{7,6},{8,9},{9,8},{10,11... | collective-permute-start | bytes 3145736 | tf_op jit(solution)/shard_map/ppermute | solution.py:158
  303.9 44.3 %collective-permute-start.12 = (bf16[1024,512]{1,0:T(8,128)(2,1)}, bf16[1024,512]{1,0:T(8,128)(2,1)}, u32[]{:S(2)}, u32[]{:S(2)}) collective-permute-start(bf16[1024,512]{1,0:T(8,128)(2,1)} %collective-permute-done.11.refs_8_), channel_id=1, source_target_pairs={{0,1},{1,0},{2,3},{3,2},{4,5},{5,4},{6,7},{7,6},{8,9},{9,8},{10,11... | collective-permute-start | bytes 3145736 | tf_op jit(solution)/shard_map/ppermute | solution.py:158
  304.8 43.4 %collective-permute-start.4 = (bf16[1024,512]{1,0:T(8,128)(2,1)}, bf16[1024,512]{1,0:T(8,128)(2,1)}, u32[]{:S(2)}, u32[]{:S(2)}) collective-permute-start(bf16[1024,512]{1,0:T(8,128)(2,1)} %collective-permute-done.3.refs_6_), channel_id=1, source_target_pairs={{0,1},{1,0},{2,3},{3,2},{4,5},{5,4},{6,7},{7,6},{8,9},{9,8},{10,11... | collective-permute-start | bytes 3145736 | tf_op jit(solution)/shard_map/ppermute | solution.py:158
  (20 other events, 242.0 us)
Sparse Core Ops, SparseCore 0:
  10.2 30.6 all-gather.2
  42.5 128.3 all-gather.4

commit v3 on v1

v3 whole, which is shorter than its diff:
```python
import functools

import jax
import jax.numpy as jnp
from jax import lax
from jax.experimental import pallas as pl
from jax.experimental.pallas import tpu as pltpu
from jax.sharding import PartitionSpec as P

adapter_scale_factor = 0.25
F32 = jnp.float32
BF16 = jnp.bfloat16
LANES = 128
TRANS_B = (((1,), (1,)), ((), ()))
SMALL = pl.CostEstimate(flops=1, bytes_accessed=1, transcendentals=0)
TRANS_A = (((0,), (0,)), ((), ()))


def after(value, *earlier):
    return lax.optimization_barrier((value, *earlier))[0]


def around(axis):
    count = lax.axis_size(axis)
    return [(i, (i + 1) % count) for i in range(count)]


def line_step(up, down, step):
    count = lax.axis_size("fsdp")
    return (
        lax.ppermute(up, "fsdp", [(i, i + 1) for i in range(step - 1, count - 1)]),
        lax.ppermute(down, "fsdp", [(i, i - 1) for i in range(1, count - step + 1)]),
    )


def arrival(up, down, step):
    count, at = lax.axis_size("fsdp"), lax.axis_index("fsdp")
    choices = {}
    owner = 0
    for z in range(count):
        if 2 * z >= count:
            from_up, far = (True, step) if step <= z else (False, step - z)
        else:
            room = count - 1 - z
            from_up, far = (False, step) if step <= room else (True, step - room)
        choices.setdefault((from_up, far), []).append(z)
        owner = jnp.where(at == z, z - far if from_up else z + far, owner)
    pick = None
    for (from_up, far), places in choices.items():
        one = up[far] if from_up else down[far]
        if pick is None:
            pick = one
        else:
            here = functools.reduce(jnp.logical_or, [at == z for z in places])
            pick = jnp.where(here, one, pick)
    return pick, owner


def sum_over_tp(part):
    if lax.axis_size("tp") == 2:
        return part + lax.ppermute(part.astype(BF16), "tp", around("tp")).astype(F32)
    return lax.psum(part.astype(BF16), "tp").astype(F32)


def over_cores(one):
    every = [one]
    for _ in range(1, lax.axis_size("sub")):
        every.append(lax.ppermute(every[-1], "sub", around("sub")))
    return every


def in_range(start, end, at, tokens):
    start, end = start[at : at + 1, :], end[at : at + 1, :]
    position = lax.broadcasted_iota(jnp.int32, (tokens, start.shape[1]), 0)
    return (position >= start) & (position < end)


def low_kernel(sources, count, rank, with_prior, *refs):
    xs, refs = refs[:sources], refs[sources:]
    blocks, (start, end), refs = refs[:count], refs[count : count + 2], refs[count + 2 :]
    prior = refs[0] if with_prior else None
    out, total = refs[-2:]
    tokens = xs[0].shape[0]
    step = pl.program_id(0)
    rows = jnp.concatenate([block[...] for block in blocks], axis=0)
    for at, x in enumerate(xs):
        here = pl.ds(at * tokens, tokens)
        part = lax.dot_general(x[...], rows, TRANS_B, preferred_element_type=F32)

        @pl.when(step == 0)
        def _():
            total[here, :] = part

        @pl.when(step > 0)
        def _():
            total[here, :] += part

        @pl.when(step == pl.num_programs(0) - 1)
        def _():
            chosen = jnp.where(in_range(start, end, at, tokens), total[here, :], 0.0)
            low = chosen[:, :LANES]
            for lane in range(LANES, chosen.shape[1], LANES):
                low = low + chosen[:, lane : lane + LANES]
            turn = LANES // 2
            while turn >= rank:
                low = low + pltpu.roll(low, turn, 1)
                turn //= 2
            out[here, :] = low + prior[here, :] if with_prior else low


def low_rank(xs, blocks, start, end, rank, prior=None):
    tokens, depth = xs[0].shape
    chunk = min(depth, 1024)
    columns = start.shape[1]
    rows = len(xs) * tokens
    fixed = lambda shape: pl.BlockSpec(shape, lambda k: (0, 0))
    operands = [*xs, *blocks, start, end] + ([] if prior is None else [prior])
    in_specs = [pl.BlockSpec((tokens, chunk), lambda k: (0, k)) for _ in xs]
    in_specs += [pl.BlockSpec((b.shape[0], chunk), lambda k: (0, k)) for b in blocks]
    in_specs += [fixed(start.shape), fixed(end.shape)]
    if prior is not None:
        in_specs.append(fixed((rows, LANES)))
    return pl.pallas_call(
        functools.partial(low_kernel, len(xs), len(blocks), rank, prior is not None),
        grid=(depth // chunk,),
        in_specs=in_specs,
        out_specs=fixed((rows, LANES)),
        out_shape=jax.ShapeDtypeStruct((rows, LANES), F32),
        scratch_shapes=[pltpu.VMEM((rows, columns), F32)],
        compiler_params=pltpu.CompilerParams(vmem_limit_bytes=24 * 2**20),
        cost_estimate=SMALL,
    )(*operands)


def spread(low, start, end, at):
    tokens, columns = low.shape[0], start.shape[1]
    repeated = jnp.concatenate([low] * (columns // LANES), axis=1)
    return jnp.where(in_range(start, end, at, tokens), repeated, 0.0).astype(BF16)


def spread_kernel(low, start, end, out):
    out[...] = spread(low[...], start, end, 0)


def spread_out(low, start, end):
    return pl.pallas_call(
        spread_kernel,
        out_shape=jax.ShapeDtypeStruct((low.shape[0], start.shape[1]), BF16),
        compiler_params=pltpu.CompilerParams(vmem_limit_bytes=24 * 2**20),
        cost_estimate=SMALL,
    )(low, start, end)


def outer_kernel(scale, parts, low, start, end, *refs):
    xs, outs, wide = refs[: -1 - parts], refs[-1 - parts : -1], refs[-1]
    tokens = xs[0].shape[0]

    @pl.when(pl.program_id(0) == 0)
    def _():
        for at in range(len(xs)):
            here = pl.ds(at * tokens, tokens)
            wide[here, :] = spread(low[here, :], start, end, at)

    total = None
    for at, x in enumerate(xs):
        part = lax.dot_general(
            wide[pl.ds(at * tokens, tokens), :], x[...], TRANS_A, preferred_element_type=F32
        )
        total = part if total is None else total + part
    if scale != 1.0:
        total = total * scale
    rows = total.shape[0] // parts
    for at, out in enumerate(outs):
        out[...] = total[at * rows : (at + 1) * rows]


def outer(low, start, end, xs, scale, parts):
    tokens, features = xs[0].shape
    columns = start.shape[1]
    rows = columns // parts
    chunk = min(features, 512)
    fixed = lambda shape: pl.BlockSpec(shape, lambda k: (0, 0))
    moving = lambda count: pl.BlockSpec((count, chunk), lambda k: (0, k))
    return pl.pallas_call(
        functools.partial(outer_kernel, scale, parts),
        grid=(features // chunk,),
        in_specs=[fixed(low.shape), fixed(start.shape), fixed(end.shape)] + [moving(tokens)] * len(xs),
        out_specs=[moving(rows)] * parts,
        out_shape=[jax.ShapeDtypeStruct((rows, features), F32)] * parts,
        scratch_shapes=[pltpu.VMEM((len(xs) * tokens, columns), BF16)],
        compiler_params=pltpu.CompilerParams(vmem_limit_bytes=32 * 2**20),
        cost_estimate=SMALL,
    )(low, start, end, *xs)


def input_gradient_kernel(shards, factor_blocks, _, *refs):
    grads, weights = refs[:shards], refs[shards : 2 * shards]
    wide = refs[2 * shards]
    factors = refs[2 * shards + 1 : 2 * shards + 1 + factor_blocks]
    out = refs[-1]
    rows = jnp.concatenate([factor[...] for factor in factors], axis=0)
    total = jnp.dot(wide[...], rows, preferred_element_type=F32)
    for grad, weight in zip(grads, weights, strict=True):
        total += lax.dot_general(grad[...], weight[...], TRANS_B, preferred_element_type=F32)
    out[...] = total.astype(out.dtype)


def input_gradient_part(scalars, copies, grad_full, weights, wide, factors, so_far):
    tokens, features = wide.shape[0], factors[0].shape[1]
    shards = len(weights)
    rows, width = weights[-1].shape[0] if shards > 1 else features // copies, weights[0].shape[1]
    block = min(rows, 512)
    steps = rows // block
    at = lambda j, s: (0, s[shards] * steps + j)
    in_specs = [
        pl.BlockSpec((tokens, width), functools.partial(lambda k, j, s: (0, s[k]), k))
        for k in range(shards)
    ]
    in_specs.append(pl.BlockSpec((block, width), lambda j, s: (s[shards] * steps + j, 0)))
    in_specs += [pl.BlockSpec((block, width), lambda j, s: (j, 0)) for _ in range(shards - 1)]
    in_specs += [pl.BlockSpec(wide.shape, lambda j, s: (0, 0))]
    in_specs += [pl.BlockSpec((factor.shape[0], block), at) for factor in factors]
    operands = [scalars] + [grad_full] * shards + list(weights) + [wide] + list(factors)
    aliases = {}
    if so_far is not None:
        in_specs.append(pl.BlockSpec(memory_space=pl.ANY))
        operands.append(so_far)
        aliases = {len(operands) - 1: 0}
    return pl.pallas_call(
        functools.partial(input_gradient_kernel, shards, len(factors)),
        grid_spec=pltpu.PrefetchScalarGridSpec(
            num_scalar_prefetch=1,
            grid=(steps,),
            in_specs=in_specs,
            out_specs=pl.BlockSpec((tokens, block), at),
        ),
        out_shape=jax.ShapeDtypeStruct((tokens, features), BF16),
        input_output_aliases=aliases,
        compiler_params=pltpu.CompilerParams(vmem_limit_bytes=32 * 2**20),
        cost_estimate=SMALL,
    )(*operands)


def local(activations, output_gradient, base_weight, factor_down, factor_up, counts, owners):
    tokens, features = activations.shape
    columns = output_gradient.shape[1]
    own_slots, rank = factor_down.shape[:2]
    slots = owners.shape[0]
    n, subs, groups = lax.axis_size("fsdp"), lax.axis_size("sub"), lax.axis_size("groups")
    z, sub, y = lax.axis_index("fsdp"), lax.axis_index("sub"), lax.axis_index("groups")
    own_rows = own_slots * rank
    other_core = [(i, (i + 1) % subs) for i in range(subs)]

    both = range(subs)

    up_here = factor_up.reshape(own_rows, columns)
    up_line = [up_here] + [
        lax.ppermute(up_here, "fsdp", [(i, (i + far) % n) for i in range(n)]) for far in range(1, n)
    ]
    factor_here = factor_down.reshape(own_rows, features)
    fd_up, fd_down = [factor_here], [factor_here]
    copies = groups * subs
    part_rows, width = base_weight.shape[0] // copies, base_weight.shape[1]
    weight_here = lax.dynamic_index_in_dim(
        base_weight.reshape(copies, part_rows, width), y * subs + sub, 0, keepdims=False
    )
    w_up, w_down = [weight_here], [weight_here]

    def line_on(ups, downs, step, *earlier):
        if step < n:
            source = [after(one, *earlier) for one in (ups[-1], downs[-1])]
            one, two = line_step(*source, step)
            ups.append(one)
            downs.append(two)

    line_on(fd_up, fd_down, 1)
    x_cores = over_cores(activations)
    g_cores = over_cores(output_gradient)
    count_cores = over_cores(counts[0])
    if lax.axis_size("tp") == 2:
        other = lax.ppermute(output_gradient, "tp", around("tp"))
        first = lax.axis_index("tp") == 0
        grad_full = jnp.concatenate(
            [jnp.where(first, output_gradient, other), jnp.where(first, other, output_gradient)], axis=1
        )
    else:
        grad_full = lax.all_gather(output_gradient, "tp", axis=1, tiled=True)

    hot = owners[:, None] == lax.broadcasted_iota(jnp.int32, (slots, slots), 1)
    bounds = []
    for count in count_cores:
        seg_ends = jnp.cumsum(count)
        starts = jnp.sum(jnp.where(hot, (seg_ends - count)[:, None], 0), axis=0)
        ends = jnp.sum(jnp.where(hot, seg_ends[:, None], 0), axis=0)
        bounds.append((starts, ends))

    def ranges(devices, cores):
        which = jnp.concatenate(
            [(at * subs + core) * own_slots + jnp.arange(own_slots, dtype=jnp.int32) for at, core in devices]
        )
        which = jnp.repeat(which, rank)
        found = which[:, None] == jnp.arange(slots, dtype=jnp.int32)[None, :]
        return tuple(
            jnp.stack([jnp.sum(jnp.where(found, bounds[b][end][None, :], 0), axis=1) for b in cores])
            for end in range(2)
        )

    along_line = ranges([((z - j) % n, sub) for j in range(n)], both)
    round_0 = [*up_line[1:], fd_up[1], fd_down[1], grad_full, *x_cores[1:], *g_cores[1:]]

    line_on(fd_up, fd_down, 2, *round_0)
    line_on(w_up, w_down, 1, *round_0)
    low_back = low_rank([after(g_cores[0], *round_0), *g_cores[1:]], up_line, *along_line, rank)
    low_back = sum_over_tp(adapter_scale_factor * low_back)
    down_blocks = outer(low_back, *along_line, x_cores, 1.0, n)
    whose, factors = [z], [over_cores(after(factor_here, *round_0))]

    def factor_arrives(step):
        mine, owner = arrival(fd_up, fd_down, step)
        whose.append(owner)
        factors.append(over_cores(mine))

    factor_arrives(1)
    round_1 = [fd_up[-1], fd_down[-1], w_up[-1], w_down[-1], *down_blocks, *factors[0], *factors[1]]

    from_above = from_below = None

    def sum_on(step, *earlier):
        lower, upper = down_blocks[n - step], down_blocks[step]
        if step > 1:
            lower, upper = lower + from_above.astype(F32), upper + from_below.astype(F32)
        lower, upper = (after(one.astype(BF16), *earlier) for one in (lower, upper))
        return (
            lax.ppermute(lower, "fsdp", [(i, i - 1) for i in range(n - step, n)]),
            lax.ppermute(upper, "fsdp", [(i, i + 1) for i in range(step)]),
        )

    weight_arrivals = []

    def weight_arrives(step, *earlier):
        mine = [after(arrival(w_up, w_down, step)[0], *earlier)]
        for _ in range(1, groups):
            mine.append(lax.ppermute(mine[-1], "groups", around("groups")))
        weight_arrivals.append(mine)

    for step in range(3, n):
        line_on(fd_up, fd_down, step, *round_1)
    line_on(w_up, w_down, 2, *round_1)
    from_above, from_below = sum_on(1, *round_1)
    weight_arrives(1, *round_1)
    for step in range(2, n - 1):
        factor_arrives(step)
    early = len(factors)
    if early * own_rows % LANES:
        early = 0
    low_in = None
    if early:
        low_in = low_rank(
            [after(x_cores[0], *round_1), *x_cores[1:]],
            [pair[0] for pair in factors[:early]],
            *ranges([(at, sub) for at in whose[:early]], both),
            rank,
        )
    round_2 = [fd_up[-1], fd_down[-1], w_up[-1], w_down[-1], from_above, from_below]
    round_2 += weight_arrivals[0][1:] + factors[-1] + ([] if low_in is None else [low_in])

    for step in range(3, n):
        line_on(w_up, w_down, step, *round_2)
    for step in range(2, n - 1):
        from_above, from_below = sum_on(step, *round_2)
        weight_arrives(step, *round_2)
    for step in range(max(2, n - 1), n):
        factor_arrives(step)
    low_in = low_rank(
        [after(x_cores[0], *round_2), *x_cores[1:]],
        [pair[0] for pair in factors[early:]],
        *ranges([(at, sub) for at in whose[early:]], both),
        rank,
        low_in,
    )
    low_in = sum_over_tp(low_in)
    up_pieces = outer(low_in, *along_line, g_cores, adapter_scale_factor, n)
    low_mine = low_back[:tokens]
    for b in range(1, subs):
        theirs = low_back[b * tokens : (b + 1) * tokens].astype(BF16)
        low_mine = low_mine + lax.ppermute(
            theirs, "sub", [(i, (i - b) % subs) for i in range(subs)]
        ).astype(F32)
    wide = spread_out(low_mine, *ranges([(at, (sub - b) % subs) for at in whose for b in both], [0]))
    round_3 = [w_up[-1], w_down[-1], from_above, from_below, *up_pieces, wide, *factors[-1]]
    round_3 += weight_arrivals[-1][1:]

    if n > 2:
        from_above, from_below = sum_on(n - 1, *round_3)
        weight_arrives(n - 1, *round_3)
    grad_down = down_blocks[0] + from_above.astype(F32) + from_below.astype(F32)
    up_total = up_pieces[0]
    for far in range(1, n):
        got = lax.ppermute(
            after(up_pieces[far].astype(BF16), *round_3), "fsdp", [(i, (i - far) % n) for i in range(n)]
        )
        up_total = up_total + got.astype(F32)
    weight_parts = [[[base_weight] for _ in range(groups)] for _ in both]
    for arrived in weight_arrivals:
        for a, one in enumerate(arrived):
            for b, held in enumerate(over_cores(one)):
                weight_parts[b][a].append(held)
    all_factors = [one for pair in factors for one in pair]
    input_gradient = None
    for a in range(groups):
        for b in both:
            part = ((y - a) % groups) * subs + (sub - b) % subs
            scalars = jnp.stack(whose + [part]).astype(jnp.int32)
            input_gradient = input_gradient_part(
                scalars, copies, grad_full, weight_parts[b][a], wide, all_factors, input_gradient
            )
    return (
        input_gradient,
        grad_down.reshape(own_slots, rank, features),
        up_total.reshape(own_slots, rank, columns),
    )


def solution(mesh):
    placed = (
        P(("groups", "fsdp", "sub"), "tp"),
        P(("groups", "fsdp", "sub"), "tp"),
        P("tp", "fsdp"),
        P(("groups", "fsdp", "sub"), None, "tp"),
        P(("groups", "fsdp", "sub"), None, "tp"),
        P(("groups", "fsdp", "sub"), None),
        P("groups"),
    )
    return jax.shard_map(
        local,
        mesh=mesh,
        in_specs=placed,
        out_specs=(
            P(("groups", "fsdp", "sub"), "tp"),
            P(("groups", "fsdp", "sub"), None, "tp"),
            P(("groups", "fsdp", "sub"), None, "tp"),
        ),
        check_vma=False,
    )
```

time: 400 us -> 287 us (0.72)
  waiting for transfers between devices: 309 us -> 101 us
  starting transfers between devices: 0.43 us -> 63.4 us
  Pallas kernels: 0 us -> 56.6 us
  matrix products: 51.4 us -> 0 us
  other arithmetic: 5.94 us -> 34.4 us
  local copies, waits for them, and re-layouts: 8.99 us -> 29 us
  between operations: 15.3 us -> 1.35 us
  blocking collectives: 8.33 us -> 0 us
    all_gather x4 -> x0, waiting for transfers between devices: 299 us -> none  [the longest x1 191 us: local(): lax.all_gather(own_rows, ('fsdp', 'groups', 'sub'), axis=0, tiled=True)]
    ppermute x0 -> x44, waiting for transfers between devices: none -> 101 us  [the longest x6 51.6 us: line_step(): lax.ppermute(down, 'fsdp', [(i, i - 1) for i in range(1, count - step + 1)])]
    ppermute x0 -> x44, starting transfers between devices: none -> 63.4 us  [the longest x6 15.7 us: line_step(): lax.ppermute(up, 'fsdp', [(i, i + 1) for i in range(step - 1, count - 1)])]
    pallas_call x0 -> x10, Pallas kernels: none -> 56.6 us  [the longest x4 26.4 us: input_gradient_part(): pl.pallas_call(functools.partial(input_gradient_kernel, shards, len(facto...]
    dot_general x7 -> x0, matrix products: 51.4 us -> none  [the longest x1 15.6 us: local(): jnp.einsum('tfc,fdc->td', grad_full.reshape(tok_rows, shards, width), wei...]
    unnamed x5 -> x102, local copies, waits for them, and re-layouts: 5.97 us -> 22.7 us
    select_n x0 -> x7, other arithmetic: none -> 11 us  [the longest x6 9.59 us: arrival(): pick = jnp.where(here, one, pick)]
    add x0 -> x14, other arithmetic: none -> 9.67 us  [the longest x1 3.27 us: local(): grad_down = down_blocks[0] + from_above.astype(F32) + from_below.astype(F32)]
  transfers between devices with their start and end apart: 6 -> 44, of which waited for: 4 -> 15; matrix products, arithmetic and copies ran while one was open for 12% -> 14% of each run, Pallas kernels for 0% -> 18%
where the time goes in v3:
time: 287 us; the launch traced here: 286 us
  waiting for transfers between devices  101 us (35%)
  starting transfers between devices  63.4 us (22%)
  Pallas kernels  56.6 us (20%)
  other arithmetic  34.4 us (12%)
  local copies, waits for them, and re-layouts  29 us (10%)
    ppermute x6, waiting for transfers between devices, line_step(): lax.ppermute(down, 'fsdp', [(i, i - 1) for i in range(1, count - step + 1)])  51.6 us
    pallas_call x4, Pallas kernels, input_gradient_part(): pl.pallas_call(functools.partial(input_gradient_kernel, shards, len(facto...  26.4 us
    unnamed x102, local copies, waits for them, and re-layouts  22.7 us
    pallas_call x3, Pallas kernels, low_rank(): pl.pallas_call(functools.partial(low_kernel, len(xs), len(blocks), rank,...  18.8 us
    ppermute x6, waiting for transfers between devices, line_step(): lax.ppermute(up, 'fsdp', [(i, i + 1) for i in range(step - 1, count - 1)])  16.4 us
    ppermute x3, waiting for transfers between devices, local(): lax.ppermute(up_here, 'fsdp', [(i, (i + far) % n) for i in range(n)])  16.1 us
    ppermute x6, starting transfers between devices, line_step(): lax.ppermute(up, 'fsdp', [(i, i + 1) for i in range(step - 1, count - 1)])  15.7 us
    ppermute x3, starting transfers between devices, sum_on(): lax.ppermute(upper, 'fsdp', [(i, i + 1) for i in range(step)])  13.3 us
  transfers between devices with their start and end apart: 44, of which 15 were waited for; matrix products, arithmetic and copies ran while one was open for 14% of the time, Pallas kernels for 18%

profile of v3, /device:TPU:0, one launch (start us, length us, event | category | flops | bytes accessed | tf_op | source)
XLA Modules:
  0.0 285.5 jit_solution(1979760595085511115)
XLA Ops:
  1.2 4.7 %collective-permute-start.4 = (bf16[128,4096]{1,0:T(8,128)(2,1)}, bf16[128,4096]{1,0:T(8,128)(2,1)S(1)}, u32[]{:S(2)}, u32[]{:S(2)}) collective-permute-start(bf16[128,4096]{1,0:T(8,128)(2,1)} %bitcast.30), channel_id=1, source_target_pairs={{0,4},{4,8},{8,12},{1,5},{5,9},{9,13},{2,6},{6,10},{10,14},{3,7},{... | collective-permute-start | bytes 3145736 | tf_op jit(solution)/shard_map/ppermute | solution.py:31
  14.6 15.0 %collective-permute-done.4 = bf16[128,4096]{1,0:T(8,128)(2,1)S(1)} collective-permute-done((bf16[128,4096]{1,0:T(8,128)(2,1)}, bf16[128,4096]{1,0:T(8,128)(2,1)S(1)}, u32[]{:S(2)}, u32[]{:S(2)}) %collective-permute-start.4) | collective-permute-done | bytes 1048608 | tf_op jit(solution)/shard_map/ppermute | solution.py:31
  29.6 3.4 %collective-permute-start.2 = (bf16[128,1024]{1,0:T(8,128)(2,1)}, bf16[128,1024]{1,0:T(8,128)(2,1)S(1)}, u32[]{:S(2)}, u32[]{:S(2)}) collective-permute-start(bf16[128,1024]{1,0:T(8,128)(2,1)} %bitcast.39), channel_id=1, source_target_pairs={{0,8},{4,12},{8,0},{12,4},{1,9},{5,13},{9,1},{13,5},{2,10},{6,14},... | collective-permute-start | bytes 786440 | tf_op jit(solution)/shard_map/ppermute | solution.py:258
  37.4 4.2 %collective-permute-done.1.refs_3_ = bf16[128,1024]{1,0:T(8,128)(2,1)S(1)} collective-permute-done((bf16[128,1024]{1,0:T(8,128)(2,1)}, bf16[128,1024]{1,0:T(8,128)(2,1)S(1)}, u32[]{:S(2)}, u32[]{:S(2)}) %collective-permute-start.1) | collective-permute-done | bytes 262176 | tf_op jit(solution)/shard_map/ppermute | solution.py:258
  41.8 10.0 %collective-permute-done.2.refs_4_ = bf16[128,1024]{1,0:T(8,128)(2,1)S(1)} collective-permute-done((bf16[128,1024]{1,0:T(8,128)(2,1)}, bf16[128,1024]{1,0:T(8,128)(2,1)S(1)}, u32[]{:S(2)}, u32[]{:S(2)}) %collective-permute-start.2) | collective-permute-done | bytes 262176 | tf_op jit(solution)/shard_map/ppermute | solution.py:258
  60.0 6.3 %collective-permute-start.8 = (bf16[1024,512]{1,0:T(8,128)(2,1)S(1)}, bf16[1024,512]{1,0:T(8,128)(2,1)}, u32[]{:S(2)}, u32[]{:S(2)}) collective-permute-start(bf16[1024,512]{1,0:T(8,128)(2,1)S(1)} %dynamic-slice_bitcast_fusion), channel_id=1, source_target_pairs={{0,4},{4,8},{8,12},{1,5},{5,9},{9,13},{2,6},{6,10},{10,14},{3,7},{... | collective-permute-start | bytes 3145736 | tf_op jit(solution)/shard_map/ppermute | solution.py:31
  71.9 9.0 %shard_map.95 = (f32[128,4096]{1,0:T(8,128)S(1)}, f32[128,4096]{1,0:T(8,128)S(1)}, f32[128,4096]{1,0:T(8,128)S(1)}, f32[128,4096]{1,0:T(8,128)S(1)}) custom-call(f32[1024,128]{1,0:T(8,128)S(1)} %convert_add_fusion.3.low, s32[2,512]{1,0:T(2,128)S(1)} %pad_add_fusion.refs_6_.start, s32[2,512]{1,0:T(2,128)S(1)} %pad_add_fusion.1.refs_7_.end, ...), custom_call_target="tpu_custom_call" | custom-call | flops 1 | bytes 1 | tf_op jit(solution)/shard_map/pallas_call | solution.py:184
  86.8 7.5 %collective-permute-done.9 = bf16[1024,512]{1,0:T(8,128)(2,1)} collective-permute-done((bf16[1024,512]{1,0:T(8,128)(2,1)S(1)}, bf16[1024,512]{1,0:T(8,128)(2,1)}, u32[]{:S(2)}, u32[]{:S(2)}) %collective-permute-start.9) | collective-permute-done | bytes 1048608 | tf_op jit(solution)/shard_map/ppermute | solution.py:32
  94.3 20.0 %collective-permute-done.11 = bf16[128,4096]{1,0:T(8,128)(2,1)S(1)} collective-permute-done((bf16[128,4096]{1,0:T(8,128)(2,1)}, bf16[128,4096]{1,0:T(8,128)(2,1)S(1)}, u32[]{:S(2)}, u32[]{:S(2)}) %collective-permute-start.11) | collective-permute-done | bytes 1048608 | tf_op jit(solution)/shard_map/ppermute | solution.py:32
  116.3 4.7 %collective-permute-start.23 = (bf16[128,4096]{1,0:T(8,128)(2,1)S(1)}, bf16[128,4096]{1,0:T(8,128)(2,1)S(1)}, u32[]{:S(2)}, u32[]{:S(2)}) collective-permute-start(bf16[128,4096]{1,0:T(8,128)(2,1)S(1)} %convert_element_type.73), channel_id=1, source_target_pairs={{0,4},{1,5},{2,6},{3,7},{16,20},{17,21},{18,22},{19,23}} | collective-permute-start | bytes 3145736 | tf_op jit(solution)/shard_map/ppermute | solution.py:335
  127.4 14.9 %collective-permute-done.21 = bf16[128,4096]{1,0:T(8,128)(2,1)S(1)} collective-permute-done((bf16[128,4096]{1,0:T(8,128)(2,1)S(1)}, bf16[128,4096]{1,0:T(8,128)(2,1)S(1)}, u32[]{:S(2)}, u32[]{:S(2)}) %collective-permute-start.21) | collective-permute-done | bytes 1048608 | tf_op jit(solution)/shard_map/ppermute | solution.py:32
  151.7 8.9 %shard_map.96.refs_5_ = f32[1024,128]{1,0:T(8,128)S(1)} custom-call(bf16[512,4096]{1,0:T(8,128)(2,1)S(1)} %copy-done.2, bf16[512,4096]{1,0:T(8,128)(2,1)} %collective-permute-done.6.refs_1_, bf16[128,4096]{1,0:T(8,128)(2,1)S(1)} %bitcast.33, bf16[128,4096]{1,0:T(8,128)(2,1)S(1)} %broadcast_select_fusion.1.refs_3_.refs_11_, ...), custom_call_target="tpu_custom_call" | custom-call | flops 1 | bytes 1 | tf_op jit(solution)/shard_map/pallas_call | solution.py:123
  163.2 8.1 %shard_map.97 = f32[1024,128]{1,0:T(8,128)S(1)} custom-call(bf16[512,4096]{1,0:T(8,128)(2,1)S(1)} %copy-done.2, bf16[512,4096]{1,0:T(8,128)(2,1)} %collective-permute-done.6.refs_1_, bf16[128,4096]{1,0:T(8,128)(2,1)S(1)} %select_select_fusion.refs_2_.refs_15_, s32[2,128]{1,0:T(2,128)S(1)} %get-tuple-element.97.refs_3_, ...), custom_call_target="tpu_custom_call" | custom-call | flops 1 | bytes 1 | tf_op jit(solution)/shard_map/pallas_call | solution.py:123
  172.0 3.0 %add_convert_fusion.2 = (bf16[128,4096]{1,0:T(8,128)(2,1)}, bf16[128,4096]{1,0:T(8,128)(2,1)}) fusion(f32[128,4096]{1,0:T(8,128)S(1)} %copy-done.34, bf16[128,4096]{1,0:T(8,128)(2,1)S(1)} %copy-done.45, bf16[128,4096]{1,0:T(8,128)(2,1)} %collective-permute-done.22), kind=kLoop, calls=%fused_computation.4 | loop fusion | flops 3145728 | bytes 6291456 | tf_op jit(solution)/shard_map/convert_element_type | solution.py:332
  175.0 3.0 %collective-permute-start.30 = (bf16[128,4096]{1,0:T(8,128)(2,1)}, bf16[128,4096]{1,0:T(8,128)(2,1)}, u32[]{:S(2)}, u32[]{:S(2)}) collective-permute-start(bf16[128,4096]{1,0:T(8,128)(2,1)} %get-tuple-element.57), channel_id=1, source_target_pairs={{0,4},{4,8},{1,5},{5,9},{2,6},{6,10},{3,7},{7,11},{16,20},{20,24},... | collective-permute-start | bytes 3145736 | tf_op jit(solution)/shard_map/ppermute | solution.py:335
  200.5 8.6 %collective-permute-done.28 = bf16[1024,512]{1,0:T(8,128)(2,1)} collective-permute-done((bf16[1024,512]{1,0:T(8,128)(2,1)}, bf16[1024,512]{1,0:T(8,128)(2,1)}, u32[]{:S(2)}, u32[]{:S(2)}) %collective-permute-start.28) | collective-permute-done | bytes 1048608 | tf_op jit(solution)/shard_map/ppermute | solution.py:32
  211.1 4.8 %collective-permute-start.42 = (bf16[128,1024]{1,0:T(8,128)(2,1)S(1)}, bf16[128,1024]{1,0:T(8,128)(2,1)}, u32[]{:S(2)}, u32[]{:S(2)}) collective-permute-start(bf16[128,1024]{1,0:T(8,128)(2,1)S(1)} %convert_element_type.89), channel_id=1, source_target_pairs={{0,8},{4,12},{8,0},{12,4},{1,9},{5,13},{9,1},{13,5},{2,10},{6,14},... | collective-permute-start | bytes 786440 | tf_op jit(solution)/shard_map/ppermute | solution.py:399
  225.7 11.8 %collective-permute-done.42 = bf16[128,1024]{1,0:T(8,128)(2,1)} collective-permute-done((bf16[128,1024]{1,0:T(8,128)(2,1)S(1)}, bf16[128,1024]{1,0:T(8,128)(2,1)}, u32[]{:S(2)}, u32[]{:S(2)}) %collective-permute-start.42) | collective-permute-done | bytes 262176 | tf_op jit(solution)/shard_map/ppermute | solution.py:399
  238.9 5.6 %collective-permute-start.40 = (bf16[128,4096]{1,0:T(8,128)(2,1)}, bf16[128,4096]{1,0:T(8,128)(2,1)}, u32[]{:S(2)}, u32[]{:S(2)}) collective-permute-start(bf16[128,4096]{1,0:T(8,128)(2,1)} %add_convert_fusion), channel_id=1, source_target_pairs={{0,4},{4,8},{8,12},{1,5},{5,9},{9,13},{2,6},{6,10},{10,14},{3,7},{... | collective-permute-start | bytes 3145736 | tf_op jit(solution)/shard_map/ppermute | solution.py:335
  253.1 7.0 %shard_map.100.refs_17_ = bf16[512,4096]{1,0:T(8,128)(2,1)} custom-call(s32[5]{0:T(128)S(1)} %stack.139._, bf16[512,2048]{1,0:T(8,128)(2,1)S(1)} %pad_maximum_fusion.refs_0_.refs_1_.refs_2_.refs_3_, bf16[512,2048]{1,0:T(8,128)(2,1)S(1)} %pad_maximum_fusion.refs_0_.refs_1_.refs_2_.refs_3_, ...), custom_call_target="tpu_custom_call" | custom-call | flops 1 | bytes 1 | tf_op jit(solution)/shard_map/pallas_call | solution.py:229
  262.7 6.5 %shard_map.101.refs_17_ = bf16[512,4096]{1,0:T(8,128)(2,1)} custom-call(s32[5]{0:T(128)S(1)} %stack.137._, bf16[512,2048]{1,0:T(8,128)(2,1)S(1)} %pad_maximum_fusion.refs_0_.refs_1_.refs_2_.refs_3_, bf16[512,2048]{1,0:T(8,128)(2,1)S(1)} %pad_maximum_fusion.refs_0_.refs_1_.refs_2_.refs_3_, ...), custom_call_target="tpu_custom_call", output_to_operand_aliasing={{}: (18, {})} | custom-call | flops 1 | bytes 1 | tf_op jit(solution)/shard_map/pallas_call | solution.py:229
  269.3 6.7 %shard_map.102.refs_17_ = bf16[512,4096]{1,0:T(8,128)(2,1)} custom-call(s32[5]{0:T(128)S(1)} %stack.135._, bf16[512,2048]{1,0:T(8,128)(2,1)S(1)} %pad_maximum_fusion.refs_0_.refs_1_.refs_2_.refs_3_, bf16[512,2048]{1,0:T(8,128)(2,1)S(1)} %pad_maximum_fusion.refs_0_.refs_1_.refs_2_.refs_3_, ...), custom_call_target="tpu_custom_call", output_to_operand_aliasing={{}: (18, {})} | custom-call | flops 1 | bytes 1 | tf_op jit(solution)/shard_map/pallas_call | solution.py:229
  276.0 3.3 %convert_add_fusion = f32[128,4096]{1,0:T(8,128)} fusion(bf16[128,4096]{1,0:T(8,128)(2,1)} %collective-permute-done.40, f32[128,4096]{1,0:T(8,128)S(1)} %copy-done.32, bf16[128,4096]{1,0:T(8,128)(2,1)} %collective-permute-done.39), kind=kLoop, calls=%fused_computation.1 | loop fusion | flops 2097152 | bytes 6291456 | tf_op jit(solution)/shard_map/add | solution.py:396
  279.3 6.3 %shard_map.103 = bf16[512,4096]{1,0:T(8,128)(2,1)} custom-call(s32[5]{0:T(128)S(1)} %stack.113._, bf16[512,2048]{1,0:T(8,128)(2,1)S(1)} %pad_maximum_fusion.refs_0_.refs_1_.refs_2_.refs_3_, bf16[512,2048]{1,0:T(8,128)(2,1)S(1)} %pad_maximum_fusion.refs_0_.refs_1_.refs_2_.refs_3_, ...), custom_call_target="tpu_custom_call", output_to_operand_aliasing={{}: (18, {})} | custom-call | flops 1 | bytes 1 | tf_op jit(solution)/shard_map/pallas_call | solution.py:229
  (247 shorter events, 101.1 us)
Async XLA Ops:
  0.6 53.1 %collective-permute-start.6 = (bf16[512,4096]{1,0:T(8,128)(2,1)}, bf16[512,4096]{1,0:T(8,128)(2,1)}, u32[]{:S(2)}, u32[]{:S(2)}) collective-permute-start(bf16[512,4096]{1,0:T(8,128)(2,1)} %refs_0_.5), channel_id=1, source_target_pairs={{0,1},{1,0},{2,3},{3,2},{4,5},{5,4},{6,7},{7,6},{8,9},{9,8},{10,11... | collective-permute-start | bytes 12582920 | tf_op jit(solution)/shard_map/ppermute | solution.py:68
  1.2 28.4 %collective-permute-start.4 = (bf16[128,4096]{1,0:T(8,128)(2,1)}, bf16[128,4096]{1,0:T(8,128)(2,1)S(1)}, u32[]{:S(2)}, u32[]{:S(2)}) collective-permute-start(bf16[128,4096]{1,0:T(8,128)(2,1)} %bitcast.30), channel_id=1, source_target_pairs={{0,4},{4,8},{8,12},{1,5},{5,9},{9,13},{2,6},{6,10},{10,14},{3,7},{... | collective-permute-start | bytes 3145736 | tf_op jit(solution)/shard_map/ppermute | solution.py:31
  5.9 27.2 %collective-permute-start.5 = (bf16[128,4096]{1,0:T(8,128)(2,1)}, bf16[128,4096]{1,0:T(8,128)(2,1)S(1)}, u32[]{:S(2)}, u32[]{:S(2)}) collective-permute-start(bf16[128,4096]{1,0:T(8,128)(2,1)} %bitcast.31), channel_id=1, source_target_pairs={{4,0},{8,4},{12,8},{5,1},{9,5},{13,9},{6,2},{10,6},{14,10},{7,3},{... | collective-permute-start | bytes 3145736 | tf_op jit(solution)/shard_map/ppermute | solution.py:32
  7.3 28.2 %collective-permute-start = (bf16[512,1024]{1,0:T(8,128)(2,1)}, bf16[512,1024]{1,0:T(8,128)(2,1)}, u32[]{:S(2)}, u32[]{:S(2)}) collective-permute-start(bf16[512,1024]{1,0:T(8,128)(2,1)} %refs_0_.6), channel_id=1, source_target_pairs={{0,2},{2,0},{1,3},{3,1},{4,6},{6,4},{5,7},{7,5},{8,10},{10,8},{9,1... | collective-permute-start | bytes 3145736 | tf_op jit(solution)/shard_map/ppermute | solution.py:281
  10.7 31.0 %collective-permute-start.1 = (bf16[128,1024]{1,0:T(8,128)(2,1)}, bf16[128,1024]{1,0:T(8,128)(2,1)S(1)}, u32[]{:S(2)}, u32[]{:S(2)}) collective-permute-start(bf16[128,1024]{1,0:T(8,128)(2,1)} %bitcast.38), channel_id=1, source_target_pairs={{0,4},{4,8},{8,12},{12,0},{1,5},{5,9},{9,13},{13,1},{2,6},{6,10},{... | collective-permute-start | bytes 786440 | tf_op jit(solution)/shard_map/ppermute | solution.py:258
  35.5 32.1 %collective-permute-start.15 = (bf16[128,4096]{1,0:T(8,128)(2,1)S(1)}, bf16[128,4096]{1,0:T(8,128)(2,1)}, u32[]{:S(2)}, u32[]{:S(2)}) collective-permute-start(bf16[128,4096]{1,0:T(8,128)(2,1)S(1)} %broadcast_select_fusion.1.refs_3_.refs_11_), channel_id=1, source_target_pairs={{0,1},{1,0},{2,3},{3,2},{4,5},{5,4},{6,7},{7,6},{8,9},{9,8},{10,11... | collective-permute-start | bytes 3145736 | tf_op jit(solution)/shard_map/ppermute | solution.py:68
  60.0 26.8 %collective-permute-start.8 = (bf16[1024,512]{1,0:T(8,128)(2,1)S(1)}, bf16[1024,512]{1,0:T(8,128)(2,1)}, u32[]{:S(2)}, u32[]{:S(2)}) collective-permute-start(bf16[1024,512]{1,0:T(8,128)(2,1)S(1)} %dynamic-slice_bitcast_fusion), channel_id=1, source_target_pairs={{0,4},{4,8},{8,12},{1,5},{5,9},{9,13},{2,6},{6,10},{10,14},{3,7},{... | collective-permute-start | bytes 3145736 | tf_op jit(solution)/shard_map/ppermute | solution.py:31
  66.2 28.1 %collective-permute-start.9 = (bf16[1024,512]{1,0:T(8,128)(2,1)S(1)}, bf16[1024,512]{1,0:T(8,128)(2,1)}, u32[]{:S(2)}, u32[]{:S(2)}) collective-permute-start(bf16[1024,512]{1,0:T(8,128)(2,1)S(1)} %dynamic-slice_bitcast_fusion), channel_id=1, source_target_pairs={{4,0},{8,4},{12,8},{5,1},{9,5},{13,9},{6,2},{10,6},{14,10},{7,3},{... | collective-permute-start | bytes 3145736 | tf_op jit(solution)/shard_map/ppermute | solution.py:32
  67.5 26.8 %collective-permute-start.14 = (bf16[128,4096]{1,0:T(8,128)(2,1)S(1)}, bf16[128,4096]{1,0:T(8,128)(2,1)S(1)}, u32[]{:S(2)}, u32[]{:S(2)}) collective-permute-start(bf16[128,4096]{1,0:T(8,128)(2,1)S(1)} %bitcast.32), channel_id=1, source_target_pairs={{0,1},{1,0},{2,3},{3,2},{4,5},{5,4},{6,7},{7,6},{8,9},{9,8},{10,11... | collective-permute-start | bytes 3145736 | tf_op jit(solution)/shard_map/ppermute | solution.py:68
  67.6 26.7 %collective-permute-start.10 = (bf16[128,4096]{1,0:T(8,128)(2,1)}, bf16[128,4096]{1,0:T(8,128)(2,1)S(1)}, u32[]{:S(2)}, u32[]{:S(2)}) collective-permute-start(bf16[128,4096]{1,0:T(8,128)(2,1)} %copy-done.40), channel_id=1, source_target_pairs={{4,8},{8,12},{5,9},{9,13},{6,10},{10,14},{7,11},{11,15},{20,24},{2... | collective-permute-start | bytes 3145736 | tf_op jit(solution)/shard_map/ppermute | solution.py:31
  68.4 45.9 %collective-permute-start.11 = (bf16[128,4096]{1,0:T(8,128)(2,1)}, bf16[128,4096]{1,0:T(8,128)(2,1)S(1)}, u32[]{:S(2)}, u32[]{:S(2)}) collective-permute-start(bf16[128,4096]{1,0:T(8,128)(2,1)} %copy-done.42), channel_id=1, source_target_pairs={{4,0},{8,4},{5,1},{9,5},{6,2},{10,6},{7,3},{11,7},{20,16},{24,20},... | collective-permute-start | bytes 3145736 | tf_op jit(solution)/shard_map/ppermute | solution.py:32
  114.3 28.0 %collective-permute-start.21 = (bf16[128,4096]{1,0:T(8,128)(2,1)S(1)}, bf16[128,4096]{1,0:T(8,128)(2,1)S(1)}, u32[]{:S(2)}, u32[]{:S(2)}) collective-permute-start(bf16[128,4096]{1,0:T(8,128)(2,1)S(1)} %collective-permute-done.11), channel_id=1, source_target_pairs={{4,0},{5,1},{6,2},{7,3},{20,16},{21,17},{22,18},{23,19}} | collective-permute-start | bytes 3145736 | tf_op jit(solution)/shard_map/ppermute | solution.py:32
  115.6 28.3 %collective-permute-start.20 = (bf16[128,4096]{1,0:T(8,128)(2,1)S(1)}, bf16[128,4096]{1,0:T(8,128)(2,1)S(1)}, u32[]{:S(2)}, u32[]{:S(2)}) collective-permute-start(bf16[128,4096]{1,0:T(8,128)(2,1)S(1)} %collective-permute-done.10), channel_id=1, source_target_pairs={{8,12},{9,13},{10,14},{11,15},{24,28},{25,29},{26,30},{27,31}} | collective-permute-start | bytes 3145736 | tf_op jit(solution)/shard_map/ppermute | solution.py:31
  116.3 29.1 %collective-permute-start.23 = (bf16[128,4096]{1,0:T(8,128)(2,1)S(1)}, bf16[128,4096]{1,0:T(8,128)(2,1)S(1)}, u32[]{:S(2)}, u32[]{:S(2)}) collective-permute-start(bf16[128,4096]{1,0:T(8,128)(2,1)S(1)} %convert_element_type.73), channel_id=1, source_target_pairs={{0,4},{1,5},{2,6},{3,7},{16,20},{17,21},{18,22},{19,23}} | collective-permute-start | bytes 3145736 | tf_op jit(solution)/shard_map/ppermute | solution.py:335
  121.0 39.5 %collective-permute-start.22 = (bf16[128,4096]{1,0:T(8,128)(2,1)}, bf16[128,4096]{1,0:T(8,128)(2,1)}, u32[]{:S(2)}, u32[]{:S(2)}) collective-permute-start(bf16[128,4096]{1,0:T(8,128)(2,1)} %convert_element_type.72), channel_id=1, source_target_pairs={{12,8},{13,9},{14,10},{15,11},{28,24},{29,25},{30,26},{31,27}} | collective-permute-start | bytes 3145736 | tf_op jit(solution)/shard_map/ppermute | solution.py:334
  122.7 38.9 %collective-permute-start.19 = (bf16[1024,512]{1,0:T(8,128)(2,1)}, bf16[1024,512]{1,0:T(8,128)(2,1)}, u32[]{:S(2)}, u32[]{:S(2)}) collective-permute-start(bf16[1024,512]{1,0:T(8,128)(2,1)} %collective-permute-done.9), channel_id=1, source_target_pairs={{4,0},{8,4},{5,1},{9,5},{6,2},{10,6},{7,3},{11,7},{20,16},{24,20},... | collective-permute-start | bytes 3145736 | tf_op jit(solution)/shard_map/ppermute | solution.py:32
  182.1 27.0 %collective-permute-start.28 = (bf16[1024,512]{1,0:T(8,128)(2,1)}, bf16[1024,512]{1,0:T(8,128)(2,1)}, u32[]{:S(2)}, u32[]{:S(2)}) collective-permute-start(bf16[1024,512]{1,0:T(8,128)(2,1)} %collective-permute-done.19), channel_id=1, source_target_pairs={{4,0},{5,1},{6,2},{7,3},{20,16},{21,17},{22,18},{23,19}} | collective-permute-start | bytes 3145736 | tf_op jit(solution)/shard_map/ppermute | solution.py:32
  183.4 25.7 %collective-permute-start.27 = (bf16[1024,512]{1,0:T(8,128)(2,1)}, bf16[1024,512]{1,0:T(8,128)(2,1)}, u32[]{:S(2)}, u32[]{:S(2)}) collective-permute-start(bf16[1024,512]{1,0:T(8,128)(2,1)} %collective-permute-done.18), channel_id=1, source_target_pairs={{8,12},{9,13},{10,14},{11,15},{24,28},{25,29},{26,30},{27,31}} | collective-permute-start | bytes 3145736 | tf_op jit(solution)/shard_map/ppermute | solution.py:31
  200.0 62.2 %collective-permute-start.37 = (bf16[1024,512]{1,0:T(8,128)(2,1)}, bf16[1024,512]{1,0:T(8,128)(2,1)}, u32[]{:S(2)}, u32[]{:S(2)}) collective-permute-start(bf16[1024,512]{1,0:T(8,128)(2,1)} %broadcast_select_fusion.2.refs_6_), channel_id=1, source_target_pairs={{0,1},{1,0},{2,3},{3,2},{4,5},{5,4},{6,7},{7,6},{8,9},{9,8},{10,11... | collective-permute-start | bytes 3145736 | tf_op jit(solution)/shard_map/ppermute | solution.py:68
  211.1 26.4 %collective-permute-start.42 = (bf16[128,1024]{1,0:T(8,128)(2,1)S(1)}, bf16[128,1024]{1,0:T(8,128)(2,1)}, u32[]{:S(2)}, u32[]{:S(2)}) collective-permute-start(bf16[128,1024]{1,0:T(8,128)(2,1)S(1)} %convert_element_type.89), channel_id=1, source_target_pairs={{0,8},{4,12},{8,0},{12,4},{1,9},{5,13},{9,1},{13,5},{2,10},{6,14},... | collective-permute-start | bytes 786440 | tf_op jit(solution)/shard_map/ppermute | solution.py:399
  224.2 37.9 %collective-permute-start.38 = (bf16[1024,512]{1,0:T(8,128)(2,1)}, bf16[1024,512]{1,0:T(8,128)(2,1)}, u32[]{:S(2)}, u32[]{:S(2)}) collective-permute-start(bf16[1024,512]{1,0:T(8,128)(2,1)} %select_select_fusion.1.refs_7_), channel_id=1, source_target_pairs={{0,1},{1,0},{2,3},{3,2},{4,5},{5,4},{6,7},{7,6},{8,9},{9,8},{10,11... | collective-permute-start | bytes 3145736 | tf_op jit(solution)/shard_map/ppermute | solution.py:68
  224.2 44.9 %collective-permute-start.34 = (bf16[1024,512]{1,0:T(8,128)(2,1)}, bf16[1024,512]{1,0:T(8,128)(2,1)}, u32[]{:S(2)}, u32[]{:S(2)}) collective-permute-start(bf16[1024,512]{1,0:T(8,128)(2,1)} %select_select_fusion.1.refs_7_), channel_id=1, source_target_pairs={{0,16},{16,0},{1,17},{17,1},{2,18},{18,2},{3,19},{19,3},{4,20},{20... | collective-permute-start | bytes 3145736 | tf_op jit(solution)/shard_map/ppermute | solution.py:343
  237.6 38.4 %collective-permute-start.39 = (bf16[128,4096]{1,0:T(8,128)(2,1)}, bf16[128,4096]{1,0:T(8,128)(2,1)}, u32[]{:S(2)}, u32[]{:S(2)}) collective-permute-start(bf16[128,4096]{1,0:T(8,128)(2,1)} %add_convert_fusion.1), channel_id=1, source_target_pairs={{4,0},{8,4},{12,8},{5,1},{9,5},{13,9},{6,2},{10,6},{14,10},{7,3},{... | collective-permute-start | bytes 3145736 | tf_op jit(solution)/shard_map/ppermute | solution.py:334
  238.9 37.1 %collective-permute-start.40 = (bf16[128,4096]{1,0:T(8,128)(2,1)}, bf16[128,4096]{1,0:T(8,128)(2,1)}, u32[]{:S(2)}, u32[]{:S(2)}) collective-permute-start(bf16[128,4096]{1,0:T(8,128)(2,1)} %add_convert_fusion), channel_id=1, source_target_pairs={{0,4},{4,8},{8,12},{1,5},{5,9},{9,13},{2,6},{6,10},{10,14},{3,7},{... | collective-permute-start | bytes 3145736 | tf_op jit(solution)/shard_map/ppermute | solution.py:335
  (71 other events, 831.0 us)

commit v4 on v3

v4 whole, which is shorter than its diff:
```python
import functools

import jax
import jax.numpy as jnp
from jax import lax
from jax.experimental import pallas as pl
from jax.experimental.pallas import tpu as pltpu
from jax.sharding import PartitionSpec as P

adapter_scale_factor = 0.25
F32 = jnp.float32
BF16 = jnp.bfloat16
LANES = 128
PIECES = 1
TRANS_B = (((1,), (1,)), ((), ()))
SMALL = pl.CostEstimate(flops=1, bytes_accessed=1, transcendentals=0)
LONG = pl.CostEstimate(flops=20 * 10**9, bytes_accessed=1, transcendentals=0)
TRANS_A = (((0,), (0,)), ((), ()))


def after(value, *earlier):
    return lax.optimization_barrier((value, *earlier))[0]


def mark_kernel(*refs):
    refs[-1][...] = jnp.zeros_like(refs[-1])


def mark(cost, *arrays):
    return pl.pallas_call(
        mark_kernel,
        in_specs=[pl.BlockSpec(memory_space=pl.ANY) for _ in arrays],
        out_shape=jax.ShapeDtypeStruct((8, LANES), F32),
        compiler_params=pltpu.CompilerParams(vmem_limit_bytes=2**20),
        cost_estimate=cost,
    )(*arrays)


def around(axis):
    count = lax.axis_size(axis)
    return [(i, (i + 1) % count) for i in range(count)]


def line_step(up, down, step):
    count, at = lax.axis_size("fsdp"), lax.axis_index("fsdp")
    if step == count - 1 and count >= 4:
        both = lax.ppermute(
            jnp.where(at == 1, down, up), "fsdp", [(count - 2, count - 1), (1, 0)]
        )
        return both, both
    return (
        lax.ppermute(up, "fsdp", [(i, i + 1) for i in range(step - 1, count - 1)]),
        lax.ppermute(down, "fsdp", [(i, i - 1) for i in range(1, count - step + 1)]),
    )


def arrives(step, place):
    count = lax.axis_size("fsdp")
    if 2 * place >= count:
        return (True, step) if step <= place else (False, step - place)
    room = count - 1 - place
    return (False, step) if step <= room else (True, step - room)


def arrival(up, down, step):
    count, at = lax.axis_size("fsdp"), lax.axis_index("fsdp")
    choices = {}
    for place in range(count):
        choices.setdefault(arrives(step, place), []).append(place)
    pick = None
    for (from_up, far), places in choices.items():
        one = up[far] if from_up else down[far]
        here = functools.reduce(jnp.logical_or, [at == place for place in places])
        pick = one if pick is None else jnp.where(here, one, pick)
    return pick


def arrival_owner(step):
    count, at = lax.axis_size("fsdp"), lax.axis_index("fsdp")
    owner = 0
    for place in range(count):
        from_up, far = arrives(step, place)
        owner = jnp.where(at == place, place - far if from_up else place + far, owner)
    return owner


def sum_over_tp(part):
    if lax.axis_size("tp") == 2:
        return part + lax.ppermute(part.astype(BF16), "tp", around("tp")).astype(F32)
    return lax.psum(part.astype(BF16), "tp").astype(F32)


def over_cores(one):
    every = [one]
    for _ in range(1, lax.axis_size("sub")):
        every.append(lax.ppermute(every[-1], "sub", around("sub")))
    return every


def in_range(start, end, at, tokens):
    start, end = start[at : at + 1, :], end[at : at + 1, :]
    position = lax.broadcasted_iota(jnp.int32, (tokens, start.shape[1]), 0)
    return (position >= start) & (position < end)


def row_pieces(xs, chunk):
    rows = xs[0].shape[0] // PIECES
    one = lambda piece: pl.BlockSpec((rows, chunk), lambda k: (piece, k))
    return [one(piece) for _ in xs for piece in range(PIECES)]


def low_kernel(sources, count, rank, with_prior, *refs):
    xs, refs = refs[: sources * PIECES], refs[sources * PIECES :]
    blocks, (start, end), refs = refs[:count], refs[count : count + 2], refs[count + 2 :]
    prior = refs[0] if with_prior else None
    out, total = refs[-2:]
    piece = xs[0].shape[0]
    tokens = piece * PIECES
    step = pl.program_id(0)
    rows = jnp.concatenate([block[...] for block in blocks], axis=0)
    for at, x in enumerate(xs):
        here = pl.ds(at * piece, piece)
        part = lax.dot_general(x[...], rows, TRANS_B, preferred_element_type=F32)

        @pl.when(step == 0)
        def _():
            total[here, :] = part

        @pl.when(step > 0)
        def _():
            total[here, :] += part

    @pl.when(step == pl.num_programs(0) - 1)
    def _():
        for at in range(sources):
            here = pl.ds(at * tokens, tokens)
            chosen = jnp.where(in_range(start, end, at, tokens), total[here, :], 0.0)
            low = chosen[:, :LANES]
            for lane in range(LANES, chosen.shape[1], LANES):
                low = low + chosen[:, lane : lane + LANES]
            turn = LANES // 2
            while turn >= rank:
                low = low + pltpu.roll(low, turn, 1)
                turn //= 2
            out[here, :] = low + prior[here, :] if with_prior else low


def low_rank(xs, blocks, start, end, rank, prior=None):
    tokens, depth = xs[0].shape
    chunk = min(depth, 1024)
    columns = start.shape[1]
    rows = len(xs) * tokens
    fixed = lambda shape: pl.BlockSpec(shape, lambda k: (0, 0))
    operands = [x for x in xs for _ in range(PIECES)]
    operands += [*blocks, start, end] + ([] if prior is None else [prior])
    in_specs = row_pieces(xs, chunk)
    in_specs += [pl.BlockSpec((b.shape[0], chunk), lambda k: (0, k)) for b in blocks]
    in_specs += [fixed(start.shape), fixed(end.shape)]
    if prior is not None:
        in_specs.append(fixed((rows, LANES)))
    return pl.pallas_call(
        functools.partial(low_kernel, len(xs), len(blocks), rank, prior is not None),
        grid=(depth // chunk,),
        in_specs=in_specs,
        out_specs=fixed((rows, LANES)),
        out_shape=jax.ShapeDtypeStruct((rows, LANES), F32),
        scratch_shapes=[pltpu.VMEM((rows, columns), F32)],
        compiler_params=pltpu.CompilerParams(vmem_limit_bytes=20 * 2**20),
        cost_estimate=SMALL,
    )(*operands)


def spread(low, start, end, at):
    tokens, columns = low.shape[0], start.shape[1]
    repeated = jnp.concatenate([low] * (columns // LANES), axis=1)
    return jnp.where(in_range(start, end, at, tokens), repeated, 0.0).astype(BF16)


def spread_kernel(low, start, end, *outs):
    tokens = outs[0].shape[0]
    for at, out in enumerate(outs):
        out[...] = spread(low[pl.ds(at * tokens, tokens), :], start, end, at)


def spread_out(low, start, end):
    sources, columns = start.shape
    return pl.pallas_call(
        spread_kernel,
        out_shape=[jax.ShapeDtypeStruct((low.shape[0] // sources, columns), BF16)] * sources,
        compiler_params=pltpu.CompilerParams(vmem_limit_bytes=24 * 2**20),
        cost_estimate=SMALL,
    )(low, start, end)


def outer_kernel(scale, parts, low, start, end, *refs):
    xs, outs, wide = refs[: -1 - parts], refs[-1 - parts : -1], refs[-1]
    sources = len(xs) // PIECES
    tokens = low.shape[0] // sources

    @pl.when(pl.program_id(0) == 0)
    def _():
        for at in range(sources):
            here = pl.ds(at * tokens, tokens)
            wide[here, :] = spread(low[here, :], start, end, at)

    every = jnp.concatenate([x[...] for x in xs], axis=0)
    total = lax.dot_general(wide[...], every, TRANS_A, preferred_element_type=F32)
    if scale != 1.0:
        total = total * scale
    rows = total.shape[0] // parts
    for at, out in enumerate(outs):
        out[...] = total[at * rows : (at + 1) * rows].astype(out.dtype)


def outer(low, start, end, xs, scale, parts):
    tokens, features = xs[0].shape
    columns = start.shape[1]
    rows = columns // parts
    chunk = min(features, 512)
    fixed = lambda shape: pl.BlockSpec(shape, lambda k: (0, 0))
    moving = lambda count: pl.BlockSpec((count, chunk), lambda k: (0, k))
    return pl.pallas_call(
        functools.partial(outer_kernel, scale, parts),
        grid=(features // chunk,),
        in_specs=[fixed(low.shape), fixed(start.shape), fixed(end.shape)] + row_pieces(xs, chunk),
        out_specs=[moving(rows)] * parts,
        out_shape=[
            jax.ShapeDtypeStruct((rows, features), F32 if at == 0 else BF16) for at in range(parts)
        ],
        scratch_shapes=[pltpu.VMEM((len(xs) * tokens, columns), BF16)],
        compiler_params=pltpu.CompilerParams(vmem_limit_bytes=20 * 2**20),
        cost_estimate=SMALL,
    )(low, start, end, *[x for x in xs for _ in range(PIECES)])


def trade_kernel(_, *refs):
    *factors, other, low, out = refs
    tokens, at = out.shape[0], factors[0].shape[1]
    rows = factors[0].shape[0]
    for i, factor in enumerate(factors):
        out[i * rows : (i + 1) * rows, :at] = factor[...]
    out[:, at : at + other.shape[1]] = other[...]
    at += other.shape[1]
    for first in range(0, low.shape[0], tokens):
        out[:, at : at + LANES] = low[first : first + tokens, :].astype(BF16)
        at += LANES


def to_trade(place, factors, other, low, half):
    tokens = other.shape[0]
    width = half + other.shape[1] + low.shape[0] // tokens * LANES
    fixed = lambda one: pl.BlockSpec(one.shape, lambda i, s: (0, 0))
    return pl.pallas_call(
        trade_kernel,
        grid_spec=pltpu.PrefetchScalarGridSpec(
            num_scalar_prefetch=1,
            grid=(1,),
            in_specs=[pl.BlockSpec((one.shape[0], half), lambda i, s: (0, s[0])) for one in factors]
            + [fixed(other), fixed(low)],
            out_specs=pl.BlockSpec((tokens, width), lambda i, s: (0, 0)),
        ),
        out_shape=jax.ShapeDtypeStruct((tokens, width), BF16),
        compiler_params=pltpu.CompilerParams(vmem_limit_bytes=24 * 2**20),
        cost_estimate=SMALL,
    )(jnp.asarray(place, jnp.int32).reshape(1), *factors, other, low)


def input_gradient_kernel(sources, shards, factor_blocks, _, *refs):
    weights, refs = refs[:shards], refs[shards:]
    factors, refs = refs[:factor_blocks], refs[factor_blocks:]
    wides, refs = refs[:sources], refs[sources:]
    grads, outs = refs[: sources * shards], refs[-sources:]
    rows = jnp.concatenate([factor[...] for factor in factors], axis=0)
    for at in range(sources):
        total = jnp.dot(wides[at][...], rows, preferred_element_type=F32)
        for grad, weight in zip(grads[at * shards : (at + 1) * shards], weights, strict=True):
            total += lax.dot_general(grad[...], weight[...], TRANS_B, preferred_element_type=F32)
        outs[at][...] = total.astype(BF16)


def input_gradient_part(part, inner, whose, rows, grads, weights, wides, factors, halves, so_far):
    features = factors[0].shape[1]
    sources, shards, tokens = len(grads), len(weights), grads[0].shape[0]
    width = weights[0].shape[1]
    block = min(rows, 512)
    steps = rows // block
    scalars = jnp.stack([*whose, part, inner]).astype(jnp.int32)
    in_specs = [pl.BlockSpec((block, width), lambda j, s: (s[shards] * steps + j, 0))]
    in_specs += [pl.BlockSpec((block, width), lambda j, s: (j, 0)) for _ in range(shards - 1)]
    in_specs += [
        pl.BlockSpec((one.shape[0], block), lambda j, s: (0, s[shards] * steps + j)) for one in factors
    ]
    in_specs += [
        pl.BlockSpec((one.shape[0], block), lambda j, s: (0, s[shards + 1] * steps + j)) for one in halves
    ]
    in_specs += [pl.BlockSpec(wide.shape, lambda j, s: (0, 0)) for wide in wides]
    in_specs += [
        pl.BlockSpec((tokens, width), functools.partial(lambda k, j, s: (0, s[k]), k))
        for _ in grads
        for k in range(shards)
    ]
    operands = [scalars, *weights, *factors, *halves, *wides]
    operands += [grad for grad in grads for _ in range(shards)]
    aliases = {}
    if so_far is not None:
        in_specs.append(pl.BlockSpec(memory_space=pl.ANY))
        operands.append(so_far)
        aliases = {len(operands) - 1: 0}
    return pl.pallas_call(
        functools.partial(input_gradient_kernel, sources, shards, len(factors) + len(halves)),
        grid_spec=pltpu.PrefetchScalarGridSpec(
            num_scalar_prefetch=1,
            grid=(steps,),
            in_specs=in_specs,
            out_specs=[pl.BlockSpec((tokens, block), lambda j, s: (0, s[shards] * steps + j))]
            + [pl.BlockSpec((tokens, block), lambda j, s: (0, j))] * (sources - 1),
        ),
        out_shape=[jax.ShapeDtypeStruct((tokens, features), BF16)]
        + [jax.ShapeDtypeStruct((tokens, rows), BF16)] * (sources - 1),
        input_output_aliases=aliases,
        compiler_params=pltpu.CompilerParams(vmem_limit_bytes=56 * 2**20),
        cost_estimate=SMALL,
    )(*operands)


def local(activations, output_gradient, base_weight, factor_down, factor_up, counts, owners):
    tokens, features = activations.shape
    columns = output_gradient.shape[1]
    own_slots, rank = factor_down.shape[:2]
    slots = owners.shape[0]
    n, subs, groups = lax.axis_size("fsdp"), lax.axis_size("sub"), lax.axis_size("groups")
    z, sub, y = lax.axis_index("fsdp"), lax.axis_index("sub"), lax.axis_index("groups")
    own_rows = own_slots * rank
    other_core = [(i, (i + 1) % subs) for i in range(subs)]

    both = range(subs)
    events = []

    def event(*arrays, cost=SMALL):
        events.append(mark(cost, *arrays, *events[-1:]))
        return events[-1]

    half = features // subs
    copies = groups * subs
    part_rows, width = base_weight.shape[0] // copies, base_weight.shape[1]

    def line_on(ups, downs, step, *earlier):
        if step < n:
            one, two = line_step(after(ups[-1], *earlier), after(downs[-1], *earlier), step)
            ups.append(one)
            downs.append(two)

    g_cores = over_cores(output_gradient)
    count_cores = over_cores(counts[0])
    soon = [*g_cores[1:], *count_cores[1:]]
    x_cores = over_cores(after(activations, *soon))
    factors = [factor_down.reshape(own_rows, features)]

    def factor_on(*earlier):
        if len(factors) < n:
            factors.append(lax.ppermute(after(factors[-1], *earlier), "fsdp", around("fsdp")))

    up_here = factor_up.reshape(own_rows, columns)
    up_line = [up_here] + [
        lax.ppermute(up_here, "fsdp", [(i, (i + far) % n) for i in range(n)]) for far in range(1, n)
    ]
    factor_on(*soon)

    hot = owners[:, None] == lax.broadcasted_iota(jnp.int32, (slots, slots), 1)
    bounds = []
    for count in count_cores:
        seg_ends = jnp.cumsum(count)
        starts = jnp.sum(jnp.where(hot, (seg_ends - count)[:, None], 0), axis=0)
        ends = jnp.sum(jnp.where(hot, seg_ends[:, None], 0), axis=0)
        bounds.append((starts, ends))

    def ranges(devices):
        which = jnp.concatenate(
            [(at * subs + core) * own_slots + jnp.arange(own_slots, dtype=jnp.int32) for at, core in devices]
        )
        which = jnp.repeat(which, rank)
        found = which[:, None] == jnp.arange(slots, dtype=jnp.int32)[None, :]
        return tuple(
            jnp.stack([jnp.sum(jnp.where(found, one[end][None, :], 0), axis=1) for one in bounds])
            for end in range(2)
        )

    along_line = ranges([((z - j) % n, sub) for j in range(n)])
    weight_here = lax.dynamic_index_in_dim(
        base_weight.reshape(copies, part_rows, width), sub * groups + y, 0, keepdims=False
    )
    w_up, w_down = [weight_here], [weight_here]
    came = event(*up_line[1:], weight_here)

    line_on(w_up, w_down, 1, came)
    if lax.axis_size("tp") == 2:
        tp_other = lax.ppermute(after(output_gradient, came), "tp", around("tp"))
        first = lax.axis_index("tp") == 0

        def whole_grad(one, two):
            return jnp.concatenate([jnp.where(first, one, two), jnp.where(first, two, one)], axis=1)
    else:
        tp_other = lax.all_gather(output_gradient, "tp", axis=1, tiled=True)

        def whole_grad(one, two):
            return two

    low_back = low_rank([after(g_cores[0], came), *g_cores[1:]], up_line, *along_line, rank)
    low_back = sum_over_tp(adapter_scale_factor * low_back)
    down_blocks = outer(low_back, *along_line, x_cores, 1.0, n)
    came = event(factors[-1], *x_cores[1:], cost=LONG)
    factor_on(came)
    came = event(w_up[1], w_down[1], tp_other)

    weight_arrivals, whose = [], [z] + [arrival_owner(step) for step in range(1, n)]

    def weight_arrives(step, *earlier):
        mine = [after(arrival(w_up, w_down, step), *earlier)]
        for _ in range(1, groups):
            mine.append(lax.ppermute(mine[-1], "groups", around("groups")))
        weight_arrivals.append(mine)

    def to_sum(step):
        lower, upper = down_blocks[n - step], down_blocks[step]
        if step > 1:
            lower = (lower.astype(F32) + from_above.astype(F32)).astype(BF16)
            upper = (upper.astype(F32) + from_below.astype(F32)).astype(BF16)
        elif n >= 4:
            lower = upper = jnp.where(z == 0, upper, lower)
        return lower, upper

    def sum_on(step, lower, upper, *earlier):
        lower, upper = after(lower, *earlier), after(upper, *earlier)
        if step == 1 and n >= 4:
            got = lax.ppermute(lower, "fsdp", [(n - 1, n - 2), (0, 1)])
            return got, got
        return (
            lax.ppermute(lower, "fsdp", [(i, i - 1) for i in range(n - step, n)]),
            lax.ppermute(upper, "fsdp", [(i, i + 1) for i in range(step)]),
        )

    from_above = from_below = low_in = None
    early = min(n, 3)
    if early * own_rows % LANES:
        early = 0
    for step in range(2, n):
        line_on(w_up, w_down, step, came)
        from_above, from_below = sum_on(step - 1, *to_sum(step - 1), came)
        weight_arrives(step - 1, came)
        if step == n - 1 and early:
            low_in = low_rank(
                [after(x_cores[0], came), *x_cores[1:]],
                factors[:early],
                *ranges([((z - j) % n, sub) for j in range(early)]),
                rank,
            )
        factor_on(event(factors[-1], cost=LONG))
        if step == n - 1:
            low_in = low_rank(
                x_cores, factors[early:], *ranges([((z - j) % n, sub) for j in range(early, n)]), rank, low_in
            )
            low_in = sum_over_tp(low_in)
            came = event(low_in)
        came = event(w_up[-1], w_down[-1], from_above, from_below, *weight_arrivals[-1][1:])

    traded = [None]
    for b in range(1, subs):
        there = to_trade((sub + b) % subs, factors, tp_other, low_back, half)
        there = lax.ppermute(after(there, came), "sub", [(i, (i + b) % subs) for i in range(subs)])
        traded.append((there, there[:, half:]))
    low_back_all, tp_cores = low_back, [tp_other]
    cut = tp_other.shape[1]
    for b in range(1, subs):
        rest = traded[b][1]
        tp_cores.append(rest[:, :cut])
        theirs = [rest[:, cut + at * LANES : cut + (at + 1) * LANES] for at in both]
        theirs = jnp.concatenate([theirs[(at - b) % subs] for at in both], axis=0)
        low_back_all = low_back_all + theirs.astype(F32)
    grads = [whole_grad(one, two) for one, two in zip(g_cores, tp_cores, strict=True)]
    wides = spread_out(
        low_back_all, *ranges([((z - j) % n, (sub - b) % subs) for b in both for j in range(n)])
    )

    up_pieces = outer(low_in, *along_line, g_cores, adapter_scale_factor, n)
    if n > 2:
        lower, upper = to_sum(n - 1)
        lower = jnp.concatenate([lower, up_pieces[1]], axis=1)
        upper = jnp.concatenate([upper, up_pieces[n - 1]], axis=1)

    up_total, round_4 = up_pieces[0], []
    if n > 2:
        from_above, from_below = sum_on(n - 1, lower, upper, came)
        weight_arrives(n - 1, came)
        round_4 += [from_above, from_below]
        up_total = up_total + from_above[:, features:].astype(F32) + from_below[:, features:].astype(F32)
        from_above, from_below = from_above[:, :features], from_below[:, :features]
    for far in range(1, n):
        pairs = [(i, (i - far) % n) for i in range(n)]
        if n > 2 and far == 1:
            far_piece = jnp.where(z == 0, up_pieces[1], up_pieces[n - 1])
            pairs = [(0, n - 1), (n - 1, 0)]
        elif n > 2 and far == n - 1:
            continue
        else:
            far_piece = up_pieces[far]
        got = lax.ppermute(
            after(far_piece, came, *[one[0] for one in traded[1:]]), "fsdp", pairs
        )
        up_total = up_total + got.astype(F32)
        round_4.append(got)
    up_total = up_total + came[0, 0]
    grad_down = down_blocks[0] + from_above.astype(F32) + from_below.astype(F32)
    input_gradient, others = None, []
    for a in range(groups):
        inner = (y - a) % groups
        input_gradient, *for_others = input_gradient_part(
            sub * groups + inner,
            inner,
            whose,
            part_rows,
            grads,
            [base_weight] + [arrived[a] for arrived in weight_arrivals],
            wides,
            factors,
            [one[0] for one in traded[1:]],
            input_gradient,
        )
        others.append(for_others)

    round_4.append(input_gradient)
    for a in range(groups):
        for b, one in enumerate(others[a], 1):
            got = lax.ppermute(
                after(one, *round_4), "sub", [(i, (i - b) % subs) for i in range(subs)]
            )
            part = ((sub + b) % subs) * groups + (y - a) % groups
            input_gradient = lax.dynamic_update_slice_in_dim(input_gradient, got, part * part_rows, axis=1)
    return (
        input_gradient,
        grad_down.reshape(own_slots, rank, features),
        up_total.reshape(own_slots, rank, columns),
    )


def solution(mesh):
    placed = (
        P(("groups", "fsdp", "sub"), "tp"),
        P(("groups", "fsdp", "sub"), "tp"),
        P("tp", "fsdp"),
        P(("groups", "fsdp", "sub"), None, "tp"),
        P(("groups", "fsdp", "sub"), None, "tp"),
        P(("groups", "fsdp", "sub"), None),
        P("groups"),
    )
    return jax.shard_map(
        local,
        mesh=mesh,
        in_specs=placed,
        out_specs=(
            P(("groups", "fsdp", "sub"), "tp"),
            P(("groups", "fsdp", "sub"), None, "tp"),
            P(("groups", "fsdp", "sub"), None, "tp"),
        ),
        check_vma=False,
    )
```

time: 287 us -> 247 us (0.86)
  other arithmetic: 34.4 us -> 15.4 us
  local copies, waits for them, and re-layouts: 29 us -> 10.3 us
  starting transfers between devices: 63.4 us -> 50.7 us
  waiting for transfers between devices: 101 us -> 113 us
    ppermute x5 -> x11, waiting for transfers between devices: 11.8 us -> 82.6 us  [the longest x3 34.5 us: factor_on(): lax.ppermute(after(factors[-1], *earlier), 'fsdp', around('fsdp'))]
    ppermute x6 -> x2, waiting for transfers between devices: 51.6 us -> 2.7 us  [line_step(): lax.ppermute(down, 'fsdp', [(i, i - 1) for i in range(1, count - step + 1)])]
    unnamed x102 -> x38, local copies, waits for them, and re-layouts: 22.7 us -> 2.46 us
    ppermute x5 -> x11, starting transfers between devices: 6.87 us -> 20.8 us  [the longest x2 7.13 us: local(): lax.ppermute(after(far_piece, came, *[one[0] for one in traded[1:]]), 'fs...]
    ppermute x6 -> x2, waiting for transfers between devices: 16.4 us -> 3.3 us  [line_step(): lax.ppermute(up, 'fsdp', [(i, i + 1) for i in range(step - 1, count - 1)])]
    ppermute x6 -> x2, starting transfers between devices: 15.7 us -> 5.33 us  [line_step(): lax.ppermute(up, 'fsdp', [(i, i + 1) for i in range(step - 1, count - 1)])]
    select_n x7 -> x8, other arithmetic: 11 us -> 1.64 us  [the longest x1 0.73 us: local(): far_piece = jnp.where(z == 0, up_pieces[1], up_pieces[n - 1])]
    convert_element_type x8 -> x3, other arithmetic: 9.53 us -> 0.74 us  [the longest x2 0.49 us: to_sum(): lower = (lower.astype(F32) + from_above.astype(F32)).astype(BF16)]
  transfers between devices with their start and end apart: 44 -> 30, of which waited for: 15 -> 13; matrix products, arithmetic and copies ran while one was open for 14% -> 9% of each run, Pallas kernels for 18% -> 23%
where the time goes in v4:
time: 247 us; the launch traced here: 246 us
  waiting for transfers between devices  113 us (46%)
  Pallas kernels  56.2 us (23%)
  starting transfers between devices  50.7 us (21%)
  other arithmetic  15.4 us (6%)
  local copies, waits for them, and re-layouts  10.3 us (4%)
    ppermute x3, waiting for transfers between devices, factor_on(): lax.ppermute(after(factors[-1], *earlier), 'fsdp', around('fsdp'))  34.5 us
    pallas_call x2, Pallas kernels, input_gradient_part(): pl.pallas_call(functools.partial(input_gradient_kernel, sources, shards,...  25 us
    ppermute x1, waiting for transfers between devices, sum_on(): got = lax.ppermute(lower, 'fsdp', [(n - 1, n - 2), (0, 1)])  19.8 us
    pallas_call x3, Pallas kernels, low_rank(): pl.pallas_call(functools.partial(low_kernel, len(xs), len(blocks), rank,...  19.5 us
    ppermute x3, waiting for transfers between devices, local(): lax.ppermute(up_here, 'fsdp', [(i, (i + far) % n) for i in range(n)])  15.7 us
    ppermute x1, waiting for transfers between devices, local(): tp_other = lax.ppermute(after(output_gradient, came), 'tp', around('tp'))  12.7 us
    ppermute x2, waiting for transfers between devices, local(): lax.ppermute(after(far_piece, came, *[one[0] for one in traded[1:]]), 'fs...  10.8 us
    pallas_call x2, Pallas kernels, outer(): pl.pallas_call(functools.partial(outer_kernel, scale, parts), grid=(featu...  10.8 us
  transfers between devices with their start and end apart: 30, of which 13 were waited for; matrix products, arithmetic and copies ran while one was open for 9% of the time, Pallas kernels for 23%

profile of v4, /device:TPU:0, one launch (start us, length us, event | category | flops | bytes accessed | tf_op | source)
XLA Modules:
  0.0 246.5 jit_solution(10459359287688783224)
XLA Ops:
  4.0 4.7 %collective-permute-start.2 = (bf16[128,1024]{1,0:T(8,128)(2,1)}, bf16[128,1024]{1,0:T(8,128)(2,1)S(1)}, u32[]{:S(2)}, u32[]{:S(2)}) collective-permute-start(bf16[128,1024]{1,0:T(8,128)(2,1)} %bitcast.38), channel_id=1, source_target_pairs={{0,12},{4,0},{8,4},{12,8},{1,13},{5,1},{9,5},{13,9},{2,14},{6,2},{... | collective-permute-start | bytes 786440 | tf_op jit(solution)/shard_map/ppermute | solution.py:365
  16.2 15.7 %collective-permute-done.1.refs_1_.refs_4_ = bf16[128,1024]{1,0:T(8,128)(2,1)} collective-permute-done((bf16[128,1024]{1,0:T(8,128)(2,1)}, bf16[128,1024]{1,0:T(8,128)(2,1)}, u32[]{:S(2)}, u32[]{:S(2)}) %collective-permute-start.1) | collective-permute-done | bytes 262176 | tf_op jit(solution)/shard_map/ppermute | solution.py:365
  36.2 4.6 %collective-permute-start.3 = (bf16[1024,512]{1,0:T(8,128)(2,1)}, bf16[1024,512]{1,0:T(8,128)(2,1)S(1)}, u32[]{:S(2)}, u32[]{:S(2)}) collective-permute-start(bf16[1024,512]{1,0:T(8,128)(2,1)} %dynamic-slice_bitcast_fusion.refs_3_), channel_id=1, source_target_pairs={{0,4},{4,8},{8,12},{1,5},{5,9},{9,13},{2,6},{6,10},{10,14},{3,7},{... | collective-permute-start | bytes 3145736 | tf_op jit(solution)/shard_map/ppermute | solution.py:52
  42.2 2.8 %shard_map.97 = f32[1024,128]{1,0:T(8,128)S(1)} custom-call(bf16[512,1024]{1,0:T(8,128)(2,1)S(1)} %copy-done.5, bf16[512,1024]{1,0:T(8,128)(2,1)S(1)} %collective-permute-done.6.refs_1_, bf16[128,1024]{1,0:T(8,128)(2,1)S(1)} %bitcast.41, bf16[128,1024]{1,0:T(8,128)(2,1)} %collective-permute-done.refs_0_.refs_3_, ...), custom_call_target="tpu_custom_call" | custom-call | flops 1 | bytes 1 | tf_op jit(solution)/shard_map/pallas_call | solution.py:161
  45.1 12.7 %collective-permute-done.5.refs_2_.refs_4_ = bf16[512,1024]{1,0:T(8,128)(2,1)S(1)} collective-permute-done((bf16[512,1024]{1,0:T(8,128)(2,1)S(1)}, bf16[512,1024]{1,0:T(8,128)(2,1)S(1)}, u32[]{:S(2)}, u32[]{:S(2)}) %collective-permute-start.5) | collective-permute-done | bytes 1048608 | tf_op jit(solution)/shard_map/ppermute | solution.py:397
  61.4 3.3 %collective-permute-done.3.refs_0_ = bf16[1024,512]{1,0:T(8,128)(2,1)S(1)} collective-permute-done((bf16[1024,512]{1,0:T(8,128)(2,1)}, bf16[1024,512]{1,0:T(8,128)(2,1)S(1)}, u32[]{:S(2)}, u32[]{:S(2)}) %collective-permute-start.3) | collective-permute-done | bytes 1048608 | tf_op jit(solution)/shard_map/ppermute | solution.py:52
  64.8 21.0 %collective-permute-done.8.refs_0_.refs_3_.refs_1_.refs_5_ = bf16[128,4096]{1,0:T(8,128)(2,1)S(1)} collective-permute-done((bf16[128,4096]{1,0:T(8,128)(2,1)S(1)}, bf16[128,4096]{1,0:T(8,128)(2,1)S(1)}, u32[]{:S(2)}, u32[]{:S(2)}) %collective-permute-start.8) | collective-permute-done | bytes 1048608 | tf_op jit(solution)/shard_map/ppermute | solution.py:361
  91.3 8.7 %shard_map.98 = (f32[128,4096]{1,0:T(8,128)S(1)}, bf16[128,4096]{1,0:T(8,128)(2,1)S(1)}, bf16[128,4096]{1,0:T(8,128)(2,1)S(1)}, bf16[128,4096]{1,0:T(8,128)(2,1)S(1)}) custom-call(f32[1024,128]{1,0:T(8,128)S(1)} %convert_add_fusion.3.low.refs_5_, s32[2,512]{1,0:T(2,128)S(1)} %pad_add_fusion.2.refs_6_.start, s32[2,512]{1,0:T(2,128)S(1)} %pad_add_fusion.3.refs_7_.end, ...), custom_call_target="tpu_custom_call" | custom-call | flops 1 | bytes 1 | tf_op jit(solution)/shard_map/pallas_call | solution.py:222
  100.1 7.0 %collective-permute-start.14 = (bf16[128,4096]{1,0:T(8,128)(2,1)S(1)}, bf16[128,4096]{1,0:T(8,128)(2,1)S(1)}, u32[]{:S(2)}, u32[]{:S(2)}) collective-permute-start(bf16[128,4096]{1,0:T(8,128)(2,1)S(1)} %broadcast_select_fusion.5), channel_id=1, source_target_pairs={{12,8},{0,4},{13,9},{1,5},{14,10},{2,6},{15,11},{3,7},{28,24},{16,... | collective-permute-start | bytes 3145736 | tf_op jit(solution)/shard_map/ppermute | solution.py:435
  107.1 6.7 %collective-permute-done.15.refs_0_.refs_4_.refs_2_.refs_6_ = bf16[128,4096]{1,0:T(8,128)(2,1)S(1)} collective-permute-done((bf16[128,4096]{1,0:T(8,128)(2,1)S(1)}, bf16[128,4096]{1,0:T(8,128)(2,1)S(1)}, u32[]{:S(2)}, u32[]{:S(2)}) %collective-permute-start.15) | collective-permute-done | bytes 1048608 | tf_op jit(solution)/shard_map/ppermute | solution.py:361
  113.8 19.8 %collective-permute-done.14.refs_2_.refs_3_ = bf16[128,4096]{1,0:T(8,128)(2,1)S(1)} collective-permute-done((bf16[128,4096]{1,0:T(8,128)(2,1)S(1)}, bf16[128,4096]{1,0:T(8,128)(2,1)S(1)}, u32[]{:S(2)}, u32[]{:S(2)}) %collective-permute-start.14) | collective-permute-done | bytes 1048608 | tf_op jit(solution)/shard_map/ppermute | solution.py:435
  136.2 3.1 %collective-permute-start.19 = (bf16[128,4096]{1,0:T(8,128)(2,1)S(1)}, bf16[128,4096]{1,0:T(8,128)(2,1)S(1)}, u32[]{:S(2)}, u32[]{:S(2)}) collective-permute-start(bf16[128,4096]{1,0:T(8,128)(2,1)S(1)} %add_convert_fusion.2), channel_id=1, source_target_pairs={{0,4},{4,8},{1,5},{5,9},{2,6},{6,10},{3,7},{7,11},{16,20},{20,24},... | collective-permute-start | bytes 3145736 | tf_op jit(solution)/shard_map/ppermute | solution.py:439
  143.4 8.6 %shard_map.101.refs_5_ = f32[1024,128]{1,0:T(8,128)S(1)} custom-call(bf16[512,4096]{1,0:T(8,128)(2,1)S(1)} %copy-done, bf16[512,4096]{1,0:T(8,128)(2,1)} %collective-permute-done.9.refs_1_, bf16[128,4096]{1,0:T(8,128)(2,1)S(1)} %bitcast.36, bf16[128,4096]{1,0:T(8,128)(2,1)S(1)} %collective-permute-done.8.refs_0_.refs_3_.refs_1_.refs_5_, ...), custom_call_target="tpu_custom_call" | custom-call | flops 1 | bytes 1 | tf_op jit(solution)/shard_map/pallas_call | solution.py:161
  152.0 6.8 %collective-permute-done.20.refs_2_.refs_0_.refs_3_.refs_7_ = bf16[128,4096]{1,0:T(8,128)(2,1)S(1)} collective-permute-done((bf16[128,4096]{1,0:T(8,128)(2,1)S(1)}, bf16[128,4096]{1,0:T(8,128)(2,1)S(1)}, u32[]{:S(2)}, u32[]{:S(2)}) %collective-permute-start.20) | collective-permute-done | bytes 1048608 | tf_op jit(solution)/shard_map/ppermute | solution.py:361
  158.8 8.0 %shard_map.102 = f32[1024,128]{1,0:T(8,128)S(1)} custom-call(bf16[512,4096]{1,0:T(8,128)(2,1)S(1)} %copy-done, bf16[512,4096]{1,0:T(8,128)(2,1)} %collective-permute-done.9.refs_1_, bf16[128,4096]{1,0:T(8,128)(2,1)S(1)} %collective-permute-done.20.refs_2_.refs_0_.refs_3_.refs_7_, s32[2,128]{1,0:T(2,128)S(1)} %pad_add_fusion.6.refs_3_, ...), custom_call_target="tpu_custom_call" | custom-call | flops 1 | bytes 1 | tf_op jit(solution)/shard_map/pallas_call | solution.py:161
  167.5 5.8 %collective-permute-done.21 = bf16[1024,128]{1,0:T(8,128)(2,1)S(1)} collective-permute-done((bf16[1024,128]{1,0:T(8,128)(2,1)S(1)}, bf16[1024,128]{1,0:T(8,128)(2,1)S(1)}, u32[]{:S(2)}, u32[]{:S(2)}) %collective-permute-start.21) | collective-permute-done | bytes 262176 | tf_op jit(solution)/shard_map/ppermute | solution.py:89
  173.7 4.7 %collective-permute-done.17.refs_0_.refs_1_ = bf16[1024,512]{1,0:T(8,128)(2,1)S(1)} collective-permute-done((bf16[1024,512]{1,0:T(8,128)(2,1)S(1)}, bf16[1024,512]{1,0:T(8,128)(2,1)S(1)}, u32[]{:S(2)}, u32[]{:S(2)}) %collective-permute-start.17) | collective-permute-done | bytes 1048608 | tf_op jit(solution)/shard_map/ppermute | solution.py:47
  185.7 3.4 %collective-permute-start.25 = (bf16[128,5120]{1,0:T(8,128)(2,1)}, bf16[128,5120]{1,0:T(8,128)(2,1)}, u32[]{:S(2)}, u32[]{:S(2)}) collective-permute-start(bf16[128,5120]{1,0:T(8,128)(2,1)} %pad_maximum_fusion.3), channel_id=1, source_target_pairs={{0,4},{4,8},{8,12},{1,5},{5,9},{9,13},{2,6},{6,10},{10,14},{3,7},{... | collective-permute-start | bytes 3932168 | tf_op jit(solution)/shard_map/ppermute | solution.py:439
  192.9 5.4 %collective-permute-start.26 = (bf16[128,1024]{1,0:T(8,128)(2,1)}, bf16[128,1024]{1,0:T(8,128)(2,1)}, u32[]{:S(2)}, u32[]{:S(2)}) collective-permute-start(bf16[128,1024]{1,0:T(8,128)(2,1)} %broadcast_select_fusion.8), channel_id=1, source_target_pairs={{0,12},{12,0},{1,13},{13,1},{2,14},{14,2},{3,15},{15,3},{16,28},{2... | collective-permute-start | bytes 786440 | tf_op jit(solution)/shard_map/ppermute | solution.py:506
  202.0 12.4 %shard_map.108 = (bf16[512,4096]{1,0:T(8,128)(2,1)}, bf16[512,1024]{1,0:T(8,128)(2,1)}) custom-call(s32[6]{0:T(128)} %stack.139._, bf16[4096,512]{1,0:T(8,128)(2,1)} %refs_0_.8, bf16[1024,512]{1,0:T(8,128)(2,1)} %copy-done.14, bf16[1024,512]{1,0:T(8,128)(2,1)} %copy-done.15, bf16[1024,512]{1,0:T(8,128)(2,1)} %copy-done.13, bf16[128,4096]{1,0:T(8,128)(2,1)} %bitcast.33, ...), custom_call_target="tpu_custom_call" | custom-call | flops 1 | bytes 1 | tf_op jit(solution)/shard_map/pallas_call | solution.py:309
  214.4 12.6 %shard_map.109 = (bf16[512,4096]{1,0:T(8,128)(2,1)}, bf16[512,1024]{1,0:T(8,128)(2,1)}) custom-call(s32[6]{0:T(128)} %stack.112._, bf16[4096,512]{1,0:T(8,128)(2,1)} %refs_0_.8, bf16[1024,512]{1,0:T(8,128)(2,1)} %copy-done.6, bf16[1024,512]{1,0:T(8,128)(2,1)} %copy-done.7, ...), custom_call_target="tpu_custom_call", output_to_operand_aliasing={{0}: (20, {})} | custom-call | flops 1 | bytes 1 | tf_op jit(solution)/shard_map/pallas_call | solution.py:309
  227.0 10.8 %collective-permute-done.27 = bf16[128,1024]{1,0:T(8,128)(2,1)} collective-permute-done((bf16[128,1024]{1,0:T(8,128)(2,1)S(1)}, bf16[128,1024]{1,0:T(8,128)(2,1)}, u32[]{:S(2)}, u32[]{:S(2)}) %collective-permute-start.27) | collective-permute-done | bytes 262176 | tf_op jit(solution)/shard_map/ppermute | solution.py:506
  238.3 3.2 %convert_add_fusion = f32[128,4096]{1,0:T(8,128)} fusion(f32[128,4096]{1,0:T(8,128)S(1)} %get-tuple-element.75, bf16[128,5120]{1,0:T(8,128)(2,1)} %collective-permute-done.25, bf16[128,5120]{1,0:T(8,128)(2,1)} %collective-permute-done.24), kind=kLoop, calls=%fused_computation.2 | loop fusion | flops 2097152 | bytes 6291456 | tf_op jit(solution)/shard_map/add | solution.py:512
  241.5 2.9 %add_add_fusion = f32[128,1024]{1,0:T(8,128)} fusion(bf16[128,1024]{1,0:T(8,128)(2,1)} %collective-permute-done.27, bf16[128,1024]{1,0:T(8,128)(2,1)} %collective-permute-done.26, f32[128,1024]{1,0:T(8,128)S(1)} %get-tuple-element.76, bf16[128,5120]{1,0:T(8,128)(2,1)} %collective-permute-done.25, bf16[128,5120]{1,0:T(8,128)(2,1)} %collective-permute-done.24, ...), kind=kLoop, calls=%fused_computation.18 | loop fusion | flops 1179648 | bytes 2097156 | tf_op jit(solution)/shard_map/add | solution.py:511
  (162 shorter events, 50.2 us)
Async XLA Ops:
  3.7 82.1 %collective-permute-start.9 = (bf16[512,4096]{1,0:T(8,128)(2,1)}, bf16[512,4096]{1,0:T(8,128)(2,1)}, u32[]{:S(2)}, u32[]{:S(2)}) collective-permute-start(bf16[512,4096]{1,0:T(8,128)(2,1)} %refs_0_.6), channel_id=1, source_target_pairs={{0,1},{1,0},{2,3},{3,2},{4,5},{5,4},{6,7},{7,6},{8,9},{9,8},{10,11... | collective-permute-start | bytes 12582920 | tf_op jit(solution)/shard_map/ppermute | solution.py:96
  8.8 23.1 %collective-permute-start.1 = (bf16[128,1024]{1,0:T(8,128)(2,1)}, bf16[128,1024]{1,0:T(8,128)(2,1)}, u32[]{:S(2)}, u32[]{:S(2)}) collective-permute-start(bf16[128,1024]{1,0:T(8,128)(2,1)} %bitcast.39), channel_id=1, source_target_pairs={{0,8},{4,12},{8,0},{12,4},{1,9},{5,13},{9,1},{13,5},{2,10},{6,14},... | collective-permute-start | bytes 786440 | tf_op jit(solution)/shard_map/ppermute | solution.py:365
  8.8 23.1 %collective-permute-start = (bf16[128,1024]{1,0:T(8,128)(2,1)}, bf16[128,1024]{1,0:T(8,128)(2,1)}, u32[]{:S(2)}, u32[]{:S(2)}) collective-permute-start(bf16[128,1024]{1,0:T(8,128)(2,1)} %bitcast.40), channel_id=1, source_target_pairs={{0,4},{4,8},{8,12},{12,0},{1,5},{5,9},{9,13},{13,1},{2,6},{6,10},{... | collective-permute-start | bytes 786440 | tf_op jit(solution)/shard_map/ppermute | solution.py:365
  33.2 24.6 %collective-permute-start.5 = (bf16[512,1024]{1,0:T(8,128)(2,1)S(1)}, bf16[512,1024]{1,0:T(8,128)(2,1)S(1)}, u32[]{:S(2)}, u32[]{:S(2)}) collective-permute-start(bf16[512,1024]{1,0:T(8,128)(2,1)S(1)} %copy-done.5), channel_id=1, source_target_pairs={{0,2},{2,0},{1,3},{3,1},{4,6},{6,4},{5,7},{7,5},{8,10},{10,8},{9,1... | collective-permute-start | bytes 3145736 | tf_op jit(solution)/shard_map/ppermute | solution.py:397
  34.9 26.5 %collective-permute-start.4 = (bf16[1024,512]{1,0:T(8,128)(2,1)}, bf16[1024,512]{1,0:T(8,128)(2,1)S(1)}, u32[]{:S(2)}, u32[]{:S(2)}) collective-permute-start(bf16[1024,512]{1,0:T(8,128)(2,1)} %dynamic-slice_bitcast_fusion.refs_3_), channel_id=1, source_target_pairs={{4,0},{8,4},{12,8},{5,1},{9,5},{13,9},{6,2},{10,6},{14,10},{7,3},{... | collective-permute-start | bytes 3145736 | tf_op jit(solution)/shard_map/ppermute | solution.py:53
  36.2 28.5 %collective-permute-start.3 = (bf16[1024,512]{1,0:T(8,128)(2,1)}, bf16[1024,512]{1,0:T(8,128)(2,1)S(1)}, u32[]{:S(2)}, u32[]{:S(2)}) collective-permute-start(bf16[1024,512]{1,0:T(8,128)(2,1)} %dynamic-slice_bitcast_fusion.refs_3_), channel_id=1, source_target_pairs={{0,4},{4,8},{8,12},{1,5},{5,9},{9,13},{2,6},{6,10},{10,14},{3,7},{... | collective-permute-start | bytes 3145736 | tf_op jit(solution)/shard_map/ppermute | solution.py:52
  40.9 44.9 %collective-permute-start.8 = (bf16[128,4096]{1,0:T(8,128)(2,1)S(1)}, bf16[128,4096]{1,0:T(8,128)(2,1)S(1)}, u32[]{:S(2)}, u32[]{:S(2)}) collective-permute-start(bf16[128,4096]{1,0:T(8,128)(2,1)S(1)} %bitcast.35), channel_id=1, source_target_pairs={{0,4},{4,8},{8,12},{12,0},{1,5},{5,9},{9,13},{13,1},{2,6},{6,10},{... | collective-permute-start | bytes 3145736 | tf_op jit(solution)/shard_map/ppermute | solution.py:361
  57.8 29.8 %collective-permute-start.13 = (bf16[1024,128]{1,0:T(8,128)(2,1)S(1)}, bf16[1024,128]{1,0:T(8,128)(2,1)S(1)}, u32[]{:S(2)}, u32[]{:S(2)}) collective-permute-start(bf16[1024,128]{1,0:T(8,128)(2,1)S(1)} %multiply_convert_fusion), channel_id=1, source_target_pairs={{0,2},{2,0},{1,3},{3,1},{4,6},{6,4},{5,7},{7,5},{8,10},{10,8},{9,1... | collective-permute-start | bytes 786440 | tf_op jit(solution)/shard_map/ppermute | solution.py:89
  85.8 28.0 %collective-permute-start.15 = (bf16[128,4096]{1,0:T(8,128)(2,1)S(1)}, bf16[128,4096]{1,0:T(8,128)(2,1)S(1)}, u32[]{:S(2)}, u32[]{:S(2)}) collective-permute-start(bf16[128,4096]{1,0:T(8,128)(2,1)S(1)} %collective-permute-done.8.refs_0_.refs_3_.refs_1_.refs_5_), channel_id=1, source_target_pairs={{0,4},{4,8},{8,12},{12,0},{1,5},{5,9},{9,13},{13,1},{2,6},{6,10},{... | collective-permute-start | bytes 3145736 | tf_op jit(solution)/shard_map/ppermute | solution.py:361
  87.6 46.3 %collective-permute-start.10 = (bf16[1024,512]{1,0:T(8,128)(2,1)S(1)}, bf16[1024,512]{1,0:T(8,128)(2,1)S(1)}, u32[]{:S(2)}, u32[]{:S(2)}) collective-permute-start(bf16[1024,512]{1,0:T(8,128)(2,1)S(1)} %broadcast_select_fusion.7.refs_1_), channel_id=1, source_target_pairs={{0,16},{16,0},{1,17},{17,1},{2,18},{18,2},{3,19},{19,3},{4,20},{20... | collective-permute-start | bytes 3145736 | tf_op jit(solution)/shard_map/ppermute | solution.py:420
  89.2 44.7 %collective-permute-start.11 = (bf16[1024,512]{1,0:T(8,128)(2,1)S(1)}, bf16[1024,512]{1,0:T(8,128)(2,1)S(1)}, u32[]{:S(2)}, u32[]{:S(2)}) collective-permute-start(bf16[1024,512]{1,0:T(8,128)(2,1)S(1)} %collective-permute-done.3.refs_0_), channel_id=1, source_target_pairs={{4,8},{8,12},{5,9},{9,13},{6,10},{10,14},{7,11},{11,15},{20,24},{2... | collective-permute-start | bytes 3145736 | tf_op jit(solution)/shard_map/ppermute | solution.py:52
  89.9 46.2 %collective-permute-start.12 = (bf16[1024,512]{1,0:T(8,128)(2,1)S(1)}, bf16[1024,512]{1,0:T(8,128)(2,1)S(1)}, u32[]{:S(2)}, u32[]{:S(2)}) collective-permute-start(bf16[1024,512]{1,0:T(8,128)(2,1)S(1)} %collective-permute-done.4.refs_1_), channel_id=1, source_target_pairs={{4,0},{8,4},{5,1},{9,5},{6,2},{10,6},{7,3},{11,7},{20,16},{24,20},... | collective-permute-start | bytes 3145736 | tf_op jit(solution)/shard_map/ppermute | solution.py:53
  100.1 33.5 %collective-permute-start.14 = (bf16[128,4096]{1,0:T(8,128)(2,1)S(1)}, bf16[128,4096]{1,0:T(8,128)(2,1)S(1)}, u32[]{:S(2)}, u32[]{:S(2)}) collective-permute-start(bf16[128,4096]{1,0:T(8,128)(2,1)S(1)} %broadcast_select_fusion.5), channel_id=1, source_target_pairs={{12,8},{0,4},{13,9},{1,5},{14,10},{2,6},{15,11},{3,7},{28,24},{16,... | collective-permute-start | bytes 3145736 | tf_op jit(solution)/shard_map/ppermute | solution.py:435
  113.8 45.0 %collective-permute-start.20 = (bf16[128,4096]{1,0:T(8,128)(2,1)S(1)}, bf16[128,4096]{1,0:T(8,128)(2,1)S(1)}, u32[]{:S(2)}, u32[]{:S(2)}) collective-permute-start(bf16[128,4096]{1,0:T(8,128)(2,1)S(1)} %collective-permute-done.15.refs_0_.refs_4_.refs_2_.refs_6_), channel_id=1, source_target_pairs={{0,4},{4,8},{8,12},{12,0},{1,5},{5,9},{9,13},{13,1},{2,6},{6,10},{... | collective-permute-start | bytes 3145736 | tf_op jit(solution)/shard_map/ppermute | solution.py:361
  136.2 42.2 %collective-permute-start.19 = (bf16[128,4096]{1,0:T(8,128)(2,1)S(1)}, bf16[128,4096]{1,0:T(8,128)(2,1)S(1)}, u32[]{:S(2)}, u32[]{:S(2)}) collective-permute-start(bf16[128,4096]{1,0:T(8,128)(2,1)S(1)} %add_convert_fusion.2), channel_id=1, source_target_pairs={{0,4},{4,8},{1,5},{5,9},{2,6},{6,10},{3,7},{7,11},{16,20},{20,24},... | collective-permute-start | bytes 3145736 | tf_op jit(solution)/shard_map/ppermute | solution.py:439
  139.3 39.1 %collective-permute-start.18 = (bf16[128,4096]{1,0:T(8,128)(2,1)S(1)}, bf16[128,4096]{1,0:T(8,128)(2,1)S(1)}, u32[]{:S(2)}, u32[]{:S(2)}) collective-permute-start(bf16[128,4096]{1,0:T(8,128)(2,1)S(1)} %add_convert_fusion.2), channel_id=1, source_target_pairs={{8,4},{12,8},{9,5},{13,9},{10,6},{14,10},{11,7},{15,11},{24,20},{2... | collective-permute-start | bytes 3145736 | tf_op jit(solution)/shard_map/ppermute | solution.py:438
  140.2 33.5 %collective-permute-start.16 = (bf16[1024,512]{1,0:T(8,128)(2,1)S(1)}, bf16[1024,512]{1,0:T(8,128)(2,1)S(1)}, u32[]{:S(2)}, u32[]{:S(2)}) collective-permute-start(bf16[1024,512]{1,0:T(8,128)(2,1)S(1)} %broadcast_select_fusion.6.refs_2_), channel_id=1, source_target_pairs={{0,16},{16,0},{1,17},{17,1},{2,18},{18,2},{3,19},{19,3},{4,20},{20... | collective-permute-start | bytes 3145736 | tf_op jit(solution)/shard_map/ppermute | solution.py:420
  141.9 36.5 %collective-permute-start.17 = (bf16[1024,512]{1,0:T(8,128)(2,1)S(1)}, bf16[1024,512]{1,0:T(8,128)(2,1)S(1)}, u32[]{:S(2)}, u32[]{:S(2)}) collective-permute-start(bf16[1024,512]{1,0:T(8,128)(2,1)S(1)} %broadcast_select_fusion.4), channel_id=1, source_target_pairs={{8,12},{4,0},{9,13},{5,1},{10,14},{6,2},{11,15},{7,3},{24,28},{20,... | collective-permute-start | bytes 3145736 | tf_op jit(solution)/shard_map/ppermute | solution.py:47
  178.4 12.7 %collective-permute-start.23 = (bf16[512,3328]{1,0:T(8,128)(2,1)S(1)}, bf16[512,3328]{1,0:T(8,128)(2,1)S(1)}, u32[]{:S(2)}, u32[]{:S(2)}) collective-permute-start(bf16[512,3328]{1,0:T(8,128)(2,1)S(1)} %shard_map.106), channel_id=1, source_target_pairs={{0,1},{1,0},{2,3},{3,2},{4,5},{5,4},{6,7},{7,6},{8,9},{9,8},{10,11... | collective-permute-start | bytes 10223624 | tf_op jit(solution)/shard_map/ppermute | solution.py:469
  184.2 30.2 %collective-permute-start.22 = (bf16[1024,512]{1,0:T(8,128)(2,1)S(1)}, bf16[1024,512]{1,0:T(8,128)(2,1)}, u32[]{:S(2)}, u32[]{:S(2)}) collective-permute-start(bf16[1024,512]{1,0:T(8,128)(2,1)S(1)} %select_select_fusion.refs_3_), channel_id=1, source_target_pairs={{0,16},{16,0},{1,17},{17,1},{2,18},{18,2},{3,19},{19,3},{4,20},{20... | collective-permute-start | bytes 3145736 | tf_op jit(solution)/shard_map/ppermute | solution.py:420
  185.7 41.3 %collective-permute-start.25 = (bf16[128,5120]{1,0:T(8,128)(2,1)}, bf16[128,5120]{1,0:T(8,128)(2,1)}, u32[]{:S(2)}, u32[]{:S(2)}) collective-permute-start(bf16[128,5120]{1,0:T(8,128)(2,1)} %pad_maximum_fusion.3), channel_id=1, source_target_pairs={{0,4},{4,8},{8,12},{1,5},{5,9},{9,13},{2,6},{6,10},{10,14},{3,7},{... | collective-permute-start | bytes 3932168 | tf_op jit(solution)/shard_map/ppermute | solution.py:439
  189.1 37.9 %collective-permute-start.24 = (bf16[128,5120]{1,0:T(8,128)(2,1)}, bf16[128,5120]{1,0:T(8,128)(2,1)}, u32[]{:S(2)}, u32[]{:S(2)}) collective-permute-start(bf16[128,5120]{1,0:T(8,128)(2,1)} %pad_maximum_fusion.2), channel_id=1, source_target_pairs={{4,0},{8,4},{12,8},{5,1},{9,5},{13,9},{6,2},{10,6},{14,10},{7,3},{... | collective-permute-start | bytes 3932168 | tf_op jit(solution)/shard_map/ppermute | solution.py:438
  191.1 46.7 %collective-permute-start.27 = (bf16[128,1024]{1,0:T(8,128)(2,1)S(1)}, bf16[128,1024]{1,0:T(8,128)(2,1)}, u32[]{:S(2)}, u32[]{:S(2)}) collective-permute-start(bf16[128,1024]{1,0:T(8,128)(2,1)S(1)} %get-tuple-element.71), channel_id=1, source_target_pairs={{0,8},{4,12},{8,0},{12,4},{1,9},{5,13},{9,1},{13,5},{2,10},{6,14},... | collective-permute-start | bytes 786440 | tf_op jit(solution)/shard_map/ppermute | solution.py:506
  192.9 44.9 %collective-permute-start.26 = (bf16[128,1024]{1,0:T(8,128)(2,1)}, bf16[128,1024]{1,0:T(8,128)(2,1)}, u32[]{:S(2)}, u32[]{:S(2)}) collective-permute-start(bf16[128,1024]{1,0:T(8,128)(2,1)} %broadcast_select_fusion.8), channel_id=1, source_target_pairs={{0,12},{12,0},{1,13},{13,1},{2,14},{14,2},{3,15},{15,3},{16,28},{2... | collective-permute-start | bytes 786440 | tf_op jit(solution)/shard_map/ppermute | solution.py:506
  (25 other events, 376.0 us)

commit v5 on v4

--- a/solution.py
+++ b/solution.py
@@ -352,8 +352,7 @@
 
     g_cores = over_cores(output_gradient)
     count_cores = over_cores(counts[0])
-    soon = [*g_cores[1:], *count_cores[1:]]
-    x_cores = over_cores(after(activations, *soon))
+    x_cores = over_cores(activations)
     factors = [factor_down.reshape(own_rows, features)]
 
     def factor_on(*earlier):
@@ -364,7 +363,18 @@
     up_line = [up_here] + [
         lax.ppermute(up_here, "fsdp", [(i, (i + far) % n) for i in range(n)]) for far in range(1, n)
     ]
-    factor_on(*soon)
+
+    if lax.axis_size("tp") == 2:
+        tp_other = lax.ppermute(output_gradient, "tp", around("tp"))
+        first = lax.axis_index("tp") == 0
+
+        def whole_grad(one, two):
+            return jnp.concatenate([jnp.where(first, one, two), jnp.where(first, two, one)], axis=1)
+    else:
+        tp_other = lax.all_gather(output_gradient, "tp", axis=1, tiled=True)
+
+        def whole_grad(one, two):
+            return two
 
     hot = owners[:, None] == lax.broadcasted_iota(jnp.int32, (slots, slots), 1)
     bounds = []
@@ -390,27 +400,16 @@
         base_weight.reshape(copies, part_rows, width), sub * groups + y, 0, keepdims=False
     )
     w_up, w_down = [weight_here], [weight_here]
-    came = event(*up_line[1:], weight_here)
+    came = event(*up_line[1:], *g_cores[1:], *x_cores[1:], *along_line, weight_here, tp_other)
 
     line_on(w_up, w_down, 1, came)
-    if lax.axis_size("tp") == 2:
-        tp_other = lax.ppermute(after(output_gradient, came), "tp", around("tp"))
-        first = lax.axis_index("tp") == 0
-
-        def whole_grad(one, two):
-            return jnp.concatenate([jnp.where(first, one, two), jnp.where(first, two, one)], axis=1)
-    else:
-        tp_other = lax.all_gather(output_gradient, "tp", axis=1, tiled=True)
-
-        def whole_grad(one, two):
-            return two
-
+    factor_on(came)
     low_back = low_rank([after(g_cores[0], came), *g_cores[1:]], up_line, *along_line, rank)
     low_back = sum_over_tp(adapter_scale_factor * low_back)
     down_blocks = outer(low_back, *along_line, x_cores, 1.0, n)
-    came = event(factors[-1], *x_cores[1:], cost=LONG)
+    came = event(factors[-1], cost=LONG)
     factor_on(came)
-    came = event(w_up[1], w_down[1], tp_other)
+    came = event(w_up[1], w_down[1])
 
     weight_arrivals, whose = [], [z] + [arrival_owner(step) for step in range(1, n)]
 
@@ -478,42 +477,12 @@
         low_back_all = low_back_all + theirs.astype(F32)
     grads = [whole_grad(one, two) for one, two in zip(g_cores, tp_cores, strict=True)]
     wides = spread_out(
-        low_back_all, *ranges([((z - j) % n, (sub - b) % subs) for b in both for j in range(n)])
-    )
-
-    up_pieces = outer(low_in, *along_line, g_cores, adapter_scale_factor, n)
-    if n > 2:
-        lower, upper = to_sum(n - 1)
-        lower = jnp.concatenate([lower, up_pieces[1]], axis=1)
-        upper = jnp.concatenate([upper, up_pieces[n - 1]], axis=1)
-
-    up_total, round_4 = up_pieces[0], []
-    if n > 2:
-        from_above, from_below = sum_on(n - 1, lower, upper, came)
-        weight_arrives(n - 1, came)
-        round_4 += [from_above, from_below]
-        up_total = up_total + from_above[:, features:].astype(F32) + from_below[:, features:].astype(F32)
-        from_above, from_below = from_above[:, :features], from_below[:, :features]
-    for far in range(1, n):
-        pairs = [(i, (i - far) % n) for i in range(n)]
-        if n > 2 and far == 1:
-            far_piece = jnp.where(z == 0, up_pieces[1], up_pieces[n - 1])
-            pairs = [(0, n - 1), (n - 1, 0)]
-        elif n > 2 and far == n - 1:
-            continue
-        else:
-            far_piece = up_pieces[far]
-        got = lax.ppermute(
-            after(far_piece, came, *[one[0] for one in traded[1:]]), "fsdp", pairs
-        )
-        up_total = up_total + got.astype(F32)
-        round_4.append(got)
-    up_total = up_total + came[0, 0]
-    grad_down = down_blocks[0] + from_above.astype(F32) + from_below.astype(F32)
-    input_gradient, others = None, []
-    for a in range(groups):
+        low_back_all + came[:1], *ranges([((z - j) % n, (sub - b) % subs) for b in both for j in range(n)])
+    )
+
+    def ig(a, so_far, others):
         inner = (y - a) % groups
-        input_gradient, *for_others = input_gradient_part(
+        so_far, *for_others = input_gradient_part(
             sub * groups + inner,
             inner,
             whose,
@@ -523,11 +492,36 @@
             wides,
             factors,
             [one[0] for one in traded[1:]],
-            input_gradient,
+            so_far,
         )
-        others.append(for_others)
-
-    round_4.append(input_gradient)
+        return so_far, [*others, for_others]
+
+    if n > 2:
+        from_above, from_below = sum_on(n - 1, *to_sum(n - 1), came)
+        weight_arrives(n - 1, came)
+    grad_down = down_blocks[0] + from_above.astype(F32) + from_below.astype(F32)
+
+    bits = n.bit_length() - 1
+    turned = [sum(((place >> k) & 1) << (bits - 1 - k) for k in range(bits)) for place in range(n)]
+    up_total, there = outer(
+        low_in, *ranges([(z ^ place, sub) for place in turned]), g_cores, adapter_scale_factor, 2
+    )
+    input_gradient, others, last = None, [], [came]
+    for bit in range(bits):
+        if bit:
+            there = up_total[up_total.shape[0] // 2 :].astype(BF16)
+            up_total = up_total[: up_total.shape[0] // 2]
+        if bit == 1:
+            last += [from_above, from_below, *weight_arrivals[-1][1:]]
+        got = lax.ppermute(after(there, *last), "fsdp", [(i, i ^ (1 << bit)) for i in range(n)])
+        up_total = up_total + got.astype(F32)
+        if not bit:
+            input_gradient, others = ig(0, None, others)
+            last = [came, input_gradient]
+    for a in range(1, groups):
+        input_gradient, others = ig(a, input_gradient, others)
+
+    round_4 = [from_above, from_below, got, input_gradient]
     for a in range(groups):
         for b, one in enumerate(others[a], 1):
             got = lax.ppermute(

time: 247 us -> 239 us (0.968)
  starting transfers between devices: 50.7 us -> 41.9 us
  other arithmetic: 15.4 us -> 12.7 us
    ppermute x3, waiting for transfers between devices: 23.6 us -> 7.28 us  [the longest x2 7.28 us: local(): lax.ppermute(after(there, *last), 'fsdp', [(i, i ^ 1 << bit) for i in ran...]
    ppermute x2, waiting for transfers between devices: 3.3 us -> 19.1 us  [line_step(): lax.ppermute(up, 'fsdp', [(i, i + 1) for i in range(step - 1, count - 1)])]
    ppermute x2, waiting for transfers between devices: 0.01 us -> 5.63 us  [sum_on(): lax.ppermute(upper, 'fsdp', [(i, i + 1) for i in range(step)])]
    ppermute x3, waiting for transfers between devices: 34.5 us -> 29.1 us  [factor_on(): lax.ppermute(after(factors[-1], *earlier), 'fsdp', around('fsdp'))]
    ppermute x3, starting transfers between devices: 8.62 us -> 4.13 us  [the longest x1 2.91 us: local(): tp_other = lax.ppermute(output_gradient, 'tp', around('tp'))]
    ppermute x1, starting transfers between devices: 7.02 us -> 2.57 us  [sum_on(): got = lax.ppermute(lower, 'fsdp', [(n - 1, n - 2), (0, 1)])]
    ppermute x2, waiting for transfers between devices: 5.83 us -> 10.1 us  [sum_over_tp(): lax.ppermute(part.astype(BF16), 'tp', around('tp')).astype(F32)]
    ppermute x3, waiting for transfers between devices: 15.7 us -> 11.8 us  [local(): lax.ppermute(up_here, 'fsdp', [(i, (i + far) % n) for i in range(n)])]
  transfers between devices with their start and end apart: 30 -> 30, of which waited for: 13 -> 18; matrix products, arithmetic and copies ran while one was open for 9% -> 8% of each run, Pallas kernels for 23% -> 24%
where the time goes in v5:
time: 239 us; the launch traced here: 238 us
  waiting for transfers between devices  114 us (48%)
  Pallas kernels  56.3 us (24%)
  starting transfers between devices  41.9 us (18%)
  other arithmetic  12.7 us (5%)
  local copies, waits for them, and re-layouts  11.5 us (5%)
    ppermute x3, waiting for transfers between devices, factor_on(): lax.ppermute(after(factors[-1], *earlier), 'fsdp', around('fsdp'))  29.1 us
    pallas_call x2, Pallas kernels, input_gradient_part(): pl.pallas_call(functools.partial(input_gradient_kernel, sources, shards,...  24.9 us
    pallas_call x3, Pallas kernels, low_rank(): pl.pallas_call(functools.partial(low_kernel, len(xs), len(blocks), rank,...  19.6 us
    ppermute x1, waiting for transfers between devices, sum_on(): got = lax.ppermute(lower, 'fsdp', [(n - 1, n - 2), (0, 1)])  19.1 us
    ppermute x2, waiting for transfers between devices, line_step(): lax.ppermute(up, 'fsdp', [(i, i + 1) for i in range(step - 1, count - 1)])  19.1 us
    ppermute x3, waiting for transfers between devices, local(): lax.ppermute(up_here, 'fsdp', [(i, (i + far) % n) for i in range(n)])  11.8 us
    pallas_call x2, Pallas kernels, outer(): pl.pallas_call(functools.partial(outer_kernel, scale, parts), grid=(featu...  10.8 us
    ppermute x2, waiting for transfers between devices, sum_over_tp(): lax.ppermute(part.astype(BF16), 'tp', around('tp')).astype(F32)  10.1 us
  transfers between devices with their start and end apart: 30, of which 18 were waited for; matrix products, arithmetic and copies ran while one was open for 8% of the time, Pallas kernels for 24%

profile of v5, /device:TPU:0, one launch (start us, length us, event | category | flops | bytes accessed | tf_op | source)
XLA Modules:
  0.0 237.9 jit_solution(17961161846232364553)
XLA Ops:
  1.3 2.9 %collective-permute-start.6 = (bf16[512,1024]{1,0:T(8,128)(2,1)}, bf16[512,1024]{1,0:T(8,128)(2,1)S(1)}, u32[]{:S(2)}, u32[]{:S(2)}) collective-permute-start(bf16[512,1024]{1,0:T(8,128)(2,1)} %refs_0_.11), channel_id=1, source_target_pairs={{0,2},{2,0},{1,3},{3,1},{4,6},{6,4},{5,7},{7,5},{8,10},{10,8},{9,1... | collective-permute-start | bytes 3145736 | tf_op jit(solution)/shard_map/ppermute | solution.py:368
  10.7 2.6 %collective-permute-start.1 = (bf16[128,1024]{1,0:T(8,128)(2,1)}, bf16[128,1024]{1,0:T(8,128)(2,1)}, u32[]{:S(2)}, u32[]{:S(2)}) collective-permute-start(bf16[128,1024]{1,0:T(8,128)(2,1)} %bitcast.8.refs_2_), channel_id=1, source_target_pairs={{0,8},{4,12},{8,0},{12,4},{1,9},{5,13},{9,1},{13,5},{2,10},{6,14},... | collective-permute-start | bytes 786440 | tf_op jit(solution)/shard_map/ppermute | solution.py:364
  16.9 9.9 %collective-permute-done.1.refs_1_.refs_4_ = bf16[128,1024]{1,0:T(8,128)(2,1)} collective-permute-done((bf16[128,1024]{1,0:T(8,128)(2,1)}, bf16[128,1024]{1,0:T(8,128)(2,1)}, u32[]{:S(2)}, u32[]{:S(2)}) %collective-permute-start.1) | collective-permute-done | bytes 262176 | tf_op jit(solution)/shard_map/ppermute | solution.py:364
  29.9 4.6 %collective-permute-start.9 = (bf16[128,4096]{1,0:T(8,128)(2,1)S(1)}, bf16[128,4096]{1,0:T(8,128)(2,1)S(1)}, u32[]{:S(2)}, u32[]{:S(2)}) collective-permute-start(bf16[128,4096]{1,0:T(8,128)(2,1)S(1)} %bitcast.40), channel_id=1, source_target_pairs={{0,4},{4,8},{8,12},{12,0},{1,5},{5,9},{9,13},{13,1},{2,6},{6,10},{... | collective-permute-start | bytes 3145736 | tf_op jit(solution)/shard_map/ppermute | solution.py:360
  34.7 3.0 %shard_map.97 = f32[1024,128]{1,0:T(8,128)S(1)} custom-call(bf16[512,1024]{1,0:T(8,128)(2,1)S(1)} %copy-done.9, bf16[512,1024]{1,0:T(8,128)(2,1)S(1)} %collective-permute-done.3.refs_3_.refs_1_, bf16[128,1024]{1,0:T(8,128)(2,1)} %bitcast.8.refs_2_, bf16[128,1024]{1,0:T(8,128)(2,1)S(1)} %collective-permute-done.refs_0_.refs_3_, ...), custom_call_target="tpu_custom_call" | custom-call | flops 1 | bytes 1 | tf_op jit(solution)/shard_map/pallas_call | solution.py:161
  41.3 4.4 %collective-permute-done.13 = bf16[1024,128]{1,0:T(8,128)(2,1)S(1)} collective-permute-done((bf16[1024,128]{1,0:T(8,128)(2,1)S(1)}, bf16[1024,128]{1,0:T(8,128)(2,1)S(1)}, u32[]{:S(2)}, u32[]{:S(2)}) %collective-permute-start.13) | collective-permute-done | bytes 262176 | tf_op jit(solution)/shard_map/ppermute | solution.py:89
  47.2 8.7 %shard_map.98 = (f32[128,4096]{1,0:T(8,128)S(1)}, bf16[128,4096]{1,0:T(8,128)(2,1)S(1)}, bf16[128,4096]{1,0:T(8,128)(2,1)S(1)}, bf16[128,4096]{1,0:T(8,128)(2,1)S(1)}) custom-call(f32[1024,128]{1,0:T(8,128)S(1)} %convert_add_fusion.3.low.refs_5_, s32[2,512]{1,0:T(2,128)S(1)} %pad_add_fusion.2.refs_5_.refs_6_.start, ...), custom_call_target="tpu_custom_call" | custom-call | flops 1 | bytes 1 | tf_op jit(solution)/shard_map/pallas_call | solution.py:222
  55.9 5.4 %collective-permute-done.9.refs_0_.refs_3_.refs_1_.refs_5_ = bf16[128,4096]{1,0:T(8,128)(2,1)S(1)} collective-permute-done((bf16[128,4096]{1,0:T(8,128)(2,1)S(1)}, bf16[128,4096]{1,0:T(8,128)(2,1)S(1)}, u32[]{:S(2)}, u32[]{:S(2)}) %collective-permute-start.9) | collective-permute-done | bytes 1048608 | tf_op jit(solution)/shard_map/ppermute | solution.py:360
  61.4 19.1 %collective-permute-done.7.refs_0_ = bf16[1024,512]{1,0:T(8,128)(2,1)S(1)} collective-permute-done((bf16[1024,512]{1,0:T(8,128)(2,1)S(1)}, bf16[1024,512]{1,0:T(8,128)(2,1)S(1)}, u32[]{:S(2)}, u32[]{:S(2)}) %collective-permute-start.7) | collective-permute-done | bytes 1048608 | tf_op jit(solution)/shard_map/ppermute | solution.py:52
  80.5 3.1 %collective-permute-done.8.refs_1_ = bf16[1024,512]{1,0:T(8,128)(2,1)S(1)} collective-permute-done((bf16[1024,512]{1,0:T(8,128)(2,1)S(1)}, bf16[1024,512]{1,0:T(8,128)(2,1)S(1)}, u32[]{:S(2)}, u32[]{:S(2)}) %collective-permute-start.8) | collective-permute-done | bytes 1048608 | tf_op jit(solution)/shard_map/ppermute | solution.py:53
  90.0 16.3 %collective-permute-done.15.refs_0_.refs_4_.refs_2_.refs_6_ = bf16[128,4096]{1,0:T(8,128)(2,1)S(1)} collective-permute-done((bf16[128,4096]{1,0:T(8,128)(2,1)S(1)}, bf16[128,4096]{1,0:T(8,128)(2,1)S(1)}, u32[]{:S(2)}, u32[]{:S(2)}) %collective-permute-start.15) | collective-permute-done | bytes 1048608 | tf_op jit(solution)/shard_map/ppermute | solution.py:360
  106.3 19.1 %collective-permute-done.14.refs_2_.refs_3_ = bf16[128,4096]{1,0:T(8,128)(2,1)S(1)} collective-permute-done((bf16[128,4096]{1,0:T(8,128)(2,1)S(1)}, bf16[128,4096]{1,0:T(8,128)(2,1)S(1)}, u32[]{:S(2)}, u32[]{:S(2)}) %collective-permute-start.14) | collective-permute-done | bytes 1048608 | tf_op jit(solution)/shard_map/ppermute | solution.py:434
  125.7 3.1 %collective-permute-done.12.refs_1_ = bf16[1024,512]{1,0:T(8,128)(2,1)S(1)} collective-permute-done((bf16[1024,512]{1,0:T(8,128)(2,1)S(1)}, bf16[1024,512]{1,0:T(8,128)(2,1)S(1)}, u32[]{:S(2)}, u32[]{:S(2)}) %collective-permute-start.12) | collective-permute-done | bytes 1048608 | tf_op jit(solution)/shard_map/ppermute | solution.py:53
  135.3 8.6 %shard_map.101.refs_5_ = f32[1024,128]{1,0:T(8,128)S(1)} custom-call(bf16[512,4096]{1,0:T(8,128)(2,1)S(1)} %copy-done, bf16[512,4096]{1,0:T(8,128)(2,1)} %collective-permute-done.4.refs_4_.refs_1_, bf16[128,4096]{1,0:T(8,128)(2,1)S(1)} %bitcast.41, bf16[128,4096]{1,0:T(8,128)(2,1)S(1)} %collective-permute-done.9.refs_0_.refs_3_.refs_1_.refs_5_, ...), custom_call_target="tpu_custom_call" | custom-call | flops 1 | bytes 1 | tf_op jit(solution)/shard_map/pallas_call | solution.py:161
  143.9 7.4 %collective-permute-done.20.refs_2_.refs_0_.refs_3_.refs_7_ = bf16[128,4096]{1,0:T(8,128)(2,1)S(1)} collective-permute-done((bf16[128,4096]{1,0:T(8,128)(2,1)S(1)}, bf16[128,4096]{1,0:T(8,128)(2,1)S(1)}, u32[]{:S(2)}, u32[]{:S(2)}) %collective-permute-start.20) | collective-permute-done | bytes 1048608 | tf_op jit(solution)/shard_map/ppermute | solution.py:360
  151.3 8.0 %shard_map.102 = f32[1024,128]{1,0:T(8,128)S(1)} custom-call(bf16[512,4096]{1,0:T(8,128)(2,1)S(1)} %copy-done, bf16[512,4096]{1,0:T(8,128)(2,1)} %collective-permute-done.4.refs_4_.refs_1_, bf16[128,4096]{1,0:T(8,128)(2,1)S(1)} %collective-permute-done.20.refs_2_.refs_0_.refs_3_.refs_7_, s32[2,128]{1,0:T(2,128)S(1)} %get-tuple-element.109.refs_3_, ...), custom_call_target="tpu_custom_call" | custom-call | flops 1 | bytes 1 | tf_op jit(solution)/shard_map/pallas_call | solution.py:161
  160.9 5.7 %collective-permute-done.21 = bf16[1024,128]{1,0:T(8,128)(2,1)S(1)} collective-permute-done((bf16[1024,128]{1,0:T(8,128)(2,1)S(1)}, bf16[1024,128]{1,0:T(8,128)(2,1)S(1)}, u32[]{:S(2)}, u32[]{:S(2)}) %collective-permute-start.21) | collective-permute-done | bytes 262176 | tf_op jit(solution)/shard_map/ppermute | solution.py:89
  169.5 3.8 %collective-permute-done.17.refs_0_.refs_1_ = bf16[1024,512]{1,0:T(8,128)(2,1)S(1)} collective-permute-done((bf16[1024,512]{1,0:T(8,128)(2,1)S(1)}, bf16[1024,512]{1,0:T(8,128)(2,1)S(1)}, u32[]{:S(2)}, u32[]{:S(2)}) %collective-permute-start.17) | collective-permute-done | bytes 1048608 | tf_op jit(solution)/shard_map/ppermute | solution.py:47
  180.5 4.4 %collective-permute-start.25 = (bf16[128,4096]{1,0:T(8,128)(2,1)}, bf16[128,4096]{1,0:T(8,128)(2,1)}, u32[]{:S(2)}, u32[]{:S(2)}) collective-permute-start(bf16[128,4096]{1,0:T(8,128)(2,1)} %add_convert_fusion), channel_id=1, source_target_pairs={{0,4},{4,8},{8,12},{1,5},{5,9},{9,13},{2,6},{6,10},{10,14},{3,7},{... | collective-permute-start | bytes 3145736 | tf_op jit(solution)/shard_map/ppermute | solution.py:438
  188.0 6.4 %collective-permute-done.26 = bf16[256,1024]{1,0:T(8,128)(2,1)S(1)} collective-permute-done((bf16[256,1024]{1,0:T(8,128)(2,1)S(1)}, bf16[256,1024]{1,0:T(8,128)(2,1)S(1)}, u32[]{:S(2)}, u32[]{:S(2)}) %collective-permute-start.26) | collective-permute-done | bytes 524320 | tf_op jit(solution)/shard_map/ppermute | solution.py:516
  199.1 12.4 %shard_map.108 = (bf16[512,4096]{1,0:T(8,128)(2,1)}, bf16[512,1024]{1,0:T(8,128)(2,1)}) custom-call(s32[6]{0:T(128)} %stack.157._, bf16[4096,512]{1,0:T(8,128)(2,1)} %refs_0_.10, bf16[1024,512]{1,0:T(8,128)(2,1)} %copy-done.20, bf16[1024,512]{1,0:T(8,128)(2,1)} %copy-done.21, bf16[1024,512]{1,0:T(8,128)(2,1)} %copy-done.19, bf16[128,4096]{1,0:T(8,128)(2,1)} %bitcast.38, ...), custom_call_target="tpu_custom_call" | custom-call | flops 1 | bytes 1 | tf_op jit(solution)/shard_map/pallas_call | solution.py:309
  211.5 3.1 %collective-permute-done.25 = bf16[128,4096]{1,0:T(8,128)(2,1)} collective-permute-done((bf16[128,4096]{1,0:T(8,128)(2,1)}, bf16[128,4096]{1,0:T(8,128)(2,1)}, u32[]{:S(2)}, u32[]{:S(2)}) %collective-permute-start.25) | collective-permute-done | bytes 1048608 | tf_op jit(solution)/shard_map/ppermute | solution.py:438
  217.8 12.6 %shard_map.109 = (bf16[512,4096]{1,0:T(8,128)(2,1)}, bf16[512,1024]{1,0:T(8,128)(2,1)}) custom-call(s32[6]{0:T(128)} %stack.130._, bf16[4096,512]{1,0:T(8,128)(2,1)} %refs_0_.10, bf16[1024,512]{1,0:T(8,128)(2,1)} %copy-done.10, bf16[1024,512]{1,0:T(8,128)(2,1)} %copy-done.11, ...), custom_call_target="tpu_custom_call", output_to_operand_aliasing={{0}: (20, {})} | custom-call | flops 1 | bytes 1 | tf_op jit(solution)/shard_map/pallas_call | solution.py:309
  231.7 3.2 %convert_add_fusion = f32[128,4096]{1,0:T(8,128)} fusion(bf16[128,4096]{1,0:T(8,128)(2,1)} %collective-permute-done.25, f32[128,4096]{1,0:T(8,128)S(1)} %copy-done.17, bf16[128,4096]{1,0:T(8,128)(2,1)} %collective-permute-done.24), kind=kLoop, calls=%fused_computation.2 | loop fusion | flops 2097152 | bytes 6291456 | tf_op jit(solution)/shard_map/add | solution.py:502
  (181 shorter events, 58.7 us)
Async XLA Ops:
  0.7 27.3 %collective-permute-start.4 = (bf16[512,4096]{1,0:T(8,128)(2,1)}, bf16[512,4096]{1,0:T(8,128)(2,1)}, u32[]{:S(2)}, u32[]{:S(2)}) collective-permute-start(bf16[512,4096]{1,0:T(8,128)(2,1)} %refs_0_.8), channel_id=1, source_target_pairs={{0,1},{1,0},{2,3},{3,2},{4,5},{5,4},{6,7},{7,6},{8,9},{9,8},{10,11... | collective-permute-start | bytes 12582920 | tf_op jit(solution)/shard_map/ppermute | solution.py:96
  1.2 26.7 %collective-permute-start.3 = (bf16[512,1024]{1,0:T(8,128)(2,1)}, bf16[512,1024]{1,0:T(8,128)(2,1)S(1)}, u32[]{:S(2)}, u32[]{:S(2)}) collective-permute-start(bf16[512,1024]{1,0:T(8,128)(2,1)} %refs_0_.11), channel_id=1, source_target_pairs={{0,1},{1,0},{2,3},{3,2},{4,5},{5,4},{6,7},{7,6},{8,9},{9,8},{10,11... | collective-permute-start | bytes 3145736 | tf_op jit(solution)/shard_map/ppermute | solution.py:96
  1.3 26.6 %collective-permute-start.6 = (bf16[512,1024]{1,0:T(8,128)(2,1)}, bf16[512,1024]{1,0:T(8,128)(2,1)S(1)}, u32[]{:S(2)}, u32[]{:S(2)}) collective-permute-start(bf16[512,1024]{1,0:T(8,128)(2,1)} %refs_0_.11), channel_id=1, source_target_pairs={{0,2},{2,0},{1,3},{3,1},{4,6},{6,4},{5,7},{7,5},{8,10},{10,8},{9,1... | collective-permute-start | bytes 3145736 | tf_op jit(solution)/shard_map/ppermute | solution.py:368
  10.7 16.0 %collective-permute-start.1 = (bf16[128,1024]{1,0:T(8,128)(2,1)}, bf16[128,1024]{1,0:T(8,128)(2,1)}, u32[]{:S(2)}, u32[]{:S(2)}) collective-permute-start(bf16[128,1024]{1,0:T(8,128)(2,1)} %bitcast.8.refs_2_), channel_id=1, source_target_pairs={{0,8},{4,12},{8,0},{12,4},{1,9},{5,13},{9,1},{13,5},{2,10},{6,14},... | collective-permute-start | bytes 786440 | tf_op jit(solution)/shard_map/ppermute | solution.py:364
  15.0 12.9 %collective-permute-start.2 = (bf16[128,1024]{1,0:T(8,128)(2,1)}, bf16[128,1024]{1,0:T(8,128)(2,1)S(1)}, u32[]{:S(2)}, u32[]{:S(2)}) collective-permute-start(bf16[128,1024]{1,0:T(8,128)(2,1)} %bitcast.8.refs_2_), channel_id=1, source_target_pairs={{0,12},{4,0},{8,4},{12,8},{1,13},{5,1},{9,5},{13,9},{2,14},{6,2},{... | collective-permute-start | bytes 786440 | tf_op jit(solution)/shard_map/ppermute | solution.py:364
  29.9 31.4 %collective-permute-start.9 = (bf16[128,4096]{1,0:T(8,128)(2,1)S(1)}, bf16[128,4096]{1,0:T(8,128)(2,1)S(1)}, u32[]{:S(2)}, u32[]{:S(2)}) collective-permute-start(bf16[128,4096]{1,0:T(8,128)(2,1)S(1)} %bitcast.40), channel_id=1, source_target_pairs={{0,4},{4,8},{8,12},{12,0},{1,5},{5,9},{9,13},{13,1},{2,6},{6,10},{... | collective-permute-start | bytes 3145736 | tf_op jit(solution)/shard_map/ppermute | solution.py:360
  39.3 41.2 %collective-permute-start.7 = (bf16[1024,512]{1,0:T(8,128)(2,1)S(1)}, bf16[1024,512]{1,0:T(8,128)(2,1)S(1)}, u32[]{:S(2)}, u32[]{:S(2)}) collective-permute-start(bf16[1024,512]{1,0:T(8,128)(2,1)S(1)} %copy-done.15), channel_id=1, source_target_pairs={{0,4},{4,8},{8,12},{1,5},{5,9},{9,13},{2,6},{6,10},{10,14},{3,7},{... | collective-permute-start | bytes 3145736 | tf_op jit(solution)/shard_map/ppermute | solution.py:52
  45.8 37.8 %collective-permute-start.8 = (bf16[1024,512]{1,0:T(8,128)(2,1)S(1)}, bf16[1024,512]{1,0:T(8,128)(2,1)S(1)}, u32[]{:S(2)}, u32[]{:S(2)}) collective-permute-start(bf16[1024,512]{1,0:T(8,128)(2,1)S(1)} %copy-done.15), channel_id=1, source_target_pairs={{4,0},{8,4},{12,8},{5,1},{9,5},{13,9},{6,2},{10,6},{14,10},{7,3},{... | collective-permute-start | bytes 3145736 | tf_op jit(solution)/shard_map/ppermute | solution.py:53
  61.3 45.0 %collective-permute-start.15 = (bf16[128,4096]{1,0:T(8,128)(2,1)S(1)}, bf16[128,4096]{1,0:T(8,128)(2,1)S(1)}, u32[]{:S(2)}, u32[]{:S(2)}) collective-permute-start(bf16[128,4096]{1,0:T(8,128)(2,1)S(1)} %collective-permute-done.9.refs_0_.refs_3_.refs_1_.refs_5_), channel_id=1, source_target_pairs={{0,4},{4,8},{8,12},{12,0},{1,5},{5,9},{9,13},{13,1},{2,6},{6,10},{... | collective-permute-start | bytes 3145736 | tf_op jit(solution)/shard_map/ppermute | solution.py:360
  83.6 41.8 %collective-permute-start.14 = (bf16[128,4096]{1,0:T(8,128)(2,1)S(1)}, bf16[128,4096]{1,0:T(8,128)(2,1)S(1)}, u32[]{:S(2)}, u32[]{:S(2)}) collective-permute-start(bf16[128,4096]{1,0:T(8,128)(2,1)S(1)} %broadcast_select_fusion.5), channel_id=1, source_target_pairs={{12,8},{0,4},{13,9},{1,5},{14,10},{2,6},{15,11},{3,7},{28,24},{16,... | collective-permute-start | bytes 3145736 | tf_op jit(solution)/shard_map/ppermute | solution.py:434
  86.4 39.3 %collective-permute-start.10 = (bf16[1024,512]{1,0:T(8,128)(2,1)S(1)}, bf16[1024,512]{1,0:T(8,128)(2,1)S(1)}, u32[]{:S(2)}, u32[]{:S(2)}) collective-permute-start(bf16[1024,512]{1,0:T(8,128)(2,1)S(1)} %broadcast_select_fusion.7.refs_1_), channel_id=1, source_target_pairs={{0,16},{16,0},{1,17},{17,1},{2,18},{18,2},{3,19},{19,3},{4,20},{20... | collective-permute-start | bytes 3145736 | tf_op jit(solution)/shard_map/ppermute | solution.py:419
  87.9 40.9 %collective-permute-start.12 = (bf16[1024,512]{1,0:T(8,128)(2,1)S(1)}, bf16[1024,512]{1,0:T(8,128)(2,1)S(1)}, u32[]{:S(2)}, u32[]{:S(2)}) collective-permute-start(bf16[1024,512]{1,0:T(8,128)(2,1)S(1)} %collective-permute-done.8.refs_1_), channel_id=1, source_target_pairs={{4,0},{8,4},{5,1},{9,5},{6,2},{10,6},{7,3},{11,7},{20,16},{24,20},... | collective-permute-start | bytes 3145736 | tf_op jit(solution)/shard_map/ppermute | solution.py:53
  89.2 39.6 %collective-permute-start.11 = (bf16[1024,512]{1,0:T(8,128)(2,1)S(1)}, bf16[1024,512]{1,0:T(8,128)(2,1)S(1)}, u32[]{:S(2)}, u32[]{:S(2)}) collective-permute-start(bf16[1024,512]{1,0:T(8,128)(2,1)S(1)} %collective-permute-done.7.refs_0_), channel_id=1, source_target_pairs={{4,8},{8,12},{5,9},{9,13},{6,10},{10,14},{7,11},{11,15},{20,24},{2... | collective-permute-start | bytes 3145736 | tf_op jit(solution)/shard_map/ppermute | solution.py:52
  106.3 45.0 %collective-permute-start.20 = (bf16[128,4096]{1,0:T(8,128)(2,1)S(1)}, bf16[128,4096]{1,0:T(8,128)(2,1)S(1)}, u32[]{:S(2)}, u32[]{:S(2)}) collective-permute-start(bf16[128,4096]{1,0:T(8,128)(2,1)S(1)} %collective-permute-done.15.refs_0_.refs_4_.refs_2_.refs_6_), channel_id=1, source_target_pairs={{0,4},{4,8},{8,12},{12,0},{1,5},{5,9},{9,13},{13,1},{2,6},{6,10},{... | collective-permute-start | bytes 3145736 | tf_op jit(solution)/shard_map/ppermute | solution.py:360
  128.8 40.6 %collective-permute-start.19 = (bf16[128,4096]{1,0:T(8,128)(2,1)S(1)}, bf16[128,4096]{1,0:T(8,128)(2,1)S(1)}, u32[]{:S(2)}, u32[]{:S(2)}) collective-permute-start(bf16[128,4096]{1,0:T(8,128)(2,1)S(1)} %add_convert_fusion.2), channel_id=1, source_target_pairs={{0,4},{4,8},{1,5},{5,9},{2,6},{6,10},{3,7},{7,11},{16,20},{20,24},... | collective-permute-start | bytes 3145736 | tf_op jit(solution)/shard_map/ppermute | solution.py:438
  131.2 38.3 %collective-permute-start.18 = (bf16[128,4096]{1,0:T(8,128)(2,1)S(1)}, bf16[128,4096]{1,0:T(8,128)(2,1)S(1)}, u32[]{:S(2)}, u32[]{:S(2)}) collective-permute-start(bf16[128,4096]{1,0:T(8,128)(2,1)S(1)} %add_convert_fusion.2), channel_id=1, source_target_pairs={{8,4},{12,8},{9,5},{13,9},{10,6},{14,10},{11,7},{15,11},{24,20},{2... | collective-permute-start | bytes 3145736 | tf_op jit(solution)/shard_map/ppermute | solution.py:437
  132.1 37.4 %collective-permute-start.16 = (bf16[1024,512]{1,0:T(8,128)(2,1)S(1)}, bf16[1024,512]{1,0:T(8,128)(2,1)S(1)}, u32[]{:S(2)}, u32[]{:S(2)}) collective-permute-start(bf16[1024,512]{1,0:T(8,128)(2,1)S(1)} %broadcast_select_fusion.6.refs_2_), channel_id=1, source_target_pairs={{0,16},{16,0},{1,17},{17,1},{2,18},{18,2},{3,19},{19,3},{4,20},{20... | collective-permute-start | bytes 3145736 | tf_op jit(solution)/shard_map/ppermute | solution.py:419
  133.8 39.5 %collective-permute-start.17 = (bf16[1024,512]{1,0:T(8,128)(2,1)S(1)}, bf16[1024,512]{1,0:T(8,128)(2,1)S(1)}, u32[]{:S(2)}, u32[]{:S(2)}) collective-permute-start(bf16[1024,512]{1,0:T(8,128)(2,1)S(1)} %broadcast_select_fusion.4), channel_id=1, source_target_pairs={{8,12},{4,0},{9,13},{5,1},{10,14},{6,2},{11,15},{7,3},{24,28},{20,... | collective-permute-start | bytes 3145736 | tf_op jit(solution)/shard_map/ppermute | solution.py:47
  173.3 21.3 %collective-permute-start.23 = (bf16[512,3328]{1,0:T(8,128)(2,1)S(1)}, bf16[512,3328]{1,0:T(8,128)(2,1)S(1)}, u32[]{:S(2)}, u32[]{:S(2)}) collective-permute-start(bf16[512,3328]{1,0:T(8,128)(2,1)S(1)} %shard_map.106), channel_id=1, source_target_pairs={{0,1},{1,0},{2,3},{3,2},{4,5},{5,4},{6,7},{7,6},{8,9},{9,8},{10,11... | collective-permute-start | bytes 10223624 | tf_op jit(solution)/shard_map/ppermute | solution.py:468
  179.6 14.8 %collective-permute-start.26 = (bf16[256,1024]{1,0:T(8,128)(2,1)S(1)}, bf16[256,1024]{1,0:T(8,128)(2,1)S(1)}, u32[]{:S(2)}, u32[]{:S(2)}) collective-permute-start(bf16[256,1024]{1,0:T(8,128)(2,1)S(1)} %get-tuple-element.65), channel_id=1, source_target_pairs={{0,4},{4,0},{8,12},{12,8},{1,5},{5,1},{9,13},{13,9},{2,6},{6,2},{1... | collective-permute-start | bytes 1572872 | tf_op jit(solution)/shard_map/ppermute | solution.py:516
  180.5 34.1 %collective-permute-start.25 = (bf16[128,4096]{1,0:T(8,128)(2,1)}, bf16[128,4096]{1,0:T(8,128)(2,1)}, u32[]{:S(2)}, u32[]{:S(2)}) collective-permute-start(bf16[128,4096]{1,0:T(8,128)(2,1)} %add_convert_fusion), channel_id=1, source_target_pairs={{0,4},{4,8},{8,12},{1,5},{5,9},{9,13},{2,6},{6,10},{10,14},{3,7},{... | collective-permute-start | bytes 3145736 | tf_op jit(solution)/shard_map/ppermute | solution.py:438
  184.9 31.7 %collective-permute-start.24 = (bf16[128,4096]{1,0:T(8,128)(2,1)}, bf16[128,4096]{1,0:T(8,128)(2,1)}, u32[]{:S(2)}, u32[]{:S(2)}) collective-permute-start(bf16[128,4096]{1,0:T(8,128)(2,1)} %add_convert_fusion.1), channel_id=1, source_target_pairs={{4,0},{8,4},{12,8},{5,1},{9,5},{13,9},{6,2},{10,6},{14,10},{7,3},{... | collective-permute-start | bytes 3145736 | tf_op jit(solution)/shard_map/ppermute | solution.py:437
  186.4 30.2 %collective-permute-start.22 = (bf16[1024,512]{1,0:T(8,128)(2,1)S(1)}, bf16[1024,512]{1,0:T(8,128)(2,1)}, u32[]{:S(2)}, u32[]{:S(2)}) collective-permute-start(bf16[1024,512]{1,0:T(8,128)(2,1)S(1)} %select_select_fusion.refs_3_), channel_id=1, source_target_pairs={{0,16},{16,0},{1,17},{17,1},{2,18},{18,2},{3,19},{19,3},{4,20},{20... | collective-permute-start | bytes 3145736 | tf_op jit(solution)/shard_map/ppermute | solution.py:419
  216.6 14.6 %collective-permute-start.27 = (bf16[128,1024]{1,0:T(8,128)(2,1)}, bf16[128,1024]{1,0:T(8,128)(2,1)S(1)}, u32[]{:S(2)}, u32[]{:S(2)}) collective-permute-start(bf16[128,1024]{1,0:T(8,128)(2,1)} %slice.39), channel_id=1, source_target_pairs={{0,8},{4,12},{8,0},{12,4},{1,9},{5,13},{9,1},{13,5},{2,10},{6,14},... | collective-permute-start | bytes 786440 | tf_op jit(solution)/shard_map/ppermute | solution.py:516
  (31 other events, 408.4 us)

commit v6 on v5

--- a/solution.py
+++ b/solution.py
@@ -265,16 +265,18 @@
     )(jnp.asarray(place, jnp.int32).reshape(1), *factors, other, low)
 
 
-def input_gradient_kernel(sources, shards, factor_blocks, _, *refs):
+def input_gradient_kernel(sources, shards, factor_blocks, scalars, *refs):
     weights, refs = refs[:shards], refs[shards:]
     factors, refs = refs[:factor_blocks], refs[factor_blocks:]
-    wides, refs = refs[:sources], refs[sources:]
-    grads, outs = refs[: sources * shards], refs[-sources:]
+    wides, grads, outs = refs[:sources], refs[sources : 2 * sources], refs[-sources:]
+    width = weights[0].shape[1]
     rows = jnp.concatenate([factor[...] for factor in factors], axis=0)
+    every = jnp.concatenate([weight[...] for weight in weights], axis=1)
+    places = [pl.ds(pl.multiple_of(scalars[k] * width, width), width) for k in range(shards)]
     for at in range(sources):
-        total = jnp.dot(wides[at][...], rows, preferred_element_type=F32)
-        for grad, weight in zip(grads[at * shards : (at + 1) * shards], weights, strict=True):
-            total += lax.dot_general(grad[...], weight[...], TRANS_B, preferred_element_type=F32)
+        ours = jnp.concatenate([grads[at][:, columns] for columns in places], axis=1)
+        total = lax.dot_general(ours, every, TRANS_B, preferred_element_type=F32)
+        total += jnp.dot(wides[at][...], rows, preferred_element_type=F32)
         outs[at][...] = total.astype(BF16)
 
 
@@ -293,14 +295,8 @@
     in_specs += [
         pl.BlockSpec((one.shape[0], block), lambda j, s: (0, s[shards + 1] * steps + j)) for one in halves
     ]
-    in_specs += [pl.BlockSpec(wide.shape, lambda j, s: (0, 0)) for wide in wides]
-    in_specs += [
-        pl.BlockSpec((tokens, width), functools.partial(lambda k, j, s: (0, s[k]), k))
-        for _ in grads
-        for k in range(shards)
-    ]
-    operands = [scalars, *weights, *factors, *halves, *wides]
-    operands += [grad for grad in grads for _ in range(shards)]
+    in_specs += [pl.BlockSpec(memory_space=pltpu.VMEM)] * (2 * sources)
+    operands = [scalars, *weights, *factors, *halves, *wides, *grads]
     aliases = {}
     if so_far is not None:
         in_specs.append(pl.BlockSpec(memory_space=pl.ANY))
@@ -318,7 +314,7 @@
         out_shape=[jax.ShapeDtypeStruct((tokens, features), BF16)]
         + [jax.ShapeDtypeStruct((tokens, rows), BF16)] * (sources - 1),
         input_output_aliases=aliases,
-        compiler_params=pltpu.CompilerParams(vmem_limit_bytes=56 * 2**20),
+        compiler_params=pltpu.CompilerParams(vmem_limit_bytes=51 * 2**20),
         cost_estimate=SMALL,
     )(*operands)
 
@@ -407,9 +403,10 @@
     low_back = low_rank([after(g_cores[0], came), *g_cores[1:]], up_line, *along_line, rank)
     low_back = sum_over_tp(adapter_scale_factor * low_back)
     down_blocks = outer(low_back, *along_line, x_cores, 1.0, n)
+    own_grad = whole_grad(output_gradient, tp_other)
     came = event(factors[-1], cost=LONG)
     factor_on(came)
-    came = event(w_up[1], w_down[1])
+    came = event(w_up[1], w_down[1], own_grad)
 
     weight_arrivals, whose = [], [z] + [arrival_owner(step) for step in range(1, n)]
 
@@ -475,7 +472,7 @@
         theirs = [rest[:, cut + at * LANES : cut + (at + 1) * LANES] for at in both]
         theirs = jnp.concatenate([theirs[(at - b) % subs] for at in both], axis=0)
         low_back_all = low_back_all + theirs.astype(F32)
-    grads = [whole_grad(one, two) for one, two in zip(g_cores, tp_cores, strict=True)]
+    grads = [own_grad] + [whole_grad(one, two) for one, two in zip(g_cores[1:], tp_cores[1:], strict=True)]
     wides = spread_out(
         low_back_all + came[:1], *ranges([((z - j) % n, (sub - b) % subs) for b in both for j in range(n)])
     )
@@ -514,21 +511,26 @@
         if bit == 1:
             last += [from_above, from_below, *weight_arrivals[-1][1:]]
         got = lax.ppermute(after(there, *last), "fsdp", [(i, i ^ (1 << bit)) for i in range(n)])
-        up_total = up_total + got.astype(F32)
         if not bit:
-            input_gradient, others = ig(0, None, others)
+            got = after(got, *wides, *grads)
+        if bit < bits - 1:
+            up_total = up_total + got.astype(F32)
+        if not bit:
+            for a in range(groups):
+                input_gradient, others = ig(a, input_gradient, others)
             last = [came, input_gradient]
-    for a in range(1, groups):
-        input_gradient, others = ig(a, input_gradient, others)
-
-    round_4 = [from_above, from_below, got, input_gradient]
+
+    round_4 = [from_above, from_below, input_gradient]
     for a in range(groups):
         for b, one in enumerate(others[a], 1):
-            got = lax.ppermute(
+            theirs = lax.ppermute(
                 after(one, *round_4), "sub", [(i, (i - b) % subs) for i in range(subs)]
             )
             part = ((sub + b) % subs) * groups + (y - a) % groups
-            input_gradient = lax.dynamic_update_slice_in_dim(input_gradient, got, part * part_rows, axis=1)
+            input_gradient = lax.dynamic_update_slice_in_dim(
+                input_gradient, theirs, part * part_rows, axis=1
+            )
+    up_total = up_total + after(got, input_gradient).astype(F32)
     return (
         input_gradient,
         grad_down.reshape(own_slots, rank, features),

time: 239 us -> 237 us (level)
  waiting for transfers between devices: 114 us -> 108 us
  starting transfers between devices: 41.9 us -> 46.1 us
    ppermute x2, waiting for transfers between devices: 6.22 us -> 25.5 us  [line_step(): lax.ppermute(down, 'fsdp', [(i, i - 1) for i in range(1, count - step + 1)])]
    ppermute x2, waiting for transfers between devices: 19.1 us -> 0.01 us  [line_step(): lax.ppermute(up, 'fsdp', [(i, i + 1) for i in range(step - 1, count - 1)])]
    ppermute x2, waiting for transfers between devices: 5.63 us -> 0.01 us  [sum_on(): lax.ppermute(upper, 'fsdp', [(i, i + 1) for i in range(step)])]
    ppermute x3, waiting for transfers between devices: 29.1 us -> 24 us  [factor_on(): lax.ppermute(after(factors[-1], *earlier), 'fsdp', around('fsdp'))]
    ppermute x3, starting transfers between devices: 4.59 us -> 0.81 us  [factor_on(): lax.ppermute(after(factors[-1], *earlier), 'fsdp', around('fsdp'))]
    ppermute x3, waiting for transfers between devices: 11.8 us -> 15.5 us  [local(): lax.ppermute(up_here, 'fsdp', [(i, (i + far) % n) for i in range(n)])]
    ppermute x2, starting transfers between devices: 1.21 us -> 4.47 us  [local(): lax.ppermute(after(there, *last), 'fsdp', [(i, i ^ 1 << bit) for i in ran...]
    ppermute x2, waiting for transfers between devices: 7.28 us -> 10 us  [local(): lax.ppermute(after(there, *last), 'fsdp', [(i, i ^ 1 << bit) for i in ran...]
  transfers between devices with their start and end apart: 30 -> 30, of which waited for: 18 -> 12; matrix products, arithmetic and copies ran while one was open for 8% -> 7% of each run, Pallas kernels for 24% -> 24%
where the time goes in v6:
time: 237 us; the launch traced here: 236 us
  waiting for transfers between devices  108 us (46%)
  Pallas kernels  56.3 us (24%)
  starting transfers between devices  46.1 us (19%)
  other arithmetic  12.3 us (5%)
  local copies, waits for them, and re-layouts  11.7 us (5%)
    ppermute x2, waiting for transfers between devices, line_step(): lax.ppermute(down, 'fsdp', [(i, i - 1) for i in range(1, count - step + 1)])  25.5 us
    ppermute x3, waiting for transfers between devices, factor_on(): lax.ppermute(after(factors[-1], *earlier), 'fsdp', around('fsdp'))  24 us
    pallas_call x2, Pallas kernels, input_gradient_part(): pl.pallas_call(functools.partial(input_gradient_kernel, sources, shards,...  23.3 us
    pallas_call x3, Pallas kernels, low_rank(): pl.pallas_call(functools.partial(low_kernel, len(xs), len(blocks), rank,...  19.4 us
    ppermute x1, waiting for transfers between devices, sum_on(): got = lax.ppermute(lower, 'fsdp', [(n - 1, n - 2), (0, 1)])  18.8 us
    ppermute x3, waiting for transfers between devices, local(): lax.ppermute(up_here, 'fsdp', [(i, (i + far) % n) for i in range(n)])  15.5 us
    pallas_call x2, Pallas kernels, outer(): pl.pallas_call(functools.partial(outer_kernel, scale, parts), grid=(featu...  10.8 us
    ppermute x2, waiting for transfers between devices, local(): lax.ppermute(after(there, *last), 'fsdp', [(i, i ^ 1 << bit) for i in ran...  10 us
  transfers between devices with their start and end apart: 30, of which 12 were waited for; matrix products, arithmetic and copies ran while one was open for 7% of the time, Pallas kernels for 24%

profile of v6, /device:TPU:0, one launch (start us, length us, event | category | flops | bytes accessed | tf_op | source)
XLA Modules:
  0.0 236.1 jit_solution(4378897288592842689)
XLA Ops:
  1.2 2.6 %collective-permute-start.6 = (bf16[512,1024]{1,0:T(8,128)(2,1)}, bf16[512,1024]{1,0:T(8,128)(2,1)S(1)}, u32[]{:S(2)}, u32[]{:S(2)}) collective-permute-start(bf16[512,1024]{1,0:T(8,128)(2,1)} %refs_0_.11), channel_id=1, source_target_pairs={{0,2},{2,0},{1,3},{3,1},{4,6},{6,4},{5,7},{7,5},{8,10},{10,8},{9,1... | collective-permute-start | bytes 3145736 | tf_op jit(solution)/shard_map/ppermute | solution.py:364
  4.2 3.6 %collective-permute-start.2 = (bf16[128,1024]{1,0:T(8,128)(2,1)}, bf16[128,1024]{1,0:T(8,128)(2,1)S(1)}, u32[]{:S(2)}, u32[]{:S(2)}) collective-permute-start(bf16[128,1024]{1,0:T(8,128)(2,1)} %bitcast.43), channel_id=1, source_target_pairs={{0,12},{4,0},{8,4},{12,8},{1,13},{5,1},{9,5},{13,9},{2,14},{6,2},{... | collective-permute-start | bytes 786440 | tf_op jit(solution)/shard_map/ppermute | solution.py:360
  11.0 2.6 %collective-permute-start.1 = (bf16[128,1024]{1,0:T(8,128)(2,1)}, bf16[128,1024]{1,0:T(8,128)(2,1)}, u32[]{:S(2)}, u32[]{:S(2)}) collective-permute-start(bf16[128,1024]{1,0:T(8,128)(2,1)} %bitcast.44), channel_id=1, source_target_pairs={{0,8},{4,12},{8,0},{12,4},{1,9},{5,13},{9,1},{13,5},{2,10},{6,14},... | collective-permute-start | bytes 786440 | tf_op jit(solution)/shard_map/ppermute | solution.py:360
  16.3 15.5 %collective-permute-done.1.refs_1_.refs_4_ = bf16[128,1024]{1,0:T(8,128)(2,1)} collective-permute-done((bf16[128,1024]{1,0:T(8,128)(2,1)}, bf16[128,1024]{1,0:T(8,128)(2,1)}, u32[]{:S(2)}, u32[]{:S(2)}) %collective-permute-start.1) | collective-permute-done | bytes 262176 | tf_op jit(solution)/shard_map/ppermute | solution.py:360
  33.1 2.8 %shard_map.97 = f32[1024,128]{1,0:T(8,128)S(1)} custom-call(bf16[512,1024]{1,0:T(8,128)(2,1)S(1)} %copy-done.12, bf16[512,1024]{1,0:T(8,128)(2,1)S(1)} %collective-permute-done.3.refs_3_.refs_1_, bf16[128,1024]{1,0:T(8,128)(2,1)S(1)} %bitcast.46, bf16[128,1024]{1,0:T(8,128)(2,1)S(1)} %collective-permute-done.refs_0_.refs_3_, ...), custom_call_target="tpu_custom_call" | custom-call | flops 1 | bytes 1 | tf_op jit(solution)/shard_map/pallas_call | solution.py:161
  39.2 4.4 %collective-permute-done.13 = bf16[1024,128]{1,0:T(8,128)(2,1)S(1)} collective-permute-done((bf16[1024,128]{1,0:T(8,128)(2,1)S(1)}, bf16[1024,128]{1,0:T(8,128)(2,1)S(1)}, u32[]{:S(2)}, u32[]{:S(2)}) %collective-permute-start.13) | collective-permute-done | bytes 262176 | tf_op jit(solution)/shard_map/ppermute | solution.py:89
  43.7 4.3 %collective-permute-start.7 = (bf16[1024,512]{1,0:T(8,128)(2,1)S(1)}, bf16[1024,512]{1,0:T(8,128)(2,1)S(1)}, u32[]{:S(2)}, u32[]{:S(2)}) collective-permute-start(bf16[1024,512]{1,0:T(8,128)(2,1)S(1)} %dynamic-slice_bitcast_fusion.refs_7_), channel_id=1, source_target_pairs={{0,4},{4,8},{8,12},{1,5},{5,9},{9,13},{2,6},{6,10},{10,14},{3,7},{... | collective-permute-start | bytes 3145736 | tf_op jit(solution)/shard_map/ppermute | solution.py:52
  48.1 8.7 %shard_map.98 = (f32[128,4096]{1,0:T(8,128)S(1)}, bf16[128,4096]{1,0:T(8,128)(2,1)S(1)}, bf16[128,4096]{1,0:T(8,128)(2,1)S(1)}, bf16[128,4096]{1,0:T(8,128)(2,1)S(1)}) custom-call(f32[1024,128]{1,0:T(8,128)S(1)} %convert_add_fusion.3.low.refs_5_, s32[2,512]{1,0:T(2,128)S(1)} %pad_add_fusion.2.refs_5_.refs_6_.start, ...), custom_call_target="tpu_custom_call" | custom-call | flops 1 | bytes 1 | tf_op jit(solution)/shard_map/pallas_call | solution.py:222
  56.9 3.0 %collective-permute-done.9.refs_0_.refs_3_.refs_1_.refs_5_ = bf16[128,4096]{1,0:T(8,128)(2,1)S(1)} collective-permute-done((bf16[128,4096]{1,0:T(8,128)(2,1)S(1)}, bf16[128,4096]{1,0:T(8,128)(2,1)S(1)}, u32[]{:S(2)}, u32[]{:S(2)}) %collective-permute-start.9) | collective-permute-done | bytes 1048608 | tf_op jit(solution)/shard_map/ppermute | solution.py:356
  60.0 22.2 %collective-permute-done.8.refs_1_ = bf16[1024,512]{1,0:T(8,128)(2,1)S(1)} collective-permute-done((bf16[1024,512]{1,0:T(8,128)(2,1)S(1)}, bf16[1024,512]{1,0:T(8,128)(2,1)S(1)}, u32[]{:S(2)}, u32[]{:S(2)}) %collective-permute-start.8) | collective-permute-done | bytes 1048608 | tf_op jit(solution)/shard_map/ppermute | solution.py:53
  86.1 5.1 %collective-permute-start.14 = (bf16[128,4096]{1,0:T(8,128)(2,1)S(1)}, bf16[128,4096]{1,0:T(8,128)(2,1)S(1)}, u32[]{:S(2)}, u32[]{:S(2)}) collective-permute-start(bf16[128,4096]{1,0:T(8,128)(2,1)S(1)} %broadcast_select_fusion.1), channel_id=1, source_target_pairs={{12,8},{0,4},{13,9},{1,5},{14,10},{2,6},{15,11},{3,7},{28,24},{16,... | collective-permute-start | bytes 3145736 | tf_op jit(solution)/shard_map/ppermute | solution.py:431
  91.1 13.7 %collective-permute-done.15.refs_0_.refs_4_.refs_2_.refs_6_ = bf16[128,4096]{1,0:T(8,128)(2,1)S(1)} collective-permute-done((bf16[128,4096]{1,0:T(8,128)(2,1)S(1)}, bf16[128,4096]{1,0:T(8,128)(2,1)S(1)}, u32[]{:S(2)}, u32[]{:S(2)}) %collective-permute-start.15) | collective-permute-done | bytes 1048608 | tf_op jit(solution)/shard_map/ppermute | solution.py:356
  104.8 18.8 %collective-permute-done.14.refs_2_.refs_3_ = bf16[128,4096]{1,0:T(8,128)(2,1)S(1)} collective-permute-done((bf16[128,4096]{1,0:T(8,128)(2,1)S(1)}, bf16[128,4096]{1,0:T(8,128)(2,1)S(1)}, u32[]{:S(2)}, u32[]{:S(2)}) %collective-permute-start.14) | collective-permute-done | bytes 1048608 | tf_op jit(solution)/shard_map/ppermute | solution.py:431
  123.9 3.3 %collective-permute-done.12.refs_1_ = bf16[1024,512]{1,0:T(8,128)(2,1)S(1)} collective-permute-done((bf16[1024,512]{1,0:T(8,128)(2,1)S(1)}, bf16[1024,512]{1,0:T(8,128)(2,1)S(1)}, u32[]{:S(2)}, u32[]{:S(2)}) %collective-permute-start.12) | collective-permute-done | bytes 1048608 | tf_op jit(solution)/shard_map/ppermute | solution.py:53
  133.9 8.7 %shard_map.101.refs_5_ = f32[1024,128]{1,0:T(8,128)S(1)} custom-call(bf16[512,4096]{1,0:T(8,128)(2,1)S(1)} %copy-done, bf16[512,4096]{1,0:T(8,128)(2,1)} %collective-permute-done.4.refs_4_.refs_1_, bf16[128,4096]{1,0:T(8,128)(2,1)S(1)} %bitcast.41, bf16[128,4096]{1,0:T(8,128)(2,1)S(1)} %collective-permute-done.9.refs_0_.refs_3_.refs_1_.refs_5_, ...), custom_call_target="tpu_custom_call" | custom-call | flops 1 | bytes 1 | tf_op jit(solution)/shard_map/pallas_call | solution.py:161
  142.5 7.3 %collective-permute-done.20.refs_2_.refs_0_.refs_3_.refs_7_ = bf16[128,4096]{1,0:T(8,128)(2,1)S(1)} collective-permute-done((bf16[128,4096]{1,0:T(8,128)(2,1)S(1)}, bf16[128,4096]{1,0:T(8,128)(2,1)S(1)}, u32[]{:S(2)}, u32[]{:S(2)}) %collective-permute-start.20) | collective-permute-done | bytes 1048608 | tf_op jit(solution)/shard_map/ppermute | solution.py:356
  149.9 8.0 %shard_map.102 = f32[1024,128]{1,0:T(8,128)S(1)} custom-call(bf16[512,4096]{1,0:T(8,128)(2,1)S(1)} %copy-done, bf16[512,4096]{1,0:T(8,128)(2,1)} %collective-permute-done.4.refs_4_.refs_1_, bf16[128,4096]{1,0:T(8,128)(2,1)S(1)} %collective-permute-done.20.refs_2_.refs_0_.refs_3_.refs_7_, s32[2,128]{1,0:T(2,128)S(1)} %get-tuple-element.113.refs_3_, ...), custom_call_target="tpu_custom_call" | custom-call | flops 1 | bytes 1 | tf_op jit(solution)/shard_map/pallas_call | solution.py:161
  159.4 4.9 %collective-permute-done.21 = bf16[1024,128]{1,0:T(8,128)(2,1)S(1)} collective-permute-done((bf16[1024,128]{1,0:T(8,128)(2,1)S(1)}, bf16[1024,128]{1,0:T(8,128)(2,1)S(1)}, u32[]{:S(2)}, u32[]{:S(2)}) %collective-permute-start.21) | collective-permute-done | bytes 262176 | tf_op jit(solution)/shard_map/ppermute | solution.py:89
  166.5 4.1 %collective-permute-done.17.refs_0_.refs_1_ = bf16[1024,512]{1,0:T(8,128)(2,1)S(1)} collective-permute-done((bf16[1024,512]{1,0:T(8,128)(2,1)S(1)}, bf16[1024,512]{1,0:T(8,128)(2,1)S(1)}, u32[]{:S(2)}, u32[]{:S(2)}) %collective-permute-start.17) | collective-permute-done | bytes 1048608 | tf_op jit(solution)/shard_map/ppermute | solution.py:47
  185.2 2.7 %collective-permute-start.28 = (bf16[256,1024]{1,0:T(8,128)(2,1)S(1)}, bf16[256,1024]{1,0:T(8,128)(2,1)S(1)}, u32[]{:S(2)}, u32[]{:S(2)}) collective-permute-start(bf16[256,1024]{1,0:T(8,128)(2,1)S(1)} %get-tuple-element.71), channel_id=1, source_target_pairs={{0,4},{4,0},{8,12},{12,8},{1,5},{5,1},{9,13},{13,9},{2,6},{6,2},{1... | collective-permute-start | bytes 1572872 | tf_op jit(solution)/shard_map/ppermute | solution.py:513
  192.3 11.7 %shard_map.108 = (bf16[512,4096]{1,0:T(8,128)(2,1)}, bf16[512,1024]{1,0:T(8,128)(2,1)S(1)}) custom-call(s32[6]{0:T(128)S(1)} %stack.157.scalars, bf16[4096,512]{1,0:T(8,128)(2,1)} %refs_0_.10, bf16[1024,512]{1,0:T(8,128)(2,1)S(1)} %broadcast_select_fusion.7.refs_1_, bf16[1024,512]{1,0:T(8,128)(2,1)} %copy-done.34, bf16[1024,512]{1,0:T(8,128)(2,1)} %copy-done.33, ...), custom_call_target="tpu_custom_call" | custom-call | flops 1 | bytes 1 | tf_op jit(solution)/shard_map/pallas_call | solution.py:305
  206.0 11.7 %shard_map.109 = (bf16[512,4096]{1,0:T(8,128)(2,1)}, bf16[512,1024]{1,0:T(8,128)(2,1)S(1)}) custom-call(s32[6]{0:T(128)S(1)} %stack.130.scalars, bf16[4096,512]{1,0:T(8,128)(2,1)} %refs_0_.10, bf16[1024,512]{1,0:T(8,128)(2,1)S(1)} %copy-done.23, bf16[1024,512]{1,0:T(8,128)(2,1)} %copy-done.24, ...), custom_call_target="tpu_custom_call", output_to_operand_aliasing={{0}: (14, {})} | custom-call | flops 1 | bytes 1 | tf_op jit(solution)/shard_map/pallas_call | solution.py:305
  218.3 2.9 %convert_add_fusion = f32[128,4096]{1,0:T(8,128)} fusion(bf16[128,4096]{1,0:T(8,128)(2,1)S(1)} %collective-permute-done.25, f32[128,4096]{1,0:T(8,128)S(1)} %copy-done.31, bf16[128,4096]{1,0:T(8,128)(2,1)} %collective-permute-done.24), kind=kLoop, calls=%fused_computation.2 | loop fusion | flops 2097152 | bytes 6291456 | tf_op jit(solution)/shard_map/add | solution.py:499
  225.2 10.0 %collective-permute-done.29 = bf16[128,1024]{1,0:T(8,128)(2,1)S(1)} collective-permute-done((bf16[128,1024]{1,0:T(8,128)(2,1)S(1)}, bf16[128,1024]{1,0:T(8,128)(2,1)S(1)}, u32[]{:S(2)}, u32[]{:S(2)}) %collective-permute-start.29) | collective-permute-done | bytes 262176 | tf_op jit(solution)/shard_map/ppermute | solution.py:513
  (207 shorter events, 52.1 us)
Async XLA Ops:
  0.7 31.2 %collective-permute-start.4 = (bf16[512,4096]{1,0:T(8,128)(2,1)}, bf16[512,4096]{1,0:T(8,128)(2,1)}, u32[]{:S(2)}, u32[]{:S(2)}) collective-permute-start(bf16[512,4096]{1,0:T(8,128)(2,1)} %refs_0_.8), channel_id=1, source_target_pairs={{0,1},{1,0},{2,3},{3,2},{4,5},{5,4},{6,7},{7,6},{8,9},{9,8},{10,11... | collective-permute-start | bytes 12582920 | tf_op jit(solution)/shard_map/ppermute | solution.py:96
  1.2 30.6 %collective-permute-start.6 = (bf16[512,1024]{1,0:T(8,128)(2,1)}, bf16[512,1024]{1,0:T(8,128)(2,1)S(1)}, u32[]{:S(2)}, u32[]{:S(2)}) collective-permute-start(bf16[512,1024]{1,0:T(8,128)(2,1)} %refs_0_.11), channel_id=1, source_target_pairs={{0,2},{2,0},{1,3},{3,1},{4,6},{6,4},{5,7},{7,5},{8,10},{10,8},{9,1... | collective-permute-start | bytes 3145736 | tf_op jit(solution)/shard_map/ppermute | solution.py:364
  3.7 28.1 %collective-permute-start.3 = (bf16[512,1024]{1,0:T(8,128)(2,1)}, bf16[512,1024]{1,0:T(8,128)(2,1)S(1)}, u32[]{:S(2)}, u32[]{:S(2)}) collective-permute-start(bf16[512,1024]{1,0:T(8,128)(2,1)} %refs_0_.11), channel_id=1, source_target_pairs={{0,1},{1,0},{2,3},{3,2},{4,5},{5,4},{6,7},{7,6},{8,9},{9,8},{10,11... | collective-permute-start | bytes 3145736 | tf_op jit(solution)/shard_map/ppermute | solution.py:96
  11.0 20.8 %collective-permute-start.1 = (bf16[128,1024]{1,0:T(8,128)(2,1)}, bf16[128,1024]{1,0:T(8,128)(2,1)}, u32[]{:S(2)}, u32[]{:S(2)}) collective-permute-start(bf16[128,1024]{1,0:T(8,128)(2,1)} %bitcast.44), channel_id=1, source_target_pairs={{0,8},{4,12},{8,0},{12,4},{1,9},{5,13},{9,1},{13,5},{2,10},{6,14},... | collective-permute-start | bytes 786440 | tf_op jit(solution)/shard_map/ppermute | solution.py:360
  14.5 17.2 %collective-permute-start = (bf16[128,1024]{1,0:T(8,128)(2,1)}, bf16[128,1024]{1,0:T(8,128)(2,1)S(1)}, u32[]{:S(2)}, u32[]{:S(2)}) collective-permute-start(bf16[128,1024]{1,0:T(8,128)(2,1)} %bitcast.45), channel_id=1, source_target_pairs={{0,4},{4,8},{8,12},{12,0},{1,5},{5,9},{9,13},{13,1},{2,6},{6,10},{... | collective-permute-start | bytes 786440 | tf_op jit(solution)/shard_map/ppermute | solution.py:360
  31.9 28.0 %collective-permute-start.9 = (bf16[128,4096]{1,0:T(8,128)(2,1)S(1)}, bf16[128,4096]{1,0:T(8,128)(2,1)S(1)}, u32[]{:S(2)}, u32[]{:S(2)}) collective-permute-start(bf16[128,4096]{1,0:T(8,128)(2,1)S(1)} %bitcast.40), channel_id=1, source_target_pairs={{0,4},{4,8},{8,12},{12,0},{1,5},{5,9},{9,13},{13,1},{2,6},{6,10},{... | collective-permute-start | bytes 3145736 | tf_op jit(solution)/shard_map/ppermute | solution.py:356
  37.7 44.5 %collective-permute-start.8 = (bf16[1024,512]{1,0:T(8,128)(2,1)S(1)}, bf16[1024,512]{1,0:T(8,128)(2,1)S(1)}, u32[]{:S(2)}, u32[]{:S(2)}) collective-permute-start(bf16[1024,512]{1,0:T(8,128)(2,1)S(1)} %dynamic-slice_bitcast_fusion.refs_7_), channel_id=1, source_target_pairs={{4,0},{8,4},{12,8},{5,1},{9,5},{13,9},{6,2},{10,6},{14,10},{7,3},{... | collective-permute-start | bytes 3145736 | tf_op jit(solution)/shard_map/ppermute | solution.py:53
  43.7 38.5 %collective-permute-start.7 = (bf16[1024,512]{1,0:T(8,128)(2,1)S(1)}, bf16[1024,512]{1,0:T(8,128)(2,1)S(1)}, u32[]{:S(2)}, u32[]{:S(2)}) collective-permute-start(bf16[1024,512]{1,0:T(8,128)(2,1)S(1)} %dynamic-slice_bitcast_fusion.refs_7_), channel_id=1, source_target_pairs={{0,4},{4,8},{8,12},{1,5},{5,9},{9,13},{2,6},{6,10},{10,14},{3,7},{... | collective-permute-start | bytes 3145736 | tf_op jit(solution)/shard_map/ppermute | solution.py:52
  59.9 45.0 %collective-permute-start.15 = (bf16[128,4096]{1,0:T(8,128)(2,1)S(1)}, bf16[128,4096]{1,0:T(8,128)(2,1)S(1)}, u32[]{:S(2)}, u32[]{:S(2)}) collective-permute-start(bf16[128,4096]{1,0:T(8,128)(2,1)S(1)} %collective-permute-done.9.refs_0_.refs_3_.refs_1_.refs_5_), channel_id=1, source_target_pairs={{0,4},{4,8},{8,12},{12,0},{1,5},{5,9},{9,13},{13,1},{2,6},{6,10},{... | collective-permute-start | bytes 3145736 | tf_op jit(solution)/shard_map/ppermute | solution.py:356
  82.4 41.5 %collective-permute-start.10 = (bf16[1024,512]{1,0:T(8,128)(2,1)S(1)}, bf16[1024,512]{1,0:T(8,128)(2,1)S(1)}, u32[]{:S(2)}, u32[]{:S(2)}) collective-permute-start(bf16[1024,512]{1,0:T(8,128)(2,1)S(1)} %broadcast_select_fusion.7.refs_1_), channel_id=1, source_target_pairs={{0,16},{16,0},{1,17},{17,1},{2,18},{18,2},{3,19},{19,3},{4,20},{20... | collective-permute-start | bytes 3145736 | tf_op jit(solution)/shard_map/ppermute | solution.py:416
  84.0 39.9 %collective-permute-start.11 = (bf16[1024,512]{1,0:T(8,128)(2,1)S(1)}, bf16[1024,512]{1,0:T(8,128)(2,1)S(1)}, u32[]{:S(2)}, u32[]{:S(2)}) collective-permute-start(bf16[1024,512]{1,0:T(8,128)(2,1)S(1)} %collective-permute-done.7.refs_0_), channel_id=1, source_target_pairs={{4,8},{8,12},{5,9},{9,13},{6,10},{10,14},{7,11},{11,15},{20,24},{2... | collective-permute-start | bytes 3145736 | tf_op jit(solution)/shard_map/ppermute | solution.py:52
  84.8 42.5 %collective-permute-start.12 = (bf16[1024,512]{1,0:T(8,128)(2,1)S(1)}, bf16[1024,512]{1,0:T(8,128)(2,1)S(1)}, u32[]{:S(2)}, u32[]{:S(2)}) collective-permute-start(bf16[1024,512]{1,0:T(8,128)(2,1)S(1)} %collective-permute-done.8.refs_1_), channel_id=1, source_target_pairs={{4,0},{8,4},{5,1},{9,5},{6,2},{10,6},{7,3},{11,7},{20,16},{24,20},... | collective-permute-start | bytes 3145736 | tf_op jit(solution)/shard_map/ppermute | solution.py:53
  86.1 37.6 %collective-permute-start.14 = (bf16[128,4096]{1,0:T(8,128)(2,1)S(1)}, bf16[128,4096]{1,0:T(8,128)(2,1)S(1)}, u32[]{:S(2)}, u32[]{:S(2)}) collective-permute-start(bf16[128,4096]{1,0:T(8,128)(2,1)S(1)} %broadcast_select_fusion.1), channel_id=1, source_target_pairs={{12,8},{0,4},{13,9},{1,5},{14,10},{2,6},{15,11},{3,7},{28,24},{16,... | collective-permute-start | bytes 3145736 | tf_op jit(solution)/shard_map/ppermute | solution.py:431
  104.8 45.0 %collective-permute-start.20 = (bf16[128,4096]{1,0:T(8,128)(2,1)S(1)}, bf16[128,4096]{1,0:T(8,128)(2,1)S(1)}, u32[]{:S(2)}, u32[]{:S(2)}) collective-permute-start(bf16[128,4096]{1,0:T(8,128)(2,1)S(1)} %collective-permute-done.15.refs_0_.refs_4_.refs_2_.refs_6_), channel_id=1, source_target_pairs={{0,4},{4,8},{8,12},{12,0},{1,5},{5,9},{9,13},{13,1},{2,6},{6,10},{... | collective-permute-start | bytes 3145736 | tf_op jit(solution)/shard_map/ppermute | solution.py:356
  127.2 43.3 %collective-permute-start.19 = (bf16[128,4096]{1,0:T(8,128)(2,1)S(1)}, bf16[128,4096]{1,0:T(8,128)(2,1)S(1)}, u32[]{:S(2)}, u32[]{:S(2)}) collective-permute-start(bf16[128,4096]{1,0:T(8,128)(2,1)S(1)} %add_convert_fusion.2), channel_id=1, source_target_pairs={{0,4},{4,8},{1,5},{5,9},{2,6},{6,10},{3,7},{7,11},{16,20},{20,24},... | collective-permute-start | bytes 3145736 | tf_op jit(solution)/shard_map/ppermute | solution.py:435
  129.8 40.8 %collective-permute-start.18 = (bf16[128,4096]{1,0:T(8,128)(2,1)S(1)}, bf16[128,4096]{1,0:T(8,128)(2,1)S(1)}, u32[]{:S(2)}, u32[]{:S(2)}) collective-permute-start(bf16[128,4096]{1,0:T(8,128)(2,1)S(1)} %add_convert_fusion.2), channel_id=1, source_target_pairs={{8,4},{12,8},{9,5},{13,9},{10,6},{14,10},{11,7},{15,11},{24,20},{2... | collective-permute-start | bytes 3145736 | tf_op jit(solution)/shard_map/ppermute | solution.py:434
  130.6 35.8 %collective-permute-start.16 = (bf16[1024,512]{1,0:T(8,128)(2,1)S(1)}, bf16[1024,512]{1,0:T(8,128)(2,1)S(1)}, u32[]{:S(2)}, u32[]{:S(2)}) collective-permute-start(bf16[1024,512]{1,0:T(8,128)(2,1)S(1)} %broadcast_select_fusion.6.refs_2_), channel_id=1, source_target_pairs={{0,16},{16,0},{1,17},{17,1},{2,18},{18,2},{3,19},{19,3},{4,20},{20... | collective-permute-start | bytes 3145736 | tf_op jit(solution)/shard_map/ppermute | solution.py:416
  132.4 38.1 %collective-permute-start.17 = (bf16[1024,512]{1,0:T(8,128)(2,1)S(1)}, bf16[1024,512]{1,0:T(8,128)(2,1)S(1)}, u32[]{:S(2)}, u32[]{:S(2)}) collective-permute-start(bf16[1024,512]{1,0:T(8,128)(2,1)S(1)} %broadcast_select_fusion), channel_id=1, source_target_pairs={{8,12},{4,0},{9,13},{5,1},{10,14},{6,2},{11,15},{7,3},{24,28},{20,... | collective-permute-start | bytes 3145736 | tf_op jit(solution)/shard_map/ppermute | solution.py:47
  171.5 12.6 %collective-permute-start.23 = (bf16[512,3328]{1,0:T(8,128)(2,1)}, bf16[512,3328]{1,0:T(8,128)(2,1)}, u32[]{:S(2)}, u32[]{:S(2)}) collective-permute-start(bf16[512,3328]{1,0:T(8,128)(2,1)} %shard_map.106), channel_id=1, source_target_pairs={{0,1},{1,0},{2,3},{3,2},{4,5},{5,4},{6,7},{7,6},{8,9},{9,8},{10,11... | collective-permute-start | bytes 10223624 | tf_op jit(solution)/shard_map/ppermute | solution.py:465
  179.4 25.6 %collective-permute-start.22 = (bf16[1024,512]{1,0:T(8,128)(2,1)S(1)}, bf16[1024,512]{1,0:T(8,128)(2,1)S(1)}, u32[]{:S(2)}, u32[]{:S(2)}) collective-permute-start(bf16[1024,512]{1,0:T(8,128)(2,1)S(1)} %select_select_fusion.refs_3_), channel_id=1, source_target_pairs={{0,16},{16,0},{1,17},{17,1},{2,18},{18,2},{3,19},{19,3},{4,20},{20... | collective-permute-start | bytes 3145736 | tf_op jit(solution)/shard_map/ppermute | solution.py:416
  181.1 36.6 %collective-permute-start.25 = (bf16[128,4096]{1,0:T(8,128)(2,1)S(1)}, bf16[128,4096]{1,0:T(8,128)(2,1)S(1)}, u32[]{:S(2)}, u32[]{:S(2)}) collective-permute-start(bf16[128,4096]{1,0:T(8,128)(2,1)S(1)} %add_convert_fusion), channel_id=1, source_target_pairs={{0,4},{4,8},{8,12},{1,5},{5,9},{9,13},{2,6},{6,10},{10,14},{3,7},{... | collective-permute-start | bytes 3145736 | tf_op jit(solution)/shard_map/ppermute | solution.py:435
  182.6 35.1 %collective-permute-start.24 = (bf16[128,4096]{1,0:T(8,128)(2,1)S(1)}, bf16[128,4096]{1,0:T(8,128)(2,1)}, u32[]{:S(2)}, u32[]{:S(2)}) collective-permute-start(bf16[128,4096]{1,0:T(8,128)(2,1)S(1)} %add_convert_fusion.1), channel_id=1, source_target_pairs={{4,0},{8,4},{12,8},{5,1},{9,5},{13,9},{6,2},{10,6},{14,10},{7,3},{... | collective-permute-start | bytes 3145736 | tf_op jit(solution)/shard_map/ppermute | solution.py:434
  185.2 36.0 %collective-permute-start.28 = (bf16[256,1024]{1,0:T(8,128)(2,1)S(1)}, bf16[256,1024]{1,0:T(8,128)(2,1)S(1)}, u32[]{:S(2)}, u32[]{:S(2)}) collective-permute-start(bf16[256,1024]{1,0:T(8,128)(2,1)S(1)} %get-tuple-element.71), channel_id=1, source_target_pairs={{0,4},{4,0},{8,12},{12,8},{1,5},{5,1},{9,13},{13,9},{2,6},{6,2},{1... | collective-permute-start | bytes 1572872 | tf_op jit(solution)/shard_map/ppermute | solution.py:513
  221.4 13.9 %collective-permute-start.29 = (bf16[128,1024]{1,0:T(8,128)(2,1)S(1)}, bf16[128,1024]{1,0:T(8,128)(2,1)S(1)}, u32[]{:S(2)}, u32[]{:S(2)}) collective-permute-start(bf16[128,1024]{1,0:T(8,128)(2,1)S(1)} %slice.39), channel_id=1, source_target_pairs={{0,8},{4,12},{8,0},{12,4},{1,9},{5,13},{9,1},{13,5},{2,10},{6,14},... | collective-permute-start | bytes 786440 | tf_op jit(solution)/shard_map/ppermute | solution.py:513
  (44 other events, 557.1 us)

commit v7 on v6

--- a/solution.py
+++ b/solution.py
@@ -360,18 +360,6 @@
         lax.ppermute(up_here, "fsdp", [(i, (i + far) % n) for i in range(n)]) for far in range(1, n)
     ]
 
-    if lax.axis_size("tp") == 2:
-        tp_other = lax.ppermute(output_gradient, "tp", around("tp"))
-        first = lax.axis_index("tp") == 0
-
-        def whole_grad(one, two):
-            return jnp.concatenate([jnp.where(first, one, two), jnp.where(first, two, one)], axis=1)
-    else:
-        tp_other = lax.all_gather(output_gradient, "tp", axis=1, tiled=True)
-
-        def whole_grad(one, two):
-            return two
-
     hot = owners[:, None] == lax.broadcasted_iota(jnp.int32, (slots, slots), 1)
     bounds = []
     for count in count_cores:
@@ -396,17 +384,29 @@
         base_weight.reshape(copies, part_rows, width), sub * groups + y, 0, keepdims=False
     )
     w_up, w_down = [weight_here], [weight_here]
-    came = event(*up_line[1:], *g_cores[1:], *x_cores[1:], *along_line, weight_here, tp_other)
+    came = event(*up_line[1:], *g_cores[1:], *x_cores[1:], *along_line, weight_here)
 
     line_on(w_up, w_down, 1, came)
     factor_on(came)
     low_back = low_rank([after(g_cores[0], came), *g_cores[1:]], up_line, *along_line, rank)
     low_back = sum_over_tp(adapter_scale_factor * low_back)
+    if lax.axis_size("tp") == 2:
+        tp_other = lax.ppermute(after(output_gradient, low_back), "tp", around("tp"))
+        first = lax.axis_index("tp") == 0
+
+        def whole_grad(one, two):
+            return jnp.concatenate([jnp.where(first, one, two), jnp.where(first, two, one)], axis=1)
+    else:
+        tp_other = lax.all_gather(output_gradient, "tp", axis=1, tiled=True)
+
+        def whole_grad(one, two):
+            return two
+
     down_blocks = outer(low_back, *along_line, x_cores, 1.0, n)
     own_grad = whole_grad(output_gradient, tp_other)
     came = event(factors[-1], cost=LONG)
     factor_on(came)
-    came = event(w_up[1], w_down[1], own_grad)
+    came = event(w_up[1], w_down[1], tp_other)
 
     weight_arrivals, whose = [], [z] + [arrival_owner(step) for step in range(1, n)]
 

time: 237 us -> 232 us (0.979)
  waiting for transfers between devices: 108 us -> 113 us
  starting transfers between devices: 46.1 us -> 42.7 us
  local copies, waits for them, and re-layouts: 11.7 us -> 8.9 us
  Pallas kernels: 56.3 us -> 53.6 us
    ppermute x2, waiting for transfers between devices: 9.32 us -> 4.88 us  [sum_over_tp(): lax.ppermute(part.astype(BF16), 'tp', around('tp')).astype(F32)]
    ppermute x3, waiting for transfers between devices: 24 us -> 26.8 us  [factor_on(): lax.ppermute(after(factors[-1], *earlier), 'fsdp', around('fsdp'))]
    ppermute x2, waiting for transfers between devices: 10 us -> 12.5 us  [local(): lax.ppermute(after(there, *last), 'fsdp', [(i, i ^ 1 << bit) for i in ran...]
    unnamed x76 -> x40, local copies, waits for them, and re-layouts: 5.42 us -> 3.59 us
  transfers between devices with their start and end apart: 30 -> 30, of which waited for: 12 -> 13; matrix products, arithmetic and copies ran while one was open for 7% -> 7% of each run, Pallas kernels for 24% -> 23%
where the time goes in v7:
time: 232 us
  waiting for transfers between devices  113 us (49%)
  Pallas kernels  53.6 us (23%)
  starting transfers between devices  42.7 us (18%)
  other arithmetic  11.6 us (5%)
  local copies, waits for them, and re-layouts  8.9 us (4%)
    ppermute x3, waiting for transfers between devices, factor_on(): lax.ppermute(after(factors[-1], *earlier), 'fsdp', around('fsdp'))  26.8 us
    ppermute x2, waiting for transfers between devices, line_step(): lax.ppermute(down, 'fsdp', [(i, i - 1) for i in range(1, count - step + 1)])  25.4 us
    pallas_call x2, Pallas kernels, input_gradient_part(): pl.pallas_call(functools.partial(input_gradient_kernel, sources, shards,...  23.3 us
    ppermute x1, waiting for transfers between devices, sum_on(): got = lax.ppermute(lower, 'fsdp', [(n - 1, n - 2), (0, 1)])  18.9 us
    pallas_call x3, Pallas kernels, low_rank(): pl.pallas_call(functools.partial(low_kernel, len(xs), len(blocks), rank,...  18.4 us
    ppermute x3, waiting for transfers between devices, local(): lax.ppermute(up_here, 'fsdp', [(i, (i + far) % n) for i in range(n)])  17.1 us
    ppermute x2, waiting for transfers between devices, local(): lax.ppermute(after(there, *last), 'fsdp', [(i, i ^ 1 << bit) for i in ran...  12.5 us
    pallas_call x2, Pallas kernels, outer(): pl.pallas_call(functools.partial(outer_kernel, scale, parts), grid=(featu...  10.8 us
  transfers between devices with their start and end apart: 30, of which 13 were waited for; matrix products, arithmetic and copies ran while one was open for 7% of the time, Pallas kernels for 23%

profile of v7, /device:TPU:0, one launch (start us, length us, event | category | flops | bytes accessed | tf_op | source)
XLA Modules:
  0.0 231.6 jit_solution(311380899357555511)
XLA Ops:
  1.2 4.7 %collective-permute-start.2 = (bf16[128,1024]{1,0:T(8,128)(2,1)}, bf16[128,1024]{1,0:T(8,128)(2,1)S(1)}, u32[]{:S(2)}, u32[]{:S(2)}) collective-permute-start(bf16[128,1024]{1,0:T(8,128)(2,1)} %bitcast.43), channel_id=1, source_target_pairs={{0,12},{4,0},{8,4},{12,8},{1,13},{5,1},{9,5},{13,9},{2,14},{6,2},{... | collective-permute-start | bytes 786440 | tf_op jit(solution)/shard_map/ppermute | solution.py:360
  12.8 16.1 %collective-permute-done.1.refs_1_.refs_4_ = bf16[128,1024]{1,0:T(8,128)(2,1)S(1)} collective-permute-done((bf16[128,1024]{1,0:T(8,128)(2,1)}, bf16[128,1024]{1,0:T(8,128)(2,1)S(1)}, u32[]{:S(2)}, u32[]{:S(2)}) %collective-permute-start.1) | collective-permute-done | bytes 262176 | tf_op jit(solution)/shard_map/ppermute | solution.py:360
  30.0 1.8 shard_map.95
  35.0 5.1 %collective-permute-start.6 = (bf16[1024,512]{1,0:T(8,128)(2,1)S(1)}, bf16[1024,512]{1,0:T(8,128)(2,1)S(1)}, u32[]{:S(2)}, u32[]{:S(2)}) collective-permute-start(bf16[1024,512]{1,0:T(8,128)(2,1)S(1)} %dynamic-slice_bitcast_fusion.refs_7_), channel_id=1, source_target_pairs={{0,4},{4,8},{8,12},{1,5},{5,9},{9,13},{2,6},{6,10},{10,14},{3,7},{... | collective-permute-start | bytes 3145736 | tf_op jit(solution)/shard_map/ppermute | solution.py:52
  40.8 8.7 %shard_map.98 = (f32[128,4096]{1,0:T(8,128)S(1)}, bf16[128,4096]{1,0:T(8,128)(2,1)S(1)}, bf16[128,4096]{1,0:T(8,128)(2,1)S(1)}, bf16[128,4096]{1,0:T(8,128)(2,1)S(1)}) custom-call(f32[1024,128]{1,0:T(8,128)S(1)} %convert_add_fusion.3.low.refs_5_, s32[2,512]{1,0:T(2,128)S(1)} %pad_add_fusion.2.refs_5_.refs_6_.start, ...), custom_call_target="tpu_custom_call" | custom-call | flops 1 | bytes 1 | tf_op jit(solution)/shard_map/pallas_call | solution.py:222
  50.9 6.1 %collective-permute-done.10.refs_0_.refs_3_.refs_1_.refs_5_ = bf16[128,4096]{1,0:T(8,128)(2,1)S(1)} collective-permute-done((bf16[128,4096]{1,0:T(8,128)(2,1)S(1)}, bf16[128,4096]{1,0:T(8,128)(2,1)S(1)}, u32[]{:S(2)}, u32[]{:S(2)}) %collective-permute-start.10) | collective-permute-done | bytes 1048608 | tf_op jit(solution)/shard_map/ppermute | solution.py:356
  57.1 22.3 %collective-permute-done.7.refs_1_ = bf16[1024,512]{1,0:T(8,128)(2,1)S(1)} collective-permute-done((bf16[1024,512]{1,0:T(8,128)(2,1)S(1)}, bf16[1024,512]{1,0:T(8,128)(2,1)S(1)}, u32[]{:S(2)}, u32[]{:S(2)}) %collective-permute-start.7) | collective-permute-done | bytes 1048608 | tf_op jit(solution)/shard_map/ppermute | solution.py:53
  83.1 5.4 %collective-permute-start.14 = (bf16[128,4096]{1,0:T(8,128)(2,1)S(1)}, bf16[128,4096]{1,0:T(8,128)(2,1)S(1)}, u32[]{:S(2)}, u32[]{:S(2)}) collective-permute-start(bf16[128,4096]{1,0:T(8,128)(2,1)S(1)} %broadcast_select_fusion.5), channel_id=1, source_target_pairs={{12,8},{0,4},{13,9},{1,5},{14,10},{2,6},{15,11},{3,7},{28,24},{16,... | collective-permute-start | bytes 3145736 | tf_op jit(solution)/shard_map/ppermute | solution.py:431
  88.5 13.4 %collective-permute-done.15.refs_0_.refs_4_.refs_2_.refs_6_ = bf16[128,4096]{1,0:T(8,128)(2,1)S(1)} collective-permute-done((bf16[128,4096]{1,0:T(8,128)(2,1)S(1)}, bf16[128,4096]{1,0:T(8,128)(2,1)S(1)}, u32[]{:S(2)}, u32[]{:S(2)}) %collective-permute-start.15) | collective-permute-done | bytes 1048608 | tf_op jit(solution)/shard_map/ppermute | solution.py:356
  102.0 18.9 %collective-permute-done.14.refs_2_.refs_3_ = bf16[128,4096]{1,0:T(8,128)(2,1)S(1)} collective-permute-done((bf16[128,4096]{1,0:T(8,128)(2,1)S(1)}, bf16[128,4096]{1,0:T(8,128)(2,1)S(1)}, u32[]{:S(2)}, u32[]{:S(2)}) %collective-permute-start.14) | collective-permute-done | bytes 1048608 | tf_op jit(solution)/shard_map/ppermute | solution.py:431
  121.2 3.2 %collective-permute-done.13.refs_1_ = bf16[1024,512]{1,0:T(8,128)(2,1)S(1)} collective-permute-done((bf16[1024,512]{1,0:T(8,128)(2,1)S(1)}, bf16[1024,512]{1,0:T(8,128)(2,1)S(1)}, u32[]{:S(2)}, u32[]{:S(2)}) %collective-permute-start.13) | collective-permute-done | bytes 1048608 | tf_op jit(solution)/shard_map/ppermute | solution.py:53
  124.3 2.5 %collective-permute-start.19 = (bf16[128,4096]{1,0:T(8,128)(2,1)S(1)}, bf16[128,4096]{1,0:T(8,128)(2,1)S(1)}, u32[]{:S(2)}, u32[]{:S(2)}) collective-permute-start(bf16[128,4096]{1,0:T(8,128)(2,1)S(1)} %add_convert_fusion.2), channel_id=1, source_target_pairs={{0,4},{4,8},{1,5},{5,9},{2,6},{6,10},{3,7},{7,11},{16,20},{20,24},... | collective-permute-start | bytes 3145736 | tf_op jit(solution)/shard_map/ppermute | solution.py:435
  131.0 8.6 %shard_map.101.refs_5_ = f32[1024,128]{1,0:T(8,128)S(1)} custom-call(bf16[512,4096]{1,0:T(8,128)(2,1)S(1)} %copy-done, bf16[512,4096]{1,0:T(8,128)(2,1)} %collective-permute-done.4.refs_4_.refs_1_, bf16[128,4096]{1,0:T(8,128)(2,1)S(1)} %bitcast.41, bf16[128,4096]{1,0:T(8,128)(2,1)S(1)} %collective-permute-done.10.refs_0_.refs_3_.refs_1_.refs_5_, ...), custom_call_target="tpu_custom_call" | custom-call | flops 1 | bytes 1 | tf_op jit(solution)/shard_map/pallas_call | solution.py:161
  139.6 7.4 %collective-permute-done.20.refs_2_.refs_0_.refs_3_.refs_7_ = bf16[128,4096]{1,0:T(8,128)(2,1)S(1)} collective-permute-done((bf16[128,4096]{1,0:T(8,128)(2,1)S(1)}, bf16[128,4096]{1,0:T(8,128)(2,1)S(1)}, u32[]{:S(2)}, u32[]{:S(2)}) %collective-permute-start.20) | collective-permute-done | bytes 1048608 | tf_op jit(solution)/shard_map/ppermute | solution.py:356
  147.0 8.0 %shard_map.102 = f32[1024,128]{1,0:T(8,128)S(1)} custom-call(bf16[512,4096]{1,0:T(8,128)(2,1)S(1)} %copy-done, bf16[512,4096]{1,0:T(8,128)(2,1)} %collective-permute-done.4.refs_4_.refs_1_, bf16[128,4096]{1,0:T(8,128)(2,1)S(1)} %collective-permute-done.20.refs_2_.refs_0_.refs_3_.refs_7_, s32[2,128]{1,0:T(2,128)S(1)} %get-tuple-element.115.refs_3_, ...), custom_call_target="tpu_custom_call" | custom-call | flops 1 | bytes 1 | tf_op jit(solution)/shard_map/pallas_call | solution.py:161
  156.6 4.9 %collective-permute-done.21 = bf16[1024,128]{1,0:T(8,128)(2,1)S(1)} collective-permute-done((bf16[1024,128]{1,0:T(8,128)(2,1)S(1)}, bf16[1024,128]{1,0:T(8,128)(2,1)S(1)}, u32[]{:S(2)}, u32[]{:S(2)}) %collective-permute-start.21) | collective-permute-done | bytes 262176 | tf_op jit(solution)/shard_map/ppermute | solution.py:89
  161.8 6.3 %collective-permute-done.17.refs_0_.refs_1_ = bf16[1024,512]{1,0:T(8,128)(2,1)S(1)} collective-permute-done((bf16[1024,512]{1,0:T(8,128)(2,1)S(1)}, bf16[1024,512]{1,0:T(8,128)(2,1)S(1)}, u32[]{:S(2)}, u32[]{:S(2)}) %collective-permute-start.17) | collective-permute-done | bytes 1048608 | tf_op jit(solution)/shard_map/ppermute | solution.py:47
  171.6 2.1 shard_map.110
  175.3 3.3 %collective-permute-start.25 = (bf16[128,4096]{1,0:T(8,128)(2,1)}, bf16[128,4096]{1,0:T(8,128)(2,1)}, u32[]{:S(2)}, u32[]{:S(2)}) collective-permute-start(bf16[128,4096]{1,0:T(8,128)(2,1)} %add_convert_fusion), channel_id=1, source_target_pairs={{0,4},{4,8},{8,12},{1,5},{5,9},{9,13},{2,6},{6,10},{10,14},{3,7},{... | collective-permute-start | bytes 3145736 | tf_op jit(solution)/shard_map/ppermute | solution.py:435
  180.0 2.7 %collective-permute-start.28 = (bf16[256,1024]{1,0:T(8,128)(2,1)S(1)}, bf16[256,1024]{1,0:T(8,128)(2,1)S(1)}, u32[]{:S(2)}, u32[]{:S(2)}) collective-permute-start(bf16[256,1024]{1,0:T(8,128)(2,1)S(1)} %get-tuple-element.73), channel_id=1, source_target_pairs={{0,4},{4,0},{8,12},{12,8},{1,5},{5,1},{9,13},{13,9},{2,6},{6,2},{1... | collective-permute-start | bytes 1572872 | tf_op jit(solution)/shard_map/ppermute | solution.py:513
  186.3 11.7 %shard_map.108 = (bf16[512,4096]{1,0:T(8,128)(2,1)}, bf16[512,1024]{1,0:T(8,128)(2,1)S(1)}) custom-call(s32[6]{0:T(128)S(1)} %stack.157.scalars, bf16[4096,512]{1,0:T(8,128)(2,1)} %refs_0_.10, bf16[1024,512]{1,0:T(8,128)(2,1)S(1)} %copy-done.10, bf16[1024,512]{1,0:T(8,128)(2,1)} %copy-done.16, bf16[1024,512]{1,0:T(8,128)(2,1)} %copy-done.15, ...), custom_call_target="tpu_custom_call" | custom-call | flops 1 | bytes 1 | tf_op jit(solution)/shard_map/pallas_call | solution.py:305
  200.4 11.7 %shard_map.109 = (bf16[512,4096]{1,0:T(8,128)(2,1)}, bf16[512,1024]{1,0:T(8,128)(2,1)S(1)}) custom-call(s32[6]{0:T(128)S(1)} %stack.130.scalars, bf16[4096,512]{1,0:T(8,128)(2,1)} %refs_0_.10, bf16[1024,512]{1,0:T(8,128)(2,1)S(1)} %collective-permute-done.11.refs_4_.refs_1_, bf16[1024,512]{1,0:T(8,128)(2,1)} %copy-done.6, ...), custom_call_target="tpu_custom_call", output_to_operand_aliasing={{0}: (14, {})} | custom-call | flops 1 | bytes 1 | tf_op jit(solution)/shard_map/pallas_call | solution.py:305
  212.7 3.2 %convert_add_fusion = f32[128,4096]{1,0:T(8,128)} fusion(bf16[128,4096]{1,0:T(8,128)(2,1)} %collective-permute-done.25, f32[128,4096]{1,0:T(8,128)S(1)} %copy-done.12, bf16[128,4096]{1,0:T(8,128)(2,1)} %collective-permute-done.24), kind=kLoop, calls=%fused_computation.2 | loop fusion | flops 2097152 | bytes 6291456 | tf_op jit(solution)/shard_map/add | solution.py:499
  219.1 11.7 %collective-permute-done.29 = bf16[128,1024]{1,0:T(8,128)(2,1)S(1)} collective-permute-done((bf16[128,1024]{1,0:T(8,128)(2,1)S(1)}, bf16[128,1024]{1,0:T(8,128)(2,1)S(1)}, u32[]{:S(2)}, u32[]{:S(2)}) %collective-permute-start.29) | collective-permute-done | bytes 262176 | tf_op jit(solution)/shard_map/ppermute | solution.py:513
  (171 shorter events, 40.6 us)
Async XLA Ops:
  0.7 28.3 %collective-permute-start.4 = (bf16[512,4096]{1,0:T(8,128)(2,1)}, bf16[512,4096]{1,0:T(8,128)(2,1)}, u32[]{:S(2)}, u32[]{:S(2)}) collective-permute-start(bf16[512,4096]{1,0:T(8,128)(2,1)} %refs_0_.8), channel_id=1, source_target_pairs={{0,1},{1,0},{2,3},{3,2},{4,5},{5,4},{6,7},{7,6},{8,9},{9,8},{10,11... | collective-permute-start | bytes 12582920 | tf_op jit(solution)/shard_map/ppermute | solution.py:96
  5.8 23.1 %collective-permute-start.1 = (bf16[128,1024]{1,0:T(8,128)(2,1)}, bf16[128,1024]{1,0:T(8,128)(2,1)S(1)}, u32[]{:S(2)}, u32[]{:S(2)}) collective-permute-start(bf16[128,1024]{1,0:T(8,128)(2,1)} %bitcast.44), channel_id=1, source_target_pairs={{0,8},{4,12},{8,0},{12,4},{1,9},{5,13},{9,1},{13,5},{2,10},{6,14},... | collective-permute-start | bytes 786440 | tf_op jit(solution)/shard_map/ppermute | solution.py:360
  6.0 23.0 %collective-permute-start.3 = (bf16[512,1024]{1,0:T(8,128)(2,1)}, bf16[512,1024]{1,0:T(8,128)(2,1)S(1)}, u32[]{:S(2)}, u32[]{:S(2)}) collective-permute-start(bf16[512,1024]{1,0:T(8,128)(2,1)} %refs_0_.11), channel_id=1, source_target_pairs={{0,1},{1,0},{2,3},{3,2},{4,5},{5,4},{6,7},{7,6},{8,9},{9,8},{10,11... | collective-permute-start | bytes 3145736 | tf_op jit(solution)/shard_map/ppermute | solution.py:96
  10.0 19.0 %collective-permute-start = (bf16[128,1024]{1,0:T(8,128)(2,1)S(1)}, bf16[128,1024]{1,0:T(8,128)(2,1)S(1)}, u32[]{:S(2)}, u32[]{:S(2)}) collective-permute-start(bf16[128,1024]{1,0:T(8,128)(2,1)S(1)} %bitcast.45), channel_id=1, source_target_pairs={{0,4},{4,8},{8,12},{12,0},{1,5},{5,9},{9,13},{13,1},{2,6},{6,10},{... | collective-permute-start | bytes 786440 | tf_op jit(solution)/shard_map/ppermute | solution.py:360
  29.0 28.0 %collective-permute-start.10 = (bf16[128,4096]{1,0:T(8,128)(2,1)S(1)}, bf16[128,4096]{1,0:T(8,128)(2,1)S(1)}, u32[]{:S(2)}, u32[]{:S(2)}) collective-permute-start(bf16[128,4096]{1,0:T(8,128)(2,1)S(1)} %bitcast.40), channel_id=1, source_target_pairs={{0,4},{4,8},{8,12},{12,0},{1,5},{5,9},{9,13},{13,1},{2,6},{6,10},{... | collective-permute-start | bytes 3145736 | tf_op jit(solution)/shard_map/ppermute | solution.py:356
  33.7 45.7 %collective-permute-start.7 = (bf16[1024,512]{1,0:T(8,128)(2,1)S(1)}, bf16[1024,512]{1,0:T(8,128)(2,1)S(1)}, u32[]{:S(2)}, u32[]{:S(2)}) collective-permute-start(bf16[1024,512]{1,0:T(8,128)(2,1)S(1)} %dynamic-slice_bitcast_fusion.refs_7_), channel_id=1, source_target_pairs={{4,0},{8,4},{12,8},{5,1},{9,5},{13,9},{6,2},{10,6},{14,10},{7,3},{... | collective-permute-start | bytes 3145736 | tf_op jit(solution)/shard_map/ppermute | solution.py:53
  35.0 44.4 %collective-permute-start.6 = (bf16[1024,512]{1,0:T(8,128)(2,1)S(1)}, bf16[1024,512]{1,0:T(8,128)(2,1)S(1)}, u32[]{:S(2)}, u32[]{:S(2)}) collective-permute-start(bf16[1024,512]{1,0:T(8,128)(2,1)S(1)} %dynamic-slice_bitcast_fusion.refs_7_), channel_id=1, source_target_pairs={{0,4},{4,8},{8,12},{1,5},{5,9},{9,13},{2,6},{6,10},{10,14},{3,7},{... | collective-permute-start | bytes 3145736 | tf_op jit(solution)/shard_map/ppermute | solution.py:52
  40.2 39.3 %collective-permute-start.9 = (bf16[512,1024]{1,0:T(8,128)(2,1)S(1)}, bf16[512,1024]{1,0:T(8,128)(2,1)S(1)}, u32[]{:S(2)}, u32[]{:S(2)}) collective-permute-start(bf16[512,1024]{1,0:T(8,128)(2,1)S(1)} %copy-done.5), channel_id=1, source_target_pairs={{0,2},{2,0},{1,3},{3,1},{4,6},{6,4},{5,7},{7,5},{8,10},{10,8},{9,1... | collective-permute-start | bytes 3145736 | tf_op jit(solution)/shard_map/ppermute | solution.py:394
  57.0 45.0 %collective-permute-start.15 = (bf16[128,4096]{1,0:T(8,128)(2,1)S(1)}, bf16[128,4096]{1,0:T(8,128)(2,1)S(1)}, u32[]{:S(2)}, u32[]{:S(2)}) collective-permute-start(bf16[128,4096]{1,0:T(8,128)(2,1)S(1)} %collective-permute-done.10.refs_0_.refs_3_.refs_1_.refs_5_), channel_id=1, source_target_pairs={{0,4},{4,8},{8,12},{12,0},{1,5},{5,9},{9,13},{13,1},{2,6},{6,10},{... | collective-permute-start | bytes 3145736 | tf_op jit(solution)/shard_map/ppermute | solution.py:356
  79.5 41.7 %collective-permute-start.11 = (bf16[1024,512]{1,0:T(8,128)(2,1)S(1)}, bf16[1024,512]{1,0:T(8,128)(2,1)S(1)}, u32[]{:S(2)}, u32[]{:S(2)}) collective-permute-start(bf16[1024,512]{1,0:T(8,128)(2,1)S(1)} %broadcast_select_fusion.7.refs_1_), channel_id=1, source_target_pairs={{0,16},{16,0},{1,17},{17,1},{2,18},{18,2},{3,19},{19,3},{4,20},{20... | collective-permute-start | bytes 3145736 | tf_op jit(solution)/shard_map/ppermute | solution.py:416
  81.1 40.1 %collective-permute-start.12 = (bf16[1024,512]{1,0:T(8,128)(2,1)S(1)}, bf16[1024,512]{1,0:T(8,128)(2,1)S(1)}, u32[]{:S(2)}, u32[]{:S(2)}) collective-permute-start(bf16[1024,512]{1,0:T(8,128)(2,1)S(1)} %collective-permute-done.6.refs_0_), channel_id=1, source_target_pairs={{4,8},{8,12},{5,9},{9,13},{6,10},{10,14},{7,11},{11,15},{20,24},{2... | collective-permute-start | bytes 3145736 | tf_op jit(solution)/shard_map/ppermute | solution.py:52
  81.8 42.5 %collective-permute-start.13 = (bf16[1024,512]{1,0:T(8,128)(2,1)S(1)}, bf16[1024,512]{1,0:T(8,128)(2,1)S(1)}, u32[]{:S(2)}, u32[]{:S(2)}) collective-permute-start(bf16[1024,512]{1,0:T(8,128)(2,1)S(1)} %collective-permute-done.7.refs_1_), channel_id=1, source_target_pairs={{4,0},{8,4},{5,1},{9,5},{6,2},{10,6},{7,3},{11,7},{20,16},{24,20},... | collective-permute-start | bytes 3145736 | tf_op jit(solution)/shard_map/ppermute | solution.py:53
  83.1 37.8 %collective-permute-start.14 = (bf16[128,4096]{1,0:T(8,128)(2,1)S(1)}, bf16[128,4096]{1,0:T(8,128)(2,1)S(1)}, u32[]{:S(2)}, u32[]{:S(2)}) collective-permute-start(bf16[128,4096]{1,0:T(8,128)(2,1)S(1)} %broadcast_select_fusion.5), channel_id=1, source_target_pairs={{12,8},{0,4},{13,9},{1,5},{14,10},{2,6},{15,11},{3,7},{28,24},{16,... | collective-permute-start | bytes 3145736 | tf_op jit(solution)/shard_map/ppermute | solution.py:431
  102.0 45.0 %collective-permute-start.20 = (bf16[128,4096]{1,0:T(8,128)(2,1)S(1)}, bf16[128,4096]{1,0:T(8,128)(2,1)S(1)}, u32[]{:S(2)}, u32[]{:S(2)}) collective-permute-start(bf16[128,4096]{1,0:T(8,128)(2,1)S(1)} %collective-permute-done.15.refs_0_.refs_4_.refs_2_.refs_6_), channel_id=1, source_target_pairs={{0,4},{4,8},{8,12},{12,0},{1,5},{5,9},{9,13},{13,1},{2,6},{6,10},{... | collective-permute-start | bytes 3145736 | tf_op jit(solution)/shard_map/ppermute | solution.py:356
  124.3 43.8 %collective-permute-start.19 = (bf16[128,4096]{1,0:T(8,128)(2,1)S(1)}, bf16[128,4096]{1,0:T(8,128)(2,1)S(1)}, u32[]{:S(2)}, u32[]{:S(2)}) collective-permute-start(bf16[128,4096]{1,0:T(8,128)(2,1)S(1)} %add_convert_fusion.2), channel_id=1, source_target_pairs={{0,4},{4,8},{1,5},{5,9},{2,6},{6,10},{3,7},{7,11},{16,20},{20,24},... | collective-permute-start | bytes 3145736 | tf_op jit(solution)/shard_map/ppermute | solution.py:435
  126.9 41.2 %collective-permute-start.18 = (bf16[128,4096]{1,0:T(8,128)(2,1)S(1)}, bf16[128,4096]{1,0:T(8,128)(2,1)S(1)}, u32[]{:S(2)}, u32[]{:S(2)}) collective-permute-start(bf16[128,4096]{1,0:T(8,128)(2,1)S(1)} %add_convert_fusion.2), channel_id=1, source_target_pairs={{8,4},{12,8},{9,5},{13,9},{10,6},{14,10},{11,7},{15,11},{24,20},{2... | collective-permute-start | bytes 3145736 | tf_op jit(solution)/shard_map/ppermute | solution.py:434
  127.7 34.1 %collective-permute-start.16 = (bf16[1024,512]{1,0:T(8,128)(2,1)S(1)}, bf16[1024,512]{1,0:T(8,128)(2,1)S(1)}, u32[]{:S(2)}, u32[]{:S(2)}) collective-permute-start(bf16[1024,512]{1,0:T(8,128)(2,1)S(1)} %broadcast_select_fusion.6.refs_2_), channel_id=1, source_target_pairs={{0,16},{16,0},{1,17},{17,1},{2,18},{18,2},{3,19},{19,3},{4,20},{20... | collective-permute-start | bytes 3145736 | tf_op jit(solution)/shard_map/ppermute | solution.py:416
  129.5 38.6 %collective-permute-start.17 = (bf16[1024,512]{1,0:T(8,128)(2,1)S(1)}, bf16[1024,512]{1,0:T(8,128)(2,1)S(1)}, u32[]{:S(2)}, u32[]{:S(2)}) collective-permute-start(bf16[1024,512]{1,0:T(8,128)(2,1)S(1)} %broadcast_select_fusion.4), channel_id=1, source_target_pairs={{8,12},{4,0},{9,13},{5,1},{10,14},{6,2},{11,15},{7,3},{24,28},{20,... | collective-permute-start | bytes 3145736 | tf_op jit(solution)/shard_map/ppermute | solution.py:47
  168.1 11.8 %collective-permute-start.23 = (bf16[512,3328]{1,0:T(8,128)(2,1)S(1)}, bf16[512,3328]{1,0:T(8,128)(2,1)S(1)}, u32[]{:S(2)}, u32[]{:S(2)}) collective-permute-start(bf16[512,3328]{1,0:T(8,128)(2,1)S(1)} %shard_map.106), channel_id=1, source_target_pairs={{0,1},{1,0},{2,3},{3,2},{4,5},{5,4},{6,7},{7,6},{8,9},{9,8},{10,11... | collective-permute-start | bytes 10223624 | tf_op jit(solution)/shard_map/ppermute | solution.py:465
  173.8 25.6 %collective-permute-start.22 = (bf16[1024,512]{1,0:T(8,128)(2,1)S(1)}, bf16[1024,512]{1,0:T(8,128)(2,1)S(1)}, u32[]{:S(2)}, u32[]{:S(2)}) collective-permute-start(bf16[1024,512]{1,0:T(8,128)(2,1)S(1)} %select_select_fusion.refs_3_), channel_id=1, source_target_pairs={{0,16},{16,0},{1,17},{17,1},{2,18},{18,2},{3,19},{19,3},{4,20},{20... | collective-permute-start | bytes 3145736 | tf_op jit(solution)/shard_map/ppermute | solution.py:416
  175.3 36.8 %collective-permute-start.25 = (bf16[128,4096]{1,0:T(8,128)(2,1)}, bf16[128,4096]{1,0:T(8,128)(2,1)}, u32[]{:S(2)}, u32[]{:S(2)}) collective-permute-start(bf16[128,4096]{1,0:T(8,128)(2,1)} %add_convert_fusion), channel_id=1, source_target_pairs={{0,4},{4,8},{8,12},{1,5},{5,9},{9,13},{2,6},{6,10},{10,14},{3,7},{... | collective-permute-start | bytes 3145736 | tf_op jit(solution)/shard_map/ppermute | solution.py:435
  178.6 33.5 %collective-permute-start.24 = (bf16[128,4096]{1,0:T(8,128)(2,1)S(1)}, bf16[128,4096]{1,0:T(8,128)(2,1)}, u32[]{:S(2)}, u32[]{:S(2)}) collective-permute-start(bf16[128,4096]{1,0:T(8,128)(2,1)S(1)} %add_convert_fusion.1), channel_id=1, source_target_pairs={{4,0},{8,4},{12,8},{5,1},{9,5},{13,9},{6,2},{10,6},{14,10},{7,3},{... | collective-permute-start | bytes 3145736 | tf_op jit(solution)/shard_map/ppermute | solution.py:434
  180.0 36.7 %collective-permute-start.28 = (bf16[256,1024]{1,0:T(8,128)(2,1)S(1)}, bf16[256,1024]{1,0:T(8,128)(2,1)S(1)}, u32[]{:S(2)}, u32[]{:S(2)}) collective-permute-start(bf16[256,1024]{1,0:T(8,128)(2,1)S(1)} %get-tuple-element.73), channel_id=1, source_target_pairs={{0,4},{4,0},{8,12},{12,8},{1,5},{5,1},{9,13},{13,9},{2,6},{6,2},{1... | collective-permute-start | bytes 1572872 | tf_op jit(solution)/shard_map/ppermute | solution.py:513
  216.9 13.9 %collective-permute-start.29 = (bf16[128,1024]{1,0:T(8,128)(2,1)S(1)}, bf16[128,1024]{1,0:T(8,128)(2,1)S(1)}, u32[]{:S(2)}, u32[]{:S(2)}) collective-permute-start(bf16[128,1024]{1,0:T(8,128)(2,1)S(1)} %slice.39), channel_id=1, source_target_pairs={{0,8},{4,12},{8,0},{12,4},{1,9},{5,13},{9,1},{13,5},{2,10},{6,14},... | collective-permute-start | bytes 786440 | tf_op jit(solution)/shard_map/ppermute | solution.py:513
  (26 other events, 366.3 us)
